TPU v7x, 32 devices: a whole 2x2x4 slice. The times are simulated.
32 devices in a mesh: grp: 8 (over y, x, core), frq: 4 (over z).
Axes of the slice: x: 2, y: 2, z: 4, core: 2. Of those that a mesh axis runs over, the one named last changes fastest.
Arguments:
- spectra: bfloat16 [8, 512, 240, 128], P('grp', 'frq'), may hold values from -6 to 6
- band_weight: float32 [512], replicated, may hold values from 0.25 to 4
Outputs:
- correlations: bfloat16 [2, 8, 4096, 1024], P(None, 'grp', 'frq')
All inputs are finite; a program needn't handle non-finite values.
Results may differ from a plain program's by a relative error of at most 0.0058.
Values may be sent and summed in bfloat16 or wider, within the bound.
No kernel may reach another device: no remote copies, remote signals or barrier semaphores. Data moves between devices by JAX's collectives and lax.ppermute only.
A program may use at most 64 MiB of HBM per device.

v0:
```python
import math

import jax
import jax.numpy as jnp
from jax import lax
from jax.sharding import PartitionSpec as P

ROUNDS = 2


def passed_along(value, axis, steps):
    count = lax.axis_size(axis)
    pairs = [(source, (source + steps) % count) for source in range(count)]
    return lax.ppermute(value, axis, pairs)


def inverse_table(band_weight):
    bin_count = band_weight.shape[0]
    lag_count = 2 * bin_count
    phase_index = (
        jnp.arange(bin_count, dtype=jnp.int32)[:, None]
        * jnp.arange(lag_count, dtype=jnp.int32)[None, :]
        % lag_count
    )
    phase_angle = phase_index.astype(jnp.float32) * (2.0 * math.pi / lag_count)
    weighting = band_weight[:, None] * (1.0 / math.sqrt(bin_count))
    return jnp.stack(
        [weighting * jnp.cos(phase_angle), -weighting * jnp.sin(phase_angle)], 1
    ).astype(jnp.bfloat16)


def cross_stack(local_block, partner_block):
    windows = local_block.shape[1]
    half_width = local_block.shape[2] // 2
    product = jnp.einsum(
        "fwa,fwb->fab", local_block, partner_block, preferred_element_type=jnp.float32
    )
    real_part = product[:, :half_width, :half_width] + product[:, half_width:, half_width:]
    imag_part = product[:, half_width:, :half_width] - product[:, :half_width, half_width:]
    scaled = jnp.stack([real_part, imag_part], 1) * (1.0 / math.sqrt(windows))
    return scaled.reshape(scaled.shape[0], 2, half_width * half_width).astype(jnp.bfloat16)


def local(spectra, band_weight):
    lag_table = inverse_table(band_weight)
    local_block = spectra[0]
    partner_block = spectra
    cross_list = []
    for turn_index in range(ROUNDS):
        partner_block = passed_along(spectra, "grp", turn_index + 1)
        cross_list.append(cross_stack(local_block, partner_block[0]))

    def to_lags(gathered):
        lagged = jnp.einsum(
            "nfcp,fcl->npl", gathered, lag_table, preferred_element_type=jnp.float32
        )
        return lagged.astype(jnp.bfloat16)

    result = jnp.concatenate(
        [
            to_lags(lax.all_to_all(member[None], "frq", split_axis=3, concat_axis=1, tiled=True))
            for member in cross_list
        ],
        0,
    )
    return result[:, None]


def solution(mesh):
    return jax.shard_map(
        local,
        mesh=mesh,
        in_specs=(P("grp", "frq", None, None), P()),
        out_specs=P(None, "grp", "frq", None),
        check_vma=False,
    )
```

profile of v0, /device:TPU:0, one launch (start us, length us, event | category | flops | bytes accessed | tf_op | source)
XLA Modules:
  0.0 377.8 jit_solution(1926828208853463765)
XLA Ops:
  0.0 2.9 collective-permute-start.1
  2.9 0.0 collective-permute-start
  2.9 171.3 %collective-permute-done.1 = bf16[1,128,240,128]{3,2,1,0:T(8,128)(2,1)} collective-permute-done((bf16[1,128,240,128]{3,2,1,0:T(8,128)(2,1)}, bf16[1,128,240,128]{3,2,1,0:T(8,128)(2,1)}, u32[]{:S(2)}, u32[]{:S(2)}) %collective-permute-start.1) | collective-permute-done | bytes 7864352 | tf_op jit(solution)/shard_map/ppermute | solution.py:14
  174.3 11.5 %fusion = f32[128,128,128]{2,1,0:T(8,128)} fusion(bf16[1,128,240,128]{3,2,1,0:T(8,128)(2,1)} %collective-permute-done.1, bf16[1,128,240,128]{3,2,1,0:T(8,128)(2,1)} %param.2), kind=kOutput, calls=%fused_computation | convolution fusion | flops 1006632960 | bytes 24117248 | tf_op jit(solution)/shard_map/fwa,fwb->fab/dot_general | solution.py:35
  185.7 12.2 %slice_add_fusion = (f32[128,64,64]{2,1,0:T(8,128)}, f32[128,64,64]{2,1,0:T(8,128)}) fusion(f32[128,128,128]{2,1,0:T(8,128)} %fusion), kind=kLoop, calls=%fused_computation.7 | loop fusion | flops 1048576 | bytes 12582912 | tf_op jit(solution)/shard_map/add | solution.py:38
  197.9 3.8 %copy.17 = f32[128,64,64]{0,2,1:T(8,128)S(1)} copy(f32[128,64,64]{2,1,0:T(8,128)} %get-tuple-element.7) | data formatting | bytes 4194304 | tf_op jit(solution)/shard_map/add | solution.py:38
  201.7 4.8 %copy.18 = f32[128,64,64]{0,2,1:T(8,128)} copy(f32[128,64,64]{2,1,0:T(8,128)} %get-tuple-element.8) | data formatting | bytes 4194304 | tf_op jit(solution)/shard_map/sub | solution.py:39
  206.5 2.0 fusion.7
  208.5 18.1 %copy.19 = bf16[1,128,2,4096]{1,2,0,3:T(2,128)(2,1)} copy(bf16[1,128,2,4096]{1,3,2,0:T(8,128)(2,1)S(1)} %fusion.7) | data formatting | bytes 4194304 | tf_op jit(solution)/shard_map/convert_element_type | solution.py:41
  226.7 5.4 %all-to-all-start.1 = ((bf16[1,128,2,4096]{1,2,0,3:T(2,128)(2,1)}), bf16[1,128,2,4096]{1,2,0,3:T(2,128)(2,1)}, u32[]{:S(2)}, u32[]{:S(2)}) async-start(bf16[1,128,2,4096]{1,2,0,3:T(2,128)(2,1)} %copy.19), calls=%async_computation.1 | async-start | bytes 4194304 | tf_op jit(solution)/shard_map/all_to_all | solution.py:61
  232.1 25.6 %collective-permute-done = bf16[1,128,240,128]{3,2,1,0:T(8,128)(2,1)} collective-permute-done((bf16[1,128,240,128]{3,2,1,0:T(8,128)(2,1)}, bf16[1,128,240,128]{3,2,1,0:T(8,128)(2,1)}, u32[]{:S(2)}, u32[]{:S(2)}) %collective-permute-start) | collective-permute-done | bytes 7864352 | tf_op jit(solution)/shard_map/ppermute | solution.py:14
  257.7 11.5 %fusion.2 = f32[128,128,128]{2,1,0:T(8,128)} fusion(bf16[1,128,240,128]{3,2,1,0:T(8,128)(2,1)} %collective-permute-done, bf16[1,128,240,128]{3,2,1,0:T(8,128)(2,1)} %param.2), kind=kOutput, calls=%fused_computation.2 | convolution fusion | flops 1006632960 | bytes 24117248 | tf_op jit(solution)/shard_map/fwa,fwb->fab/dot_general | solution.py:35
  269.2 12.2 %slice_add_fusion.1 = (f32[128,64,64]{2,1,0:T(8,128)}, f32[128,64,64]{2,1,0:T(8,128)}) fusion(f32[128,128,128]{2,1,0:T(8,128)} %fusion.2), kind=kLoop, calls=%fused_computation.9 | loop fusion | flops 1048576 | bytes 12582912 | tf_op jit(solution)/shard_map/add | solution.py:38
  281.4 3.8 %copy.13 = f32[128,64,64]{0,2,1:T(8,128)S(1)} copy(f32[128,64,64]{2,1,0:T(8,128)} %get-tuple-element.5) | data formatting | bytes 4194304 | tf_op jit(solution)/shard_map/add | solution.py:38
  285.2 4.8 %copy.14 = f32[128,64,64]{0,2,1:T(8,128)} copy(f32[128,64,64]{2,1,0:T(8,128)} %get-tuple-element.6) | data formatting | bytes 4194304 | tf_op jit(solution)/shard_map/sub | solution.py:39
  289.9 2.0 fusion.6
  292.0 18.4 %copy.15 = bf16[1,128,2,4096]{1,2,0,3:T(2,128)(2,1)} copy(bf16[1,128,2,4096]{1,3,2,0:T(8,128)(2,1)S(1)} %fusion.6) | data formatting | bytes 4194304 | tf_op jit(solution)/shard_map/convert_element_type | solution.py:41
  310.4 0.0 copy-start.3
  310.4 0.0 all-to-all-done.1
  310.4 5.2 %all-to-all-start = ((bf16[1,128,2,4096]{1,2,0,3:T(2,128)(2,1)}), bf16[1,128,2,4096]{1,2,0,3:T(2,128)(2,1)S(1)}, u32[]{:S(2)}, u32[]{:S(2)}) async-start(bf16[1,128,2,4096]{1,2,0,3:T(2,128)(2,1)} %copy.15), calls=%async_computation | async-start | bytes 4194304 | tf_op jit(solution)/shard_map/all_to_all | solution.py:61
  315.6 0.0 copy-done.3
  315.6 9.4 %multiply_convert_fusion = (bf16[512,1,1024]{2,0,1:T(8,128)(2,1)S(1)}, bf16[512,1,1024]{2,0,1:T(8,128)(2,1)}) fusion(f32[512]{0:T(512)S(1)} %get-tuple-element.10, f32[512]{0:T(512)S(1)} %get-tuple-element.9), kind=kLoop, calls=%fused_computation.26 | loop fusion | flops 9437184 | bytes 2101248 | tf_op jit(solution)/shard_map/convert.1
  324.9 4.5 %copy.24 = bf16[1,128,2,4,1024]{1,3,4,2,0:T(4,128)(2,1)} copy(bf16[1,128,2,4,1024]{1,2,4,3,0:T(2,128)(2,1)} %bitcast.11) | data formatting | bytes 4194304 | tf_op jit(solution)/shard_map/all_to_all | solution.py:61
  329.5 4.1 %reshape.201 = bf16[512,2,1024]{0,2,1:T(8,128)(2,1)} reshape(bf16[1,4,128,2,1024]{2,1,4,3,0:T(4,128)(2,1)} %bitcast.50) | data formatting | bytes 4194304 | tf_op jit(solution)/shard_map/reshape.4
  333.6 28.6 %all-to-all-done = bf16[1,128,2,4096]{1,2,0,3:T(2,128)(2,1)S(1)} async-done(((bf16[1,128,2,4096]{1,2,0,3:T(2,128)(2,1)}), bf16[1,128,2,4096]{1,2,0,3:T(2,128)(2,1)S(1)}, u32[]{:S(2)}, u32[]{:S(2)}) %all-to-all-start) | async-done | bytes 2097184 | tf_op jit(solution)/shard_map/all_to_all | solution.py:61
  362.2 2.9 copy.25
  365.1 0.0 copy-start
  365.1 4.3 %reshape.200 = bf16[512,2,1024]{0,2,1:T(8,128)(2,1)} reshape(bf16[1,4,128,2,1024]{2,1,4,3,0:T(4,128)(2,1)} %bitcast.51) | data formatting | bytes 4194304 | tf_op jit(solution)/shard_map/reshape
  369.4 0.0 copy-done
  369.4 0.0 copy-start.1
  369.4 0.0 copy-start.2
  369.4 3.7 fusion.15
  373.1 0.0 copy-done.1
  373.1 0.0 copy-done.2
  373.1 2.3 fusion.14
  375.4 2.4 maximum_bitcast_fusion
  (1 shorter events, 0.0 us)
Async XLA Ops:
  0.0 174.3 %collective-permute-start.1 = (bf16[1,128,240,128]{3,2,1,0:T(8,128)(2,1)}, bf16[1,128,240,128]{3,2,1,0:T(8,128)(2,1)}, u32[]{:S(2)}, u32[]{:S(2)}) collective-permute-start(bf16[1,128,240,128]{3,2,1,0:T(8,128)(2,1)} %param.2), channel_id=1, source_target_pairs={{0,8},{4,12},{8,16},{12,20},{16,24},{20,28},{24,0},{28,4},{1,9},{5... | collective-permute-start | bytes 23592968 | tf_op jit(solution)/shard_map/ppermute | solution.py:14
  2.9 254.8 %collective-permute-start = (bf16[1,128,240,128]{3,2,1,0:T(8,128)(2,1)}, bf16[1,128,240,128]{3,2,1,0:T(8,128)(2,1)}, u32[]{:S(2)}, u32[]{:S(2)}) collective-permute-start(bf16[1,128,240,128]{3,2,1,0:T(8,128)(2,1)} %param.2), channel_id=1, source_target_pairs={{0,4},{4,8},{8,12},{12,16},{16,20},{20,24},{24,28},{28,0},{1,5},{5... | collective-permute-start | bytes 23592968 | tf_op jit(solution)/shard_map/ppermute | solution.py:14
  226.7 83.7 %all-to-all-start.1 = ((bf16[1,128,2,4096]{1,2,0,3:T(2,128)(2,1)}), bf16[1,128,2,4096]{1,2,0,3:T(2,128)(2,1)}, u32[]{:S(2)}, u32[]{:S(2)}) async-start(bf16[1,128,2,4096]{1,2,0,3:T(2,128)(2,1)} %copy.19), calls=%async_computation.1 | async-start | bytes 4194304 | tf_op jit(solution)/shard_map/all_to_all | solution.py:61
  310.4 5.2 %copy-start.3 = (f32[512]{0:T(512)S(1)}, f32[512]{0:T(512)}, u32[]{:S(2)}) copy-start(f32[512]{0:T(512)} %param.3) | copy-start | bytes 6148
  310.4 51.8 %all-to-all-start = ((bf16[1,128,2,4096]{1,2,0,3:T(2,128)(2,1)}), bf16[1,128,2,4096]{1,2,0,3:T(2,128)(2,1)S(1)}, u32[]{:S(2)}, u32[]{:S(2)}) async-start(bf16[1,128,2,4096]{1,2,0,3:T(2,128)(2,1)} %copy.15), calls=%async_computation | async-start | bytes 4194304 | tf_op jit(solution)/shard_map/all_to_all | solution.py:61
  365.1 4.3 %copy-start = (bf16[512,2,1024]{0,2,1:T(8,128)(2,1)S(1)}, bf16[512,2,1024]{0,2,1:T(8,128)(2,1)}, u32[]{:S(2)}) copy-start(bf16[512,2,1024]{0,2,1:T(8,128)(2,1)} %reshape.201) | copy-start | bytes 6291460
  369.4 3.7 copy-start.1
  369.4 3.7 copy-start.2
where the time goes:
time: 378 us
  waiting for transfers between devices  226 us (60%)
  local copies, waits for them, and re-layouts  69.5 us (18%)
  other arithmetic  40.2 us (11%)
  matrix products  29 us (8%)
  starting transfers between devices  13.5 us (4%)
    ppermute x2, waiting for transfers between devices, passed_along(): return lax.ppermute(value, axis, pairs)  197 us
    convert_element_type x2, local copies, waits for them, and re-layouts, cross_stack(): scaled.reshape(scaled.shape[0], 2, half_width * half_width)  36.5 us
    all_to_all x2, waiting for transfers between devices, local(): lax.all_to_all(member[None], 'frq', split_axis=3, concat_axis=1, tiled=True)  28.6 us
    add x2, other arithmetic, cross_stack(): product[:, :half_width, :half_width] + product[:, half_width:, half_width:]  24.4 us
    dot_general x2, matrix products, cross_stack(): jnp.einsum('fwa,fwb->fab', local_block, partner_block, preferred_element_...  23 us
    all_to_all x2, starting transfers between devices, local(): lax.all_to_all(member[None], 'frq', split_axis=3, concat_axis=1, tiled=True)  10.6 us
    sub x2, local copies, waits for them, and re-layouts, cross_stack(): product[:, half_width:, :half_width] - product[:, :half_width, half_width:]  9.53 us
    another operation x1, other arithmetic  9.37 us
  transfers between devices with their start and end apart: 4, of which 3 were waited for; matrix products, arithmetic and copies ran while one was open for 33% of the time, Pallas kernels for 0%

commit v1 on v0

v1 whole, which is shorter than its diff:
```python
import functools
import math

import jax
import jax.numpy as jnp
from jax import lax
from jax.experimental import pallas as pl
from jax.experimental.pallas import tpu as pltpu
from jax.sharding import PartitionSpec as P

ROUNDS = 2
CHUNK = 16


def permuted(value, target):
    count = lax.axis_size("grp")
    return lax.ppermute(value, "grp", [(source, target(source) % count) for source in range(count)])


def is_odd(group):
    return (group // 2) % 2


def to_x(group):
    return group ^ 2


def to_y(group):
    return group + 4 if is_odd(group) else group - 4


def to_b(group):
    return group if is_odd(group) else group + 4


def to_other_core(group):
    return group ^ 1


def cross_body(shards, step_freqs, scalars, own, x_mine, y_mine, x_other, last_other, out, stage):
    windows, width = own.shape[1:]
    half = width // 2
    freqs = out.shape[4]
    per_shard = half // shards
    step = pl.program_id(0)
    first_core = scalars[0] == 0
    odd = scalars[1] == 1
    scale = 1.0 / math.sqrt(windows)
    lanes = lax.broadcasted_iota(jnp.int32, (half, width), 1)
    sign = jnp.where(lanes < half, 1.0, -1.0).astype(jnp.float32)

    def products(left, rights):
        return lax.dot_general(
            left,
            jnp.concatenate(rights, 1),
            (((0,), (0,)), ((), ())),
            preferred_element_type=jnp.float32,
        )

    for at in range(step_freqs):
        center, center_other, other = x_mine[at], x_other[at], last_other[at]
        before = jnp.where(odd, y_mine[at], own[at])
        after = jnp.where(odd, own[at], y_mine[at])
        pair = [
            products(center, [jnp.where(first_core, other, center_other), before]),
            products(after, [jnp.where(first_core, center_other, other), center]),
        ]
        for bundle, product in enumerate(pair):
            for turn in range(ROUNDS):
                part = product[:, turn * width : (turn + 1) * width]
                top, bottom = part[:half], part[half:]
                value = (top * sign + pltpu.roll(bottom, half, 1)) * scale
                base = (bundle * ROUNDS + turn) * half * freqs
                stage[pl.ds(base + step * step_freqs + at, half, stride=freqs), :] = value

    @pl.when(step == pl.num_programs(0) - 1)
    def _():
        for bundle in range(2):
            for turn in range(ROUNDS):
                for shard in range(shards):
                    base = ((bundle * ROUNDS + turn) * half + shard * per_shard) * freqs
                    rows = stage[pl.ds(base, per_shard * freqs), :]
                    out[shard, bundle, turn] = rows.reshape(per_shard, freqs, width).astype(out.dtype)


def cross_spectra(scalars, spectra, x_mine, y_mine, x_other, last_other, shards):
    freqs, windows, width = x_mine.shape
    step_freqs = math.gcd(freqs, 4)
    half = width // 2
    block = (step_freqs, windows, width)
    plain = pl.BlockSpec(block, lambda step, scalars: (step, 0, 0))
    out_shape = (shards, 2, ROUNDS, half // shards, freqs, width)
    return pl.pallas_call(
        functools.partial(cross_body, shards, step_freqs),
        out_shape=jax.ShapeDtypeStruct(out_shape, jnp.bfloat16),
        grid_spec=pltpu.PrefetchScalarGridSpec(
            num_scalar_prefetch=1,
            grid=(freqs // step_freqs,),
            in_specs=[
                pl.BlockSpec(block, lambda step, scalars: (scalars[2] * (freqs // step_freqs) + step, 0, 0))
            ]
            + [plain] * 4,
            out_specs=pl.BlockSpec(out_shape, lambda step, scalars: (0,) * 6),
            scratch_shapes=[pltpu.VMEM((2 * ROUNDS * half * freqs, width), jnp.float32)],
        ),
        compiler_params=pltpu.CompilerParams(vmem_limit_bytes=48 * 1024 * 1024),
        cost_estimate=pl.CostEstimate(
            flops=2 * freqs * 2 * windows * width * 2 * width,
            bytes_accessed=5 * freqs * windows * width * 2 + 4 * freqs * half * width * 2,
            transcendentals=0,
        ),
    )(scalars, spectra, x_mine, y_mine, x_other, last_other)


def lag_body(count, *refs):
    blocks, table, out = refs[:count], refs[count], refs[count + 1]
    shards, _, stations, _, width = blocks[0].shape
    half = width // 2
    rows = []
    for station in range(stations):
        spectrum = jnp.concatenate(
            [block[shard, 0, station] for block in blocks for shard in range(shards)], 0
        )
        turned = spectrum.T
        rows.append(jnp.concatenate([turned[:half], turned[half:]], 1))
    left = jnp.concatenate(rows, 0)
    out[0, 0] = jnp.dot(left, table[...], preferred_element_type=jnp.float32).astype(out.dtype)


def to_lags(blocks, table):
    shards, rounds, stations, freqs, width = blocks[0].shape
    half = width // 2
    depth, lags = table.shape
    step = math.gcd(stations, 4)
    block = pl.BlockSpec((shards, 1, step, freqs, width), lambda turn, at: (0, turn, at, 0, 0))
    return pl.pallas_call(
        functools.partial(lag_body, len(blocks)),
        out_shape=jax.ShapeDtypeStruct((rounds, 1, stations * half, lags), jnp.bfloat16),
        grid=(rounds, stations // step),
        in_specs=[block] * len(blocks) + [pl.BlockSpec((depth, lags), lambda turn, at: (0, 0))],
        out_specs=pl.BlockSpec((1, 1, step * half, lags), lambda turn, at: (turn, 0, at, 0)),
        compiler_params=pltpu.CompilerParams(vmem_limit_bytes=48 * 1024 * 1024),
        cost_estimate=pl.CostEstimate(
            flops=2 * rounds * stations * half * depth * lags,
            bytes_accessed=2 * (rounds * stations * half * (depth + lags) + depth * lags),
            transcendentals=0,
        ),
    )(*blocks, table)


def inverse_table(band_weight, halves, chunks):
    bins = band_weight.shape[0]
    shards = lax.axis_size("frq")
    lags = 2 * bins
    size = bins // (shards * 2 * chunks)
    dims = (chunks, 2, shards, size)
    weights = band_weight.reshape(shards, 2, chunks, size)
    weights = jnp.where(halves[0] == 0, weights, weights[:, ::-1]).transpose(2, 1, 0, 3).reshape(bins)
    indices = lax.broadcasted_iota(jnp.int32, dims, 2) * (2 * chunks * size)
    indices += (lax.broadcasted_iota(jnp.int32, dims, 1) ^ halves[0]) * (chunks * size)
    indices += lax.broadcasted_iota(jnp.int32, dims, 0) * size
    indices += lax.broadcasted_iota(jnp.int32, dims, 3)
    indices = indices.reshape(bins)
    phase_index = indices[:, None] * jnp.arange(lags, dtype=jnp.int32)[None, :] % lags
    phase_angle = phase_index.astype(jnp.float32) * (2.0 * math.pi / lags)
    weighting = weights[:, None] * (1.0 / math.sqrt(bins))
    table = jnp.stack(
        [weighting * jnp.cos(phase_angle), -weighting * jnp.sin(phase_angle)], 0
    ).astype(jnp.bfloat16)
    return table.reshape(2 * bins, lags)


def local(spectra, band_weight):
    shards = lax.axis_size("frq")
    group = lax.axis_index("grp").astype(jnp.int32)
    core, odd = group & 1, (group >> 1) & 1
    block = spectra[0]
    half_size = block.shape[0] // 2
    chunks = max(1, half_size // CHUNK)
    size = half_size // chunks

    def piece(source, half, chunk):
        return lax.dynamic_slice_in_dim(source, (half * chunks + chunk) * size, size, 0)

    source = block
    sent = []
    for chunk in range(chunks):
        x_piece, y_piece = piece(source, 1 - odd, chunk), piece(source, odd, chunk)
        if chunk == 0:
            x_piece, y_piece, source = lax.optimization_barrier((x_piece, y_piece, source))
        sent.append((x_piece, y_piece, permuted(x_piece, to_x), permuted(y_piece, to_y)))

    blocks = []
    for chunk, (_, own, x_mine, y_mine) in enumerate(sent):
        x_other = permuted(x_mine, to_other_core)
        last_other = permuted(jnp.where(odd == core, y_mine, own), to_other_core)
        scalars = jnp.stack([core, odd, odd * chunks + chunk])
        result = cross_spectra(scalars, source, x_mine, y_mine, x_other, last_other, shards)
        spread = lax.all_to_all(result, "frq", split_axis=0, concat_axis=0, tiled=True)
        blocks += [permuted(spread[:, 0], to_x), permuted(spread[:, 1], to_b)]

    table = inverse_table(band_weight, [1 - odd, odd], chunks)
    return to_lags(blocks, table)


def solution(mesh):
    return jax.shard_map(
        local,
        mesh=mesh,
        in_specs=(P("grp", "frq", None, None), P()),
        out_specs=P(None, "grp", "frq", None),
        check_vma=False,
    )
```

time: 378 us -> 199 us (0.53)
  waiting for transfers between devices: 226 us -> 93.2 us
  local copies, waits for them, and re-layouts: 69.5 us -> 15.5 us
  starting transfers between devices: 13.5 us -> 45.5 us
  Pallas kernels: 0 us -> 31.3 us
  matrix products: 29 us -> 0 us
  other arithmetic: 40.2 us -> 12.4 us
    ppermute x2 -> x24, waiting for transfers between devices: 197 us -> 58.7 us  [permuted(): lax.ppermute(value, 'grp', [(source, target(source) % count) for source i...]
    convert_element_type x2 -> x0, local copies, waits for them, and re-layouts: 36.5 us -> none  [cross_stack(): scaled.reshape(scaled.shape[0], 2, half_width * half_width)]
    pallas_call x0 -> x5, Pallas kernels: none -> 31.3 us  [the longest x4 22.4 us: cross_spectra(): pl.pallas_call(functools.partial(cross_body, shards, step_freqs), out_sha...]
    dot_general x4 -> x0, matrix products: 29 us -> none  [the longest x2 23 us: cross_stack(): jnp.einsum('fwa,fwb->fab', local_block, partner_block, preferred_element_...]
    ppermute x2 -> x24, starting transfers between devices: 2.94 us -> 28.7 us  [permuted(): lax.ppermute(value, 'grp', [(source, target(source) % count) for source i...]
    add x2 -> x1, other arithmetic: 24.4 us -> 0.08 us  [inverse_table(): indices += lax.broadcasted_iota(jnp.int32, dims, 3)]
    sub x2 -> x0, local copies, waits for them, and re-layouts: 9.53 us -> none  [cross_stack(): product[:, half_width:, :half_width] - product[:, :half_width, half_width:]]
    dynamic_slice x0 -> x2, local copies, waits for them, and re-layouts: none -> 7.94 us  [piece(): lax.dynamic_slice_in_dim(source, (half * chunks + chunk) * size, size, 0)]
  transfers between devices with their start and end apart: 4 -> 28, of which waited for: 3 -> 16; matrix products, arithmetic and copies ran while one was open for 33% -> 13% of each run, Pallas kernels for 0% -> 11%
where the time goes in v1:
time: 199 us; the launch traced here: 198 us
  waiting for transfers between devices  93.2 us (47%)
  starting transfers between devices  45.5 us (23%)
  Pallas kernels  31.3 us (16%)
  local copies, waits for them, and re-layouts  15.5 us (8%)
  other arithmetic  12.4 us (6%)
    ppermute x24, waiting for transfers between devices, permuted(): lax.ppermute(value, 'grp', [(source, target(source) % count) for source i...  58.7 us
    all_to_all x4, waiting for transfers between devices, local(): lax.all_to_all(result, 'frq', split_axis=0, concat_axis=0, tiled=True)  34.5 us
    ppermute x24, starting transfers between devices, permuted(): lax.ppermute(value, 'grp', [(source, target(source) % count) for source i...  28.7 us
    pallas_call x4, Pallas kernels, cross_spectra(): pl.pallas_call(functools.partial(cross_body, shards, step_freqs), out_sha...  22.4 us
    all_to_all x4, starting transfers between devices, local(): lax.all_to_all(result, 'frq', split_axis=0, concat_axis=0, tiled=True)  16.9 us
    another operation x1, other arithmetic  9.2 us
    pallas_call x1, Pallas kernels, to_lags(): pl.pallas_call(functools.partial(lag_body, len(blocks)), out_shape=jax.Sh...  8.92 us
    dynamic_slice x2, local copies, waits for them, and re-layouts, piece(): lax.dynamic_slice_in_dim(source, (half * chunks + chunk) * size, size, 0)  7.94 us
  transfers between devices with their start and end apart: 28, of which 16 were waited for; matrix products, arithmetic and copies ran while one was open for 13% of the time, Pallas kernels for 11%

profile of v1, /device:TPU:0, one launch (start us, length us, event | category | flops | bytes accessed | tf_op | source)
XLA Modules:
  0.0 198.2 jit_solution(4043937361906892738)
XLA Ops:
  0.0 2.6 %dynamic-slice_bitcast_fusion = (bf16[16,240,128]{2,1,0:T(8,128)(2,1)S(1)}, bf16[16,240,128]{2,1,0:T(8,128)(2,1)}) fusion(bf16[1,128,240,128]{3,2,1,0:T(8,128)(2,1)} %param.2, s32[]{:T(128)S(6)} %select_n.71, s32[]{:T(128)S(6)} %select_n.70), kind=kLoop, calls=%fused_computation.12 | loop fusion | bytes 3932168 | tf_op jit(solution)/shard_map/dynamic_slice | solution.py:183
  2.6 2.9 %collective-permute-start = (bf16[16,240,128]{2,1,0:T(8,128)(2,1)}, bf16[16,240,128]{2,1,0:T(8,128)(2,1)S(1)}, u32[]{:S(2)}, u32[]{:S(2)}) collective-permute-start(bf16[16,240,128]{2,1,0:T(8,128)(2,1)} %get-tuple-element.9), channel_id=1, source_target_pairs={{0,8},{4,12},{8,0},{12,4},{16,24},{20,28},{24,16},{28,20},{1,9},{5... | collective-permute-start | bytes 2949128 | tf_op jit(solution)/shard_map/ppermute | solution.py:17
  5.5 1.5 collective-permute-start.1
  7.0 20.4 %collective-permute-done.x_mine = bf16[16,240,128]{2,1,0:T(8,128)(2,1)S(1)} collective-permute-done((bf16[16,240,128]{2,1,0:T(8,128)(2,1)}, bf16[16,240,128]{2,1,0:T(8,128)(2,1)S(1)}, u32[]{:S(2)}, u32[]{:S(2)}) %collective-permute-start) | collective-permute-done | bytes 983072 | tf_op jit(solution)/shard_map/ppermute | solution.py:17
  27.5 1.2 collective-permute-done.1.y_mine
  28.7 1.0 broadcast_select_fusion.3
  29.8 0.0 collective-permute-start.3
  29.8 5.4 %constant_dynamic-slice_fusion = (bf16[16,240,128]{2,1,0:T(8,128)(2,1)}, bf16[16,240,128]{2,1,0:T(8,128)(2,1)}, bf16[16,240,128]{2,1,0:T(8,128)(2,1)}, bf16[16,2...) fusion(bf16[128,240,128]{2,1,0:T(8,128)(2,1)} %bitcast.46, s32[]{:T(128)S(6)} %select_n.81, ...), kind=kLoop, calls=%fused_computation.30 | loop fusion | bytes 11796504 | tf_op jit(solution)/shard_map/dynamic_slice | solution.py:183
  35.1 1.0 collective-permute-start.6
  36.1 1.5 collective-permute-start.7
  37.7 0.1 pad_add_fusion.4
  37.7 0.1 pad_add_fusion.3
  37.8 0.0 collective-permute-done.2.x_other
  37.8 0.0 collective-permute-done.3.last_other
  37.8 5.8 %shard_map.28 = bf16[4,2,2,16,16,128]{5,4,3,2,1,0:T(8,128)(2,1)} custom-call(s32[3]{0:T(128)S(1)} %get-tuple-element.33.scalars, bf16[128,240,128]{2,1,0:T(8,128)(2,1)} %bitcast.47, bf16[16,240,128]{2,1,0:T(8,128)(2,1)S(1)} %collective-permute-done.x_mine, bf16[16,240,128]{2,1,0:T(8,128)(2,1)S(1)} %collective-permute-done.1.y_mine, ...), custom_call_target="tpu_custom_call" | custom-call | flops 503316480 | bytes 5963776 | tf_op jit(solution)/shard_map/pallas_call | solution.py:93
  43.6 4.9 %all-to-all-start = ((bf16[4,2,2,16,16,128]{5,4,3,2,1,0:T(8,128)(2,1)}), bf16[4,2,2,16,16,128]{5,4,3,2,1,0:T(8,128)(2,1)}, u32[]{:S(2)}, u32[]{:S(2)}) async-start(bf16[4,2,2,16,16,128]{5,4,3,2,1,0:T(8,128)(2,1)} %shard_map.28), calls=%async_computation | async-start | bytes 2097152 | tf_op jit(solution)/shard_map/all_to_all | solution.py:199
  48.5 11.1 %collective-permute-done.6.x_mine = bf16[16,240,128]{2,1,0:T(8,128)(2,1)} collective-permute-done((bf16[16,240,128]{2,1,0:T(8,128)(2,1)}, bf16[16,240,128]{2,1,0:T(8,128)(2,1)}, u32[]{:S(2)}, u32[]{:S(2)}) %collective-permute-start.6) | collective-permute-done | bytes 983072 | tf_op jit(solution)/shard_map/ppermute | solution.py:17
  59.6 0.1 collective-permute-done.7.y_mine
  59.7 0.1 broadcast_select_fusion.2
  59.9 1.7 collective-permute-start.9
  61.5 1.2 collective-permute-start.12
  62.7 1.5 collective-permute-start.13
  64.3 5.7 %shard_map.29 = bf16[4,2,2,16,16,128]{5,4,3,2,1,0:T(8,128)(2,1)} custom-call(s32[3]{0:T(128)S(1)} %get-tuple-element.32.scalars, bf16[128,240,128]{2,1,0:T(8,128)(2,1)} %bitcast.48, bf16[16,240,128]{2,1,0:T(8,128)(2,1)} %collective-permute-done.6.x_mine, bf16[16,240,128]{2,1,0:T(8,128)(2,1)S(1)} %collective-permute-done.7.y_mine, ...), custom_call_target="tpu_custom_call" | custom-call | flops 503316480 | bytes 5963776 | tf_op jit(solution)/shard_map/pallas_call | solution.py:93
  69.9 4.0 %all-to-all-done = bf16[4,2,2,16,16,128]{5,4,3,2,1,0:T(8,128)(2,1)} async-done(((bf16[4,2,2,16,16,128]{5,4,3,2,1,0:T(8,128)(2,1)}), bf16[4,2,2,16,16,128]{5,4,3,2,1,0:T(8,128)(2,1)}, u32[]{:S(2)}, u32[]{:S(2)}) %all-to-all-start) | async-done | bytes 1048608 | tf_op jit(solution)/shard_map/all_to_all | solution.py:199
  74.0 4.2 %all-to-all-start.1 = ((bf16[4,2,2,16,16,128]{5,4,3,2,1,0:T(8,128)(2,1)}), bf16[4,2,2,16,16,128]{5,4,3,2,1,0:T(8,128)(2,1)}, u32[]{:S(2)}, u32[]{:S(2)}) async-start(bf16[4,2,2,16,16,128]{5,4,3,2,1,0:T(8,128)(2,1)} %shard_map.29), calls=%async_computation.1 | async-start | bytes 2097152 | tf_op jit(solution)/shard_map/all_to_all | solution.py:199
  78.2 7.3 %collective-permute-done.12.x_mine = bf16[16,240,128]{2,1,0:T(8,128)(2,1)S(1)} collective-permute-done((bf16[16,240,128]{2,1,0:T(8,128)(2,1)}, bf16[16,240,128]{2,1,0:T(8,128)(2,1)S(1)}, u32[]{:S(2)}, u32[]{:S(2)}) %collective-permute-start.12) | collective-permute-done | bytes 983072 | tf_op jit(solution)/shard_map/ppermute | solution.py:17
  85.5 1.3 collective-permute-done.13.y_mine
  86.8 0.1 broadcast_select_fusion.1
  86.9 0.7 collective-permute-start.15
  87.6 1.1 collective-permute-start.18
  88.7 1.5 collective-permute-start.19
  90.2 5.3 %shard_map.30 = bf16[4,2,2,16,16,128]{5,4,3,2,1,0:T(8,128)(2,1)} custom-call(s32[3]{0:T(128)S(1)} %get-tuple-element.31.scalars, bf16[128,240,128]{2,1,0:T(8,128)(2,1)} %bitcast.49, bf16[16,240,128]{2,1,0:T(8,128)(2,1)S(1)} %collective-permute-done.12.x_mine, bf16[16,240,128]{2,1,0:T(8,128)(2,1)S(1)} %collective-permute-done.13.y_mine, ...), custom_call_target="tpu_custom_call" | custom-call | flops 503316480 | bytes 5963776 | tf_op jit(solution)/shard_map/pallas_call | solution.py:93
  95.5 8.0 %all-to-all-done.1 = bf16[4,2,2,16,16,128]{5,4,3,2,1,0:T(8,128)(2,1)} async-done(((bf16[4,2,2,16,16,128]{5,4,3,2,1,0:T(8,128)(2,1)}), bf16[4,2,2,16,16,128]{5,4,3,2,1,0:T(8,128)(2,1)}, u32[]{:S(2)}, u32[]{:S(2)}) %all-to-all-start.1) | async-done | bytes 1048608 | tf_op jit(solution)/shard_map/all_to_all | solution.py:199
  103.5 3.5 %all-to-all-start.2 = ((bf16[4,2,2,16,16,128]{5,4,3,2,1,0:T(8,128)(2,1)}), bf16[4,2,2,16,16,128]{5,4,3,2,1,0:T(8,128)(2,1)S(1)}, u32[]{:S(2)}, u32[]{:S(2)}) async-start(bf16[4,2,2,16,16,128]{5,4,3,2,1,0:T(8,128)(2,1)} %shard_map.30), calls=%async_computation.2 | async-start | bytes 2097152 | tf_op jit(solution)/shard_map/all_to_all | solution.py:199
  107.0 4.6 %collective-permute-done.18.x_mine = bf16[16,240,128]{2,1,0:T(8,128)(2,1)} collective-permute-done((bf16[16,240,128]{2,1,0:T(8,128)(2,1)}, bf16[16,240,128]{2,1,0:T(8,128)(2,1)}, u32[]{:S(2)}, u32[]{:S(2)}) %collective-permute-start.18) | collective-permute-done | bytes 983072 | tf_op jit(solution)/shard_map/ppermute | solution.py:17
  111.7 1.1 collective-permute-done.19.y_mine
  112.7 0.1 broadcast_select_fusion
  112.9 0.7 collective-permute-start.21
  113.6 0.9 collective-permute-done.20.x_other
  114.4 1.3 collective-permute-done.21.last_other
  115.8 5.6 %shard_map.31 = bf16[4,2,2,16,16,128]{5,4,3,2,1,0:T(8,128)(2,1)} custom-call(s32[3]{0:T(128)S(1)} %get-tuple-element.11.scalars, bf16[128,240,128]{2,1,0:T(8,128)(2,1)} %bitcast.50, bf16[16,240,128]{2,1,0:T(8,128)(2,1)} %collective-permute-done.18.x_mine, bf16[16,240,128]{2,1,0:T(8,128)(2,1)S(1)} %collective-permute-done.19.y_mine, ...), custom_call_target="tpu_custom_call" | custom-call | flops 503316480 | bytes 5963776 | tf_op jit(solution)/shard_map/pallas_call | solution.py:93
  121.4 10.8 %all-to-all-done.2 = bf16[4,2,2,16,16,128]{5,4,3,2,1,0:T(8,128)(2,1)S(1)} async-done(((bf16[4,2,2,16,16,128]{5,4,3,2,1,0:T(8,128)(2,1)}), bf16[4,2,2,16,16,128]{5,4,3,2,1,0:T(8,128)(2,1)S(1)}, u32[]{:S(2)}, u32[]{:S(2)}) %all-to-all-start.2) | async-done | bytes 1048608 | tf_op jit(solution)/shard_map/all_to_all | solution.py:199
  132.2 4.3 %all-to-all-start.3 = ((bf16[4,2,2,16,16,128]{5,4,3,2,1,0:T(8,128)(2,1)}), bf16[4,2,2,16,16,128]{5,4,3,2,1,0:T(8,128)(2,1)}, u32[]{:S(2)}, u32[]{:S(2)}) async-start(bf16[4,2,2,16,16,128]{5,4,3,2,1,0:T(8,128)(2,1)} %shard_map.31), calls=%async_computation.3 | async-start | bytes 2097152 | tf_op jit(solution)/shard_map/all_to_all | solution.py:199
  136.5 0.1 iota_add_fusion
  136.6 0.1 add.105
  136.7 0.1 reshape.196
  136.8 0.1 mul.170
  136.9 2.4 %slice_bitcast_fusion.6 = (bf16[4,2,16,16,128]{4,3,2,1,0:T(8,128)(2,1)}, bf16[4,2,16,16,128]{4,3,2,1,0:T(8,128)(2,1)}) fusion(bf16[4,2,2,16,16,128]{5,4,3,2,1,0:T(8,128)(2,1)} %all-to-all-done), kind=kLoop, calls=%fused_computation.24 | loop fusion | bytes 2097152 | tf_op jit(solution)/shard_map/squeeze | solution.py:200
  139.3 1.5 collective-permute-start.4
  140.8 2.4 %collective-permute-start.5 = (bf16[4,2,16,16,128]{4,3,2,1,0:T(8,128)(2,1)}, bf16[4,2,16,16,128]{4,3,2,1,0:T(8,128)(2,1)S(1)}, u32[]{:S(2)}, u32[]{:S(2)}) collective-permute-start(bf16[4,2,16,16,128]{4,3,2,1,0:T(8,128)(2,1)} %get-tuple-element.27), channel_id=1, source_target_pairs={{0,16},{4,20},{8,8},{12,12},{16,0},{20,4},{24,24},{28,28},{1,17},{... | collective-permute-start | bytes 1572872 | tf_op jit(solution)/shard_map/ppermute | solution.py:17
  143.3 2.2 %slice_bitcast_fusion.4 = (bf16[4,2,16,16,128]{4,3,2,1,0:T(8,128)(2,1)S(1)}, bf16[4,2,16,16,128]{4,3,2,1,0:T(8,128)(2,1)}) fusion(bf16[4,2,2,16,16,128]{5,4,3,2,1,0:T(8,128)(2,1)} %all-to-all-done.1), kind=kLoop, calls=%fused_computation.22 | loop fusion | bytes 2097152 | tf_op jit(solution)/shard_map/squeeze | solution.py:200
  145.5 3.4 %collective-permute-start.11 = (bf16[4,2,16,16,128]{4,3,2,1,0:T(8,128)(2,1)S(1)}, bf16[4,2,16,16,128]{4,3,2,1,0:T(8,128)(2,1)S(1)}, u32[]{:S(2)}, u32[]{:S(2)}) collective-permute-start(bf16[4,2,16,16,128]{4,3,2,1,0:T(8,128)(2,1)S(1)} %get-tuple-element.25), channel_id=1, source_target_pairs={{0,16},{4,20},{8,8},{12,12},{16,0},{20,4},{24,24},{28,28},{1,17},{... | collective-permute-start | bytes 1572872 | tf_op jit(solution)/shard_map/ppermute | solution.py:17
  148.9 1.2 slice_bitcast_fusion.2
  150.1 11.7 %all-to-all-done.3 = bf16[4,2,2,16,16,128]{5,4,3,2,1,0:T(8,128)(2,1)} async-done(((bf16[4,2,2,16,16,128]{5,4,3,2,1,0:T(8,128)(2,1)}), bf16[4,2,2,16,16,128]{5,4,3,2,1,0:T(8,128)(2,1)}, u32[]{:S(2)}, u32[]{:S(2)}) %all-to-all-start.3) | async-done | bytes 1048608 | tf_op jit(solution)/shard_map/all_to_all | solution.py:199
  161.8 1.5 slice_bitcast_fusion
  163.3 2.4 %collective-permute-start.17 = (bf16[4,2,16,16,128]{4,3,2,1,0:T(8,128)(2,1)S(1)}, bf16[4,2,16,16,128]{4,3,2,1,0:T(8,128)(2,1)S(1)}, u32[]{:S(2)}, u32[]{:S(2)}) collective-permute-start(bf16[4,2,16,16,128]{4,3,2,1,0:T(8,128)(2,1)S(1)} %copy-done.2), channel_id=1, source_target_pairs={{0,16},{4,20},{8,8},{12,12},{16,0},{20,4},{24,24},{28,28},{1,17},{... | collective-permute-start | bytes 1572872 | tf_op jit(solution)/shard_map/ppermute | solution.py:17
  165.7 0.1 collective-permute-start.22
  165.8 3.4 %collective-permute-start.23 = (bf16[4,2,16,16,128]{4,3,2,1,0:T(8,128)(2,1)S(1)}, bf16[4,2,16,16,128]{4,3,2,1,0:T(8,128)(2,1)S(1)}, u32[]{:S(2)}, u32[]{:S(2)}) collective-permute-start(bf16[4,2,16,16,128]{4,3,2,1,0:T(8,128)(2,1)S(1)} %get-tuple-element.21), channel_id=1, source_target_pairs={{0,16},{4,20},{8,8},{12,12},{16,0},{20,4},{24,24},{28,28},{1,17},{... | collective-permute-start | bytes 1572872 | tf_op jit(solution)/shard_map/ppermute | solution.py:17
  169.2 9.2 %multiply_convert_fusion.1 = (bf16[1,512,1024]{2,1,0:T(8,128)(2,1)S(1)}, bf16[1,512,1024]{2,1,0:T(8,128)(2,1)S(1)}) fusion(s32[512]{0:T(512)S(1)} %add.105, f32[512]{0:T(512)S(1)} %mul.170, f32[512]{0:T(512)S(1)} %neg.8), kind=kLoop, calls=%fused_computation.8 | loop fusion | flops 9437184 | bytes 2103296 | tf_op jit(solution)/shard_map/convert
  178.4 1.5 pad_maximum_fusion
  180.0 0.0 collective-permute-done.17.refs_5_
  180.0 6.1 %collective-permute-done.22.refs_6_ = bf16[4,2,16,16,128]{4,3,2,1,0:T(8,128)(2,1)S(1)} collective-permute-done((bf16[4,2,16,16,128]{4,3,2,1,0:T(8,128)(2,1)S(1)}, bf16[4,2,16,16,128]{4,3,2,1,0:T(8,128)(2,1)S(1)}, u32[]{:S(2)}, u32[]{:S(2)}) %collective-permute-start.22) | collective-permute-done | bytes 524320 | tf_op jit(solution)/shard_map/ppermute | solution.py:17
  186.1 3.2 %collective-permute-done.23.refs_7_ = bf16[4,2,16,16,128]{4,3,2,1,0:T(8,128)(2,1)S(1)} collective-permute-done((bf16[4,2,16,16,128]{4,3,2,1,0:T(8,128)(2,1)S(1)}, bf16[4,2,16,16,128]{4,3,2,1,0:T(8,128)(2,1)S(1)}, u32[]{:S(2)}, u32[]{:S(2)}) %collective-permute-start.23) | collective-permute-done | bytes 524320 | tf_op jit(solution)/shard_map/ppermute | solution.py:17
  189.3 8.9 %shard_map.32 = bf16[2,1,1024,1024]{3,2,1,0:T(8,128)(2,1)} custom-call(bf16[4,2,16,16,128]{4,3,2,1,0:T(8,128)(2,1)S(1)} %collective-permute-done.4.refs_0_, bf16[4,2,16,16,128]{4,3,2,1,0:T(8,128)(2,1)S(1)} %collective-permute-done.5.refs_1_, bf16[4,2,16,16,128]{4,3,2,1,0:T(8,128)(2,1)S(1)} %collective-permute-done.10.refs_2_, ...), custom_call_target="tpu_custom_call" | custom-call | flops 4294967296 | bytes 10485760 | tf_op jit(solution)/shard_map/pallas_call | solution.py:136
  (28 shorter events, 0.1 us)
Async XLA Ops:
  2.6 24.9 %collective-permute-start = (bf16[16,240,128]{2,1,0:T(8,128)(2,1)}, bf16[16,240,128]{2,1,0:T(8,128)(2,1)S(1)}, u32[]{:S(2)}, u32[]{:S(2)}) collective-permute-start(bf16[16,240,128]{2,1,0:T(8,128)(2,1)} %get-tuple-element.9), channel_id=1, source_target_pairs={{0,8},{4,12},{8,0},{12,4},{16,24},{20,28},{24,16},{28,20},{1,9},{5... | collective-permute-start | bytes 2949128 | tf_op jit(solution)/shard_map/ppermute | solution.py:17
  5.5 23.2 %collective-permute-start.1 = (bf16[16,240,128]{2,1,0:T(8,128)(2,1)S(1)}, bf16[16,240,128]{2,1,0:T(8,128)(2,1)S(1)}, u32[]{:S(2)}, u32[]{:S(2)}) collective-permute-start(bf16[16,240,128]{2,1,0:T(8,128)(2,1)S(1)} %get-tuple-element.10), channel_id=1, source_target_pairs={{0,16},{4,20},{8,24},{12,28},{16,0},{20,4},{24,8},{28,12},{1,17},{... | collective-permute-start | bytes 2949128 | tf_op jit(solution)/shard_map/ppermute | solution.py:17
  27.5 10.4 %collective-permute-start.2 = (bf16[16,240,128]{2,1,0:T(8,128)(2,1)S(1)}, bf16[16,240,128]{2,1,0:T(8,128)(2,1)}, u32[]{:S(2)}, u32[]{:S(2)}) collective-permute-start(bf16[16,240,128]{2,1,0:T(8,128)(2,1)S(1)} %collective-permute-done.x_mine), channel_id=1, source_target_pairs={{0,4},{4,0},{8,12},{12,8},{16,20},{20,16},{24,28},{28,24},{1,5},{5... | collective-permute-start | bytes 2949128 | tf_op jit(solution)/shard_map/ppermute | solution.py:17
  29.8 8.1 %collective-permute-start.3 = (bf16[16,240,128]{2,1,0:T(8,128)(2,1)}, bf16[16,240,128]{2,1,0:T(8,128)(2,1)}, u32[]{:S(2)}, u32[]{:S(2)}) collective-permute-start(bf16[16,240,128]{2,1,0:T(8,128)(2,1)} %broadcast_select_fusion.3), channel_id=1, source_target_pairs={{0,4},{4,0},{8,12},{12,8},{16,20},{20,16},{24,28},{28,24},{1,5},{5... | collective-permute-start | bytes 2949128 | tf_op jit(solution)/shard_map/ppermute | solution.py:17
  35.1 24.5 %collective-permute-start.6 = (bf16[16,240,128]{2,1,0:T(8,128)(2,1)}, bf16[16,240,128]{2,1,0:T(8,128)(2,1)}, u32[]{:S(2)}, u32[]{:S(2)}) collective-permute-start(bf16[16,240,128]{2,1,0:T(8,128)(2,1)} %get-tuple-element.18), channel_id=1, source_target_pairs={{0,8},{4,12},{8,0},{12,4},{16,24},{20,28},{24,16},{28,20},{1,9},{5... | collective-permute-start | bytes 2949128 | tf_op jit(solution)/shard_map/ppermute | solution.py:17
  36.1 23.6 %collective-permute-start.7 = (bf16[16,240,128]{2,1,0:T(8,128)(2,1)}, bf16[16,240,128]{2,1,0:T(8,128)(2,1)S(1)}, u32[]{:S(2)}, u32[]{:S(2)}) collective-permute-start(bf16[16,240,128]{2,1,0:T(8,128)(2,1)} %get-tuple-element.17), channel_id=1, source_target_pairs={{0,16},{4,20},{8,24},{12,28},{16,0},{20,4},{24,8},{28,12},{1,17},{... | collective-permute-start | bytes 2949128 | tf_op jit(solution)/shard_map/ppermute | solution.py:17
  43.6 30.3 %all-to-all-start = ((bf16[4,2,2,16,16,128]{5,4,3,2,1,0:T(8,128)(2,1)}), bf16[4,2,2,16,16,128]{5,4,3,2,1,0:T(8,128)(2,1)}, u32[]{:S(2)}, u32[]{:S(2)}) async-start(bf16[4,2,2,16,16,128]{5,4,3,2,1,0:T(8,128)(2,1)} %shard_map.28), calls=%async_computation | async-start | bytes 2097152 | tf_op jit(solution)/shard_map/all_to_all | solution.py:199
  59.6 4.6 %collective-permute-start.8 = (bf16[16,240,128]{2,1,0:T(8,128)(2,1)}, bf16[16,240,128]{2,1,0:T(8,128)(2,1)S(1)}, u32[]{:S(2)}, u32[]{:S(2)}) collective-permute-start(bf16[16,240,128]{2,1,0:T(8,128)(2,1)} %collective-permute-done.6.x_mine), channel_id=1, source_target_pairs={{0,4},{4,0},{8,12},{12,8},{16,20},{20,16},{24,28},{28,24},{1,5},{5... | collective-permute-start | bytes 2949128 | tf_op jit(solution)/shard_map/ppermute | solution.py:17
  59.9 4.4 %collective-permute-start.9 = (bf16[16,240,128]{2,1,0:T(8,128)(2,1)S(1)}, bf16[16,240,128]{2,1,0:T(8,128)(2,1)S(1)}, u32[]{:S(2)}, u32[]{:S(2)}) collective-permute-start(bf16[16,240,128]{2,1,0:T(8,128)(2,1)S(1)} %broadcast_select_fusion.2), channel_id=1, source_target_pairs={{0,4},{4,0},{8,12},{12,8},{16,20},{20,16},{24,28},{28,24},{1,5},{5... | collective-permute-start | bytes 2949128 | tf_op jit(solution)/shard_map/ppermute | solution.py:17
  61.5 23.9 %collective-permute-start.12 = (bf16[16,240,128]{2,1,0:T(8,128)(2,1)}, bf16[16,240,128]{2,1,0:T(8,128)(2,1)S(1)}, u32[]{:S(2)}, u32[]{:S(2)}) collective-permute-start(bf16[16,240,128]{2,1,0:T(8,128)(2,1)} %get-tuple-element.16), channel_id=1, source_target_pairs={{0,8},{4,12},{8,0},{12,4},{16,24},{20,28},{24,16},{28,20},{1,9},{5... | collective-permute-start | bytes 2949128 | tf_op jit(solution)/shard_map/ppermute | solution.py:17
  62.7 24.0 %collective-permute-start.13 = (bf16[16,240,128]{2,1,0:T(8,128)(2,1)}, bf16[16,240,128]{2,1,0:T(8,128)(2,1)S(1)}, u32[]{:S(2)}, u32[]{:S(2)}) collective-permute-start(bf16[16,240,128]{2,1,0:T(8,128)(2,1)} %get-tuple-element.15), channel_id=1, source_target_pairs={{0,16},{4,20},{8,24},{12,28},{16,0},{20,4},{24,8},{28,12},{1,17},{... | collective-permute-start | bytes 2949128 | tf_op jit(solution)/shard_map/ppermute | solution.py:17
  74.0 29.5 %all-to-all-start.1 = ((bf16[4,2,2,16,16,128]{5,4,3,2,1,0:T(8,128)(2,1)}), bf16[4,2,2,16,16,128]{5,4,3,2,1,0:T(8,128)(2,1)}, u32[]{:S(2)}, u32[]{:S(2)}) async-start(bf16[4,2,2,16,16,128]{5,4,3,2,1,0:T(8,128)(2,1)} %shard_map.29), calls=%async_computation.1 | async-start | bytes 2097152 | tf_op jit(solution)/shard_map/all_to_all | solution.py:199
  85.5 4.7 %collective-permute-start.14 = (bf16[16,240,128]{2,1,0:T(8,128)(2,1)S(1)}, bf16[16,240,128]{2,1,0:T(8,128)(2,1)S(1)}, u32[]{:S(2)}, u32[]{:S(2)}) collective-permute-start(bf16[16,240,128]{2,1,0:T(8,128)(2,1)S(1)} %collective-permute-done.12.x_mine), channel_id=1, source_target_pairs={{0,4},{4,0},{8,12},{12,8},{16,20},{20,16},{24,28},{28,24},{1,5},{5... | collective-permute-start | bytes 2949128 | tf_op jit(solution)/shard_map/ppermute | solution.py:17
  86.9 3.3 %collective-permute-start.15 = (bf16[16,240,128]{2,1,0:T(8,128)(2,1)S(1)}, bf16[16,240,128]{2,1,0:T(8,128)(2,1)S(1)}, u32[]{:S(2)}, u32[]{:S(2)}) collective-permute-start(bf16[16,240,128]{2,1,0:T(8,128)(2,1)S(1)} %broadcast_select_fusion.1), channel_id=1, source_target_pairs={{0,4},{4,0},{8,12},{12,8},{16,20},{20,16},{24,28},{28,24},{1,5},{5... | collective-permute-start | bytes 2949128 | tf_op jit(solution)/shard_map/ppermute | solution.py:17
  87.6 24.1 %collective-permute-start.18 = (bf16[16,240,128]{2,1,0:T(8,128)(2,1)}, bf16[16,240,128]{2,1,0:T(8,128)(2,1)}, u32[]{:S(2)}, u32[]{:S(2)}) collective-permute-start(bf16[16,240,128]{2,1,0:T(8,128)(2,1)} %get-tuple-element.14), channel_id=1, source_target_pairs={{0,8},{4,12},{8,0},{12,4},{16,24},{20,28},{24,16},{28,20},{1,9},{5... | collective-permute-start | bytes 2949128 | tf_op jit(solution)/shard_map/ppermute | solution.py:17
  88.7 24.0 %collective-permute-start.19 = (bf16[16,240,128]{2,1,0:T(8,128)(2,1)}, bf16[16,240,128]{2,1,0:T(8,128)(2,1)S(1)}, u32[]{:S(2)}, u32[]{:S(2)}) collective-permute-start(bf16[16,240,128]{2,1,0:T(8,128)(2,1)} %get-tuple-element.13), channel_id=1, source_target_pairs={{0,16},{4,20},{8,24},{12,28},{16,0},{20,4},{24,8},{28,12},{1,17},{... | collective-permute-start | bytes 2949128 | tf_op jit(solution)/shard_map/ppermute | solution.py:17
  103.5 28.7 %all-to-all-start.2 = ((bf16[4,2,2,16,16,128]{5,4,3,2,1,0:T(8,128)(2,1)}), bf16[4,2,2,16,16,128]{5,4,3,2,1,0:T(8,128)(2,1)S(1)}, u32[]{:S(2)}, u32[]{:S(2)}) async-start(bf16[4,2,2,16,16,128]{5,4,3,2,1,0:T(8,128)(2,1)} %shard_map.30), calls=%async_computation.2 | async-start | bytes 2097152 | tf_op jit(solution)/shard_map/all_to_all | solution.py:199
  111.7 2.8 %collective-permute-start.20 = (bf16[16,240,128]{2,1,0:T(8,128)(2,1)}, bf16[16,240,128]{2,1,0:T(8,128)(2,1)S(1)}, u32[]{:S(2)}, u32[]{:S(2)}) collective-permute-start(bf16[16,240,128]{2,1,0:T(8,128)(2,1)} %collective-permute-done.18.x_mine), channel_id=1, source_target_pairs={{0,4},{4,0},{8,12},{12,8},{16,20},{20,16},{24,28},{28,24},{1,5},{5... | collective-permute-start | bytes 2949128 | tf_op jit(solution)/shard_map/ppermute | solution.py:17
  112.9 2.9 %collective-permute-start.21 = (bf16[16,240,128]{2,1,0:T(8,128)(2,1)S(1)}, bf16[16,240,128]{2,1,0:T(8,128)(2,1)S(1)}, u32[]{:S(2)}, u32[]{:S(2)}) collective-permute-start(bf16[16,240,128]{2,1,0:T(8,128)(2,1)S(1)} %broadcast_select_fusion), channel_id=1, source_target_pairs={{0,4},{4,0},{8,12},{12,8},{16,20},{20,16},{24,28},{28,24},{1,5},{5... | collective-permute-start | bytes 2949128 | tf_op jit(solution)/shard_map/ppermute | solution.py:17
  121.4 15.3 %copy-start.3 = (f32[512]{0:T(512)S(1)}, f32[512]{0:T(512)}, u32[]{:S(2)}) copy-start(f32[512]{0:T(512)} %param.3) | copy-start | bytes 6148
  132.2 7.1 %copy-start = (bf16[4,2,2,16,16,128]{5,4,3,2,1,0:T(8,128)(2,1)}, bf16[4,2,2,16,16,128]{5,4,3,2,1,0:T(8,128)(2,1)S(1)}, u32[]{:S(2)}) copy-start(bf16[4,2,2,16,16,128]{5,4,3,2,1,0:T(8,128)(2,1)S(1)} %all-to-all-done.2) | copy-start | bytes 3145732
  132.2 29.5 %all-to-all-start.3 = ((bf16[4,2,2,16,16,128]{5,4,3,2,1,0:T(8,128)(2,1)}), bf16[4,2,2,16,16,128]{5,4,3,2,1,0:T(8,128)(2,1)}, u32[]{:S(2)}, u32[]{:S(2)}) async-start(bf16[4,2,2,16,16,128]{5,4,3,2,1,0:T(8,128)(2,1)} %shard_map.31), calls=%async_computation.3 | async-start | bytes 2097152 | tf_op jit(solution)/shard_map/all_to_all | solution.py:199
  139.3 9.6 %copy-start.1 = (bf16[4,2,2,16,16,128]{5,4,3,2,1,0:T(8,128)(2,1)S(1)}, bf16[4,2,2,16,16,128]{5,4,3,2,1,0:T(8,128)(2,1)}, u32[]{:S(2)}) copy-start(bf16[4,2,2,16,16,128]{5,4,3,2,1,0:T(8,128)(2,1)} %copy-done) | copy-start | bytes 3145732
  139.3 23.9 %collective-permute-start.4 = (bf16[4,2,16,16,128]{4,3,2,1,0:T(8,128)(2,1)}, bf16[4,2,16,16,128]{4,3,2,1,0:T(8,128)(2,1)S(1)}, u32[]{:S(2)}, u32[]{:S(2)}) collective-permute-start(bf16[4,2,16,16,128]{4,3,2,1,0:T(8,128)(2,1)} %get-tuple-element.28), channel_id=1, source_target_pairs={{0,8},{4,12},{8,0},{12,4},{16,24},{20,28},{24,16},{28,20},{1,9},{5... | collective-permute-start | bytes 1572872 | tf_op jit(solution)/shard_map/ppermute | solution.py:17
  140.8 24.8 %collective-permute-start.5 = (bf16[4,2,16,16,128]{4,3,2,1,0:T(8,128)(2,1)}, bf16[4,2,16,16,128]{4,3,2,1,0:T(8,128)(2,1)S(1)}, u32[]{:S(2)}, u32[]{:S(2)}) collective-permute-start(bf16[4,2,16,16,128]{4,3,2,1,0:T(8,128)(2,1)} %get-tuple-element.27), channel_id=1, source_target_pairs={{0,16},{4,20},{8,8},{12,12},{16,0},{20,4},{24,24},{28,28},{1,17},{... | collective-permute-start | bytes 1572872 | tf_op jit(solution)/shard_map/ppermute | solution.py:17
  145.5 20.3 %collective-permute-start.10 = (bf16[4,2,16,16,128]{4,3,2,1,0:T(8,128)(2,1)}, bf16[4,2,16,16,128]{4,3,2,1,0:T(8,128)(2,1)S(1)}, u32[]{:S(2)}, u32[]{:S(2)}) collective-permute-start(bf16[4,2,16,16,128]{4,3,2,1,0:T(8,128)(2,1)} %get-tuple-element.26), channel_id=1, source_target_pairs={{0,8},{4,12},{8,0},{12,4},{16,24},{20,28},{24,16},{28,20},{1,9},{5... | collective-permute-start | bytes 1572872 | tf_op jit(solution)/shard_map/ppermute | solution.py:17
  145.5 34.5 %collective-permute-start.11 = (bf16[4,2,16,16,128]{4,3,2,1,0:T(8,128)(2,1)S(1)}, bf16[4,2,16,16,128]{4,3,2,1,0:T(8,128)(2,1)S(1)}, u32[]{:S(2)}, u32[]{:S(2)}) collective-permute-start(bf16[4,2,16,16,128]{4,3,2,1,0:T(8,128)(2,1)S(1)} %get-tuple-element.25), channel_id=1, source_target_pairs={{0,16},{4,20},{8,8},{12,12},{16,0},{20,4},{24,24},{28,28},{1,17},{... | collective-permute-start | bytes 1572872 | tf_op jit(solution)/shard_map/ppermute | solution.py:17
  150.1 29.9 %collective-permute-start.16 = (bf16[4,2,16,16,128]{4,3,2,1,0:T(8,128)(2,1)}, bf16[4,2,16,16,128]{4,3,2,1,0:T(8,128)(2,1)S(1)}, u32[]{:S(2)}, u32[]{:S(2)}) collective-permute-start(bf16[4,2,16,16,128]{4,3,2,1,0:T(8,128)(2,1)} %get-tuple-element.24), channel_id=1, source_target_pairs={{0,8},{4,12},{8,0},{12,4},{16,24},{20,28},{24,16},{28,20},{1,9},{5... | collective-permute-start | bytes 1572872 | tf_op jit(solution)/shard_map/ppermute | solution.py:17
  161.8 1.5 copy-start.2
  163.3 16.8 %collective-permute-start.17 = (bf16[4,2,16,16,128]{4,3,2,1,0:T(8,128)(2,1)S(1)}, bf16[4,2,16,16,128]{4,3,2,1,0:T(8,128)(2,1)S(1)}, u32[]{:S(2)}, u32[]{:S(2)}) collective-permute-start(bf16[4,2,16,16,128]{4,3,2,1,0:T(8,128)(2,1)S(1)} %copy-done.2), channel_id=1, source_target_pairs={{0,16},{4,20},{8,8},{12,12},{16,0},{20,4},{24,24},{28,28},{1,17},{... | collective-permute-start | bytes 1572872 | tf_op jit(solution)/shard_map/ppermute | solution.py:17
  165.7 20.4 %collective-permute-start.22 = (bf16[4,2,16,16,128]{4,3,2,1,0:T(8,128)(2,1)S(1)}, bf16[4,2,16,16,128]{4,3,2,1,0:T(8,128)(2,1)S(1)}, u32[]{:S(2)}, u32[]{:S(2)}) collective-permute-start(bf16[4,2,16,16,128]{4,3,2,1,0:T(8,128)(2,1)S(1)} %get-tuple-element.22), channel_id=1, source_target_pairs={{0,8},{4,12},{8,0},{12,4},{16,24},{20,28},{24,16},{28,20},{1,9},{5... | collective-permute-start | bytes 1572872 | tf_op jit(solution)/shard_map/ppermute | solution.py:17
  165.8 23.5 %collective-permute-start.23 = (bf16[4,2,16,16,128]{4,3,2,1,0:T(8,128)(2,1)S(1)}, bf16[4,2,16,16,128]{4,3,2,1,0:T(8,128)(2,1)S(1)}, u32[]{:S(2)}, u32[]{:S(2)}) collective-permute-start(bf16[4,2,16,16,128]{4,3,2,1,0:T(8,128)(2,1)S(1)} %get-tuple-element.21), channel_id=1, source_target_pairs={{0,16},{4,20},{8,8},{12,12},{16,0},{20,4},{24,24},{28,28},{1,17},{... | collective-permute-start | bytes 1572872 | tf_op jit(solution)/shard_map/ppermute | solution.py:17

commit v2 on v1

v2 whole, which is shorter than its diff:
```python
import functools
import math

import jax
import jax.numpy as jnp
from jax import lax
from jax.experimental import pallas as pl
from jax.experimental.pallas import tpu as pltpu
from jax.sharding import PartitionSpec as P

ROUNDS = 2
CHUNK = 16
STRAIGHT = 1
VMEM = 48 * 1024 * 1024
LITTLE = 8 * 1024 * 1024


def permuted(value, target):
    count = lax.axis_size("grp")
    return lax.ppermute(value, "grp", [(source, target(source) % count) for source in range(count)])


def permuted_far(value, target, distance):
    groups, shards = lax.axis_size("grp"), lax.axis_size("frq")
    return lax.ppermute(
        value,
        ("grp", "frq"),
        [
            (group * shards + shard, (target(group) % groups) * shards + (shard + distance) % shards)
            for group in range(groups)
            for shard in range(shards)
        ],
    )


def is_odd(group):
    return (group // 2) % 2


def to_x(group):
    return group ^ 2


def to_y(group):
    return group + 4 if is_odd(group) else group - 4


def to_b(group):
    return group if is_odd(group) else group + 4


def to_other_core(group):
    return group ^ 1


def cross_body(shards, step_freqs, early, straight, scalars, own, x_mine, y_mine, x_other, last_other, *refs):
    outs, stage = refs[early:-1], refs[-1]
    windows, width = own.shape[1:]
    half = width // 2
    per_shard, freqs = outs[0].shape[-3:-1]
    step = pl.program_id(0)
    first_core = scalars[0] == 0
    odd = scalars[1] == 1
    scale = 1.0 / math.sqrt(windows)
    lanes = lax.broadcasted_iota(jnp.int32, (half, width), 1)
    sign = jnp.where(lanes < half, 1.0, -1.0).astype(jnp.float32)

    def products(left, rights):
        return lax.dot_general(
            left,
            jnp.concatenate(rights, 1),
            (((0,), (0,)), ((), ())),
            preferred_element_type=jnp.float32,
        )

    for at in range(step_freqs):
        center, center_other, other = x_mine[at], x_other[at], last_other[at]
        before = jnp.where(odd, y_mine[at], own[at])
        after = jnp.where(odd, own[at], y_mine[at])
        pair = [
            products(center, [jnp.where(first_core, other, center_other), before]),
            products(after, [jnp.where(first_core, center_other, other), center]),
        ]
        for bundle, product in enumerate(pair):
            for turn in range(ROUNDS):
                part = product[:, turn * width : (turn + 1) * width]
                top, bottom = part[:half], part[half:]
                value = (top * sign + pltpu.roll(bottom, half, 1)) * scale
                base = (bundle * ROUNDS + turn) * half * freqs
                stage[pl.ds(base + step * step_freqs + at, half, stride=freqs), :] = value

    @pl.when(step == pl.num_programs(0) - 1)
    def _():
        for index in range(shards):
            shard = lax.rem(scalars[3] + index, shards) if straight else index
            for bundle in range(2):
                for turn in range(ROUNDS):
                    base = ((bundle * ROUNDS + turn) * half + shard * per_shard) * freqs
                    if straight:
                        base = pl.multiple_of(base, 8)
                    rows = stage[pl.ds(base, per_shard * freqs), :]
                    rows = rows.reshape(per_shard, freqs, width).astype(jnp.bfloat16)
                    if straight:
                        outs[bundle * shards + index][turn] = rows
                    else:
                        outs[0][index, bundle, turn] = rows


def cross_spectra(scalars, spectra, x_mine, y_mine, x_other, last_other, earlier, shards, straight):
    freqs, windows, width = x_mine.shape
    step_freqs = math.gcd(freqs, 4)
    half = width // 2
    block = (step_freqs, windows, width)
    plain = pl.BlockSpec(block, lambda step, scalars: (step, 0, 0))
    out_shape = (ROUNDS, half // shards, freqs, width)
    if not straight:
        out_shape = (shards, 2) + out_shape
    count = 2 * shards if straight else 1
    return pl.pallas_call(
        functools.partial(cross_body, shards, step_freqs, len(earlier), straight),
        out_shape=[jax.ShapeDtypeStruct(out_shape, jnp.bfloat16)] * count,
        grid_spec=pltpu.PrefetchScalarGridSpec(
            num_scalar_prefetch=1,
            grid=(freqs // step_freqs,),
            in_specs=[
                pl.BlockSpec(block, lambda step, scalars: (scalars[2] * (freqs // step_freqs) + step, 0, 0))
            ]
            + [plain] * 4
            + in_hbm(len(earlier)),
            out_specs=[pl.BlockSpec(out_shape, lambda step, scalars: (0,) * len(out_shape))] * count,
            scratch_shapes=[pltpu.VMEM((2 * ROUNDS * half * freqs, width), jnp.float32)],
        ),
        compiler_params=pltpu.CompilerParams(vmem_limit_bytes=VMEM),
        cost_estimate=pl.CostEstimate(
            flops=2 * freqs * 2 * windows * width * 2 * width,
            bytes_accessed=5 * freqs * windows * width * 2 + 4 * freqs * half * width * 2,
            transcendentals=0,
        ),
    )(scalars, spectra, x_mine, y_mine, x_other, last_other, *earlier)


def in_hbm(count):
    return [pl.BlockSpec(memory_space=pltpu.HBM)] * count


def last_body(scalars, own, y_mine, *refs):
    refs[-1][...] = jnp.where(scalars[0] == scalars[1], y_mine[...], own[...])


def last_after(scalars, own, y_mine, waits):
    return pl.pallas_call(
        last_body,
        out_shape=jax.ShapeDtypeStruct(y_mine.shape, jnp.bfloat16),
        in_specs=[pl.BlockSpec(memory_space=pltpu.SMEM)]
        + [pl.BlockSpec(memory_space=pltpu.VMEM)] * 2
        + in_hbm(len(waits)),
        out_specs=pl.BlockSpec(memory_space=pltpu.VMEM),
        compiler_params=pltpu.CompilerParams(vmem_limit_bytes=LITTLE),
        cost_estimate=pl.CostEstimate(flops=0, bytes_accessed=6 * y_mine.size, transcendentals=0),
    )(scalars, own, y_mine, *waits)


def bundles_body(spread, *refs):
    for bundle in range(2):
        refs[-2 + bundle][...] = spread[:, bundle]


def bundles_after(spread, waits):
    shape = jax.ShapeDtypeStruct(spread.shape[:1] + spread.shape[2:], spread.dtype)
    return pl.pallas_call(
        bundles_body,
        out_shape=[shape] * 2,
        in_specs=[pl.BlockSpec(memory_space=pltpu.VMEM)] + in_hbm(len(waits)),
        out_specs=[pl.BlockSpec(memory_space=pltpu.VMEM)] * 2,
        compiler_params=pltpu.CompilerParams(vmem_limit_bytes=LITTLE),
        cost_estimate=pl.CostEstimate(flops=0, bytes_accessed=4 * spread.size, transcendentals=0),
    )(spread, *waits)


def lag_body(order, *refs):
    count = len(order)
    blocks = [refs[order.index(at)] for at in range(count)]
    cosines, sines, *partial, out = refs[count:]
    stations, _, width = blocks[0].shape[-3:]
    half = width // 2
    real, imag = [], []
    for station in range(stations):
        spectra = []
        for block in blocks:
            if len(block.shape) == 4:
                spectra.append(block[0, station])
            else:
                spectra += [block[shard, 0, station] for shard in range(block.shape[0])]
        turned = jnp.concatenate(spectra, 0).T
        real.append(turned[:half])
        imag.append(turned[half:])
    lagged = jnp.dot(jnp.concatenate(real, 0), cosines[...], preferred_element_type=jnp.float32)
    lagged += jnp.dot(jnp.concatenate(imag, 0), sines[...], preferred_element_type=jnp.float32)
    if partial:
        lagged += partial[0][0, 0]
    out[0, 0] = lagged.astype(out.dtype)


def to_lags(blocks, order, cosines, sines, part, partial, kind):
    rounds, stations, freqs, width = blocks[0].shape[-4:]
    half = width // 2
    rows = sum(block.size for block in blocks) // (rounds * stations * width)
    lags = cosines.shape[1]
    step = math.gcd(stations, 8)

    def spec(block):
        if block.ndim == 4:
            return pl.BlockSpec((1, step, freqs, width), lambda turn, at: (turn, at, 0, 0))
        return pl.BlockSpec((block.shape[0], 1, step, freqs, width), lambda turn, at: (0, turn, at, 0, 0))

    table = pl.BlockSpec((rows, lags), lambda turn, at: (part, 0))
    lagged = pl.BlockSpec((1, 1, step * half, lags), lambda turn, at: (turn, 0, at, 0))
    return pl.pallas_call(
        functools.partial(lag_body, order),
        out_shape=jax.ShapeDtypeStruct((rounds, 1, stations * half, lags), kind),
        grid=(rounds, stations // step),
        in_specs=[spec(blocks[at]) for at in order] + [table] * 2 + [lagged] * len(partial),
        out_specs=lagged,
        compiler_params=pltpu.CompilerParams(vmem_limit_bytes=VMEM),
        cost_estimate=pl.CostEstimate(
            flops=2 * rounds * stations * half * 2 * rows * lags,
            bytes_accessed=2 * (rounds * stations * half * (2 * rows + lags) + 2 * rows * lags),
            transcendentals=0,
        ),
    )(*[blocks[at] for at in order], cosines, sines, *partial)


def inverse_table(band_weight, shard, odd, chunks, straight):
    bins = band_weight.shape[0]
    shards = lax.axis_size("frq")
    lags = 2 * bins
    size = bins // (shards * 2 * chunks)

    weights = band_weight.reshape(shards, 2, chunks, size)
    weights = jnp.where(odd == 0, weights[:, ::-1], weights).transpose(2, 1, 0, 3)
    backward = jnp.concatenate([weights[:, :, ::-1]] * 2, 2)
    backward = lax.dynamic_slice_in_dim(backward, shards - 1 - shard, shards, 2)
    weights = jnp.concatenate([weights[: chunks - straight], backward[chunks - straight :]], 0).reshape(bins)

    dims = (chunks, 2, shards, size)
    chunk, bundle, place, offset = (lax.broadcasted_iota(jnp.int32, dims, at) for at in range(4))
    source = jnp.where(chunk < chunks - straight, place, (shard + shards - place) % shards)
    indices = ((source * 2 + (bundle ^ 1 ^ odd)) * chunks + chunk) * size + offset
    indices = indices.reshape(bins)
    phase_index = indices[:, None] * jnp.arange(lags, dtype=jnp.int32)[None, :] % lags
    phase_angle = phase_index.astype(jnp.float32) * (2.0 * math.pi / lags)
    weighting = weights[:, None] * (1.0 / math.sqrt(bins))
    return (
        (weighting * jnp.cos(phase_angle)).astype(jnp.bfloat16),
        (-weighting * jnp.sin(phase_angle)).astype(jnp.bfloat16),
    )


def local(spectra, band_weight):
    shards = lax.axis_size("frq")
    group = lax.axis_index("grp").astype(jnp.int32)
    shard = lax.axis_index("frq").astype(jnp.int32)
    core, odd = group & 1, (group >> 1) & 1
    block = spectra[0]
    half_size = block.shape[0] // 2
    chunks = max(1, half_size // CHUNK)
    size = half_size // chunks
    straight = min(STRAIGHT, chunks)
    cosines, sines = inverse_table(band_weight, shard, odd, chunks, straight)

    def piece(source, half, chunk):
        return lax.dynamic_slice_in_dim(source, (half * chunks + chunk) * size, size, 0)

    sent, later = [], []
    source = block
    for chunk in range(chunks):
        x_piece, y_piece = piece(source, 1 - odd, chunk), piece(source, odd, chunk)
        x_piece, y_piece, source = lax.optimization_barrier((x_piece, y_piece, source))
        sent.append((y_piece, permuted(x_piece, to_x), permuted(y_piece, to_y)))
        if chunk:
            later += [x_piece, y_piece]

    spreads, blocks = [], [None] * chunks
    for chunk, (own, x_mine, y_mine) in enumerate(sent):
        scalars = jnp.stack([core, odd, odd * chunks + chunk, shard])
        x_other = permuted(x_mine, to_other_core)
        if chunk == 0:
            last = last_after(scalars, own, y_mine, later + [cosines, sines])
        else:
            last = jnp.where(odd == core, y_mine, own)
        last_other = permuted(last, to_other_core)
        is_straight = chunk >= chunks - straight
        waits = blocks[chunk - 3] if chunk >= 3 else []
        results = cross_spectra(
            scalars, block, x_mine, y_mine, x_other, last_other, waits, shards, is_straight
        )
        if is_straight:
            if spreads:
                pair = bundles_after(spreads[-1], results[:1])
                blocks[len(spreads) - 1] = [permuted(pair[0], to_x), permuted(pair[1], to_b)]
            arrived = {}
            for bundle, target in ((1, to_b), (0, to_x)):
                for distance in sorted(range(shards), key=lambda distance: -min(distance, shards - distance)):
                    at = bundle * shards + distance
                    arrived[at] = permuted_far(results[at], target, distance)
            blocks[chunk] = [arrived[at] for at in range(2 * shards)]
        else:
            spread = lax.all_to_all(results[0], "frq", split_axis=0, concat_axis=0, tiled=True)
            spreads.append(spread)
            if chunk + 1 < chunks - straight:
                blocks[chunk] = [permuted(spread[:, 0], to_x), permuted(spread[:, 1], to_b)]
    partial, part = [], 0
    if chunks == 4:
        early = blocks[0] + blocks[1]
        partial = [to_lags(early, range(len(early)), cosines, sines, 0, [], jnp.float32)]
        blocks, part = blocks[2:], 1
    beside = [at + len(sum(blocks[:-1], [])) for at in range(shards, 2 * shards)]
    over = [at - shards for at in beside]
    order = beside + list(range(over[0])) + over
    return to_lags(sum(blocks, []), order, cosines, sines, part, partial, jnp.bfloat16)


def solution(mesh):
    return jax.shard_map(
        local,
        mesh=mesh,
        in_specs=(P("grp", "frq", None, None), P()),
        out_specs=P(None, "grp", "frq", None),
        check_vma=False,
    )
```

time: 199 us -> 190 us (0.955)
  waiting for transfers between devices: 93.2 us -> 68 us
  local copies, waits for them, and re-layouts: 15.5 us -> 21.7 us
  Pallas kernels: 31.3 us -> 36.2 us
  starting transfers between devices: 45.5 us -> 48.7 us
    all_to_all x4 -> x3, waiting for transfers between devices: 34.5 us -> 11.7 us  [local(): lax.all_to_all(results[0], 'frq', split_axis=0, concat_axis=0, tiled=True)]
    ppermute x24 -> x22, waiting for transfers between devices: 58.7 us -> 36.4 us  [permuted(): lax.ppermute(value, 'grp', [(source, target(source) % count) for source i...]
    ppermute x0 -> x8, waiting for transfers between devices: none -> 19.8 us  [permuted_far(): lax.ppermute(value, ('grp', 'frq'), [(group * shards + shard, target(grou...]
    ppermute x0 -> x8, starting transfers between devices: none -> 12.3 us  [permuted_far(): lax.ppermute(value, ('grp', 'frq'), [(group * shards + shard, target(grou...]
    another operation x4 -> x2, other arithmetic: 10.9 us -> 0.15 us  [local(): scalars = jnp.stack([core, odd, odd * chunks + chunk, shard])]
    convert_element_type x0 -> x1, other arithmetic: none -> 9.2 us  [inverse_table(): (-weighting * jnp.sin(phase_angle)).astype(jnp.bfloat16)]
    unnamed x8 -> x18, local copies, waits for them, and re-layouts: 0.01 us -> 6.13 us
    ppermute x24 -> x22, starting transfers between devices: 28.7 us -> 23 us  [permuted(): lax.ppermute(value, 'grp', [(source, target(source) % count) for source i...]
  transfers between devices with their start and end apart: 28 -> 33, of which waited for: 16 -> 16; matrix products, arithmetic and copies ran while one was open for 13% -> 14% of each run, Pallas kernels for 11% -> 15%
where the time goes in v2:
time: 190 us; the launch traced here: 188 us
  waiting for transfers between devices  68 us (36%)
  starting transfers between devices  48.7 us (26%)
  Pallas kernels  36.2 us (19%)
  local copies, waits for them, and re-layouts  21.7 us (11%)
  other arithmetic  13.4 us (7%)
    ppermute x22, waiting for transfers between devices, permuted(): lax.ppermute(value, 'grp', [(source, target(source) % count) for source i...  36.4 us
    ppermute x22, starting transfers between devices, permuted(): lax.ppermute(value, 'grp', [(source, target(source) % count) for source i...  23 us
    ppermute x8, waiting for transfers between devices, permuted_far(): lax.ppermute(value, ('grp', 'frq'), [(group * shards + shard, target(grou...  19.8 us
    pallas_call x4, Pallas kernels, cross_spectra(): pl.pallas_call(functools.partial(cross_body, shards, step_freqs, len(earl...  19.5 us
    pallas_call x2, Pallas kernels, to_lags(): pl.pallas_call(functools.partial(lag_body, order), out_shape=jax.ShapeDty...  13.7 us
    all_to_all x3, starting transfers between devices, local(): lax.all_to_all(results[0], 'frq', split_axis=0, concat_axis=0, tiled=True)  13.4 us
    ppermute x8, starting transfers between devices, permuted_far(): lax.ppermute(value, ('grp', 'frq'), [(group * shards + shard, target(grou...  12.3 us
    all_to_all x3, waiting for transfers between devices, local(): lax.all_to_all(results[0], 'frq', split_axis=0, concat_axis=0, tiled=True)  11.7 us
  transfers between devices with their start and end apart: 33, of which 16 were waited for; matrix products, arithmetic and copies ran while one was open for 14% of the time, Pallas kernels for 15%

profile of v2, /device:TPU:0, one launch (start us, length us, event | category | flops | bytes accessed | tf_op | source)
XLA Modules:
  0.0 188.3 jit_solution(10797360573780463258)
XLA Ops:
  0.0 2.9 %dynamic-slice_bitcast_fusion = (bf16[16,240,128]{2,1,0:T(8,128)(2,1)}, bf16[16,240,128]{2,1,0:T(8,128)(2,1)}) fusion(bf16[1,128,240,128]{3,2,1,0:T(8,128)(2,1)} %param.2, s32[]{:T(128)S(6)} %select_n.79, s32[]{:T(128)S(6)} %select_n.78), kind=kLoop, calls=%fused_computation.11 | loop fusion | bytes 3932168 | tf_op jit(solution)/shard_map/dynamic_slice | solution.py:272
  2.9 2.9 %collective-permute-start.4 = (bf16[16,240,128]{2,1,0:T(8,128)(2,1)}, bf16[16,240,128]{2,1,0:T(8,128)(2,1)}, u32[]{:S(2)}, u32[]{:S(2)}) collective-permute-start(bf16[16,240,128]{2,1,0:T(8,128)(2,1)} %get-tuple-element.31), channel_id=1, source_target_pairs={{0,8},{4,12},{8,0},{12,4},{16,24},{20,28},{24,16},{28,20},{1,9},{5... | collective-permute-start | bytes 2949128 | tf_op jit(solution)/shard_map/ppermute | solution.py:20
  5.9 1.5 collective-permute-start.5
  7.4 3.0 %constant_dynamic-slice_fusion.4 = (bf16[16,240,128]{2,1,0:T(8,128)(2,1)}, bf16[16,240,128]{2,1,0:T(8,128)(2,1)}) fusion(bf16[128,240,128]{2,1,0:T(8,128)(2,1)} %bitcast.31, s32[]{:T(128)S(6)} %select_n.81, s32[]{:T(128)S(6)} %select_n.80), kind=kLoop, calls=%fused_computation.31 | loop fusion | bytes 3932168 | tf_op jit(solution)/shard_map/dynamic_slice | solution.py:272
  10.4 3.0 %constant_dynamic-slice_fusion.2 = (bf16[16,240,128]{2,1,0:T(8,128)(2,1)}, bf16[16,240,128]{2,1,0:T(8,128)(2,1)}) fusion(bf16[128,240,128]{2,1,0:T(8,128)(2,1)} %bitcast.32, s32[]{:T(128)S(6)} %select_n.83, s32[]{:T(128)S(6)} %select_n.82), kind=kLoop, calls=%fused_computation.29 | loop fusion | bytes 3932168 | tf_op jit(solution)/shard_map/dynamic_slice | solution.py:272
  13.4 0.1 reshape.90
  13.5 2.6 %constant_dynamic-slice_fusion = (bf16[16,240,128]{2,1,0:T(8,128)(2,1)S(1)}, bf16[16,240,128]{2,1,0:T(8,128)(2,1)}) fusion(bf16[128,240,128]{2,1,0:T(8,128)(2,1)} %bitcast.33, s32[]{:T(128)S(6)} %select_n.85, s32[]{:T(128)S(6)} %select_n.84), kind=kLoop, calls=%fused_computation.27 | loop fusion | bytes 3932168 | tf_op jit(solution)/shard_map/dynamic_slice | solution.py:272
  16.1 0.1 mul.137
  16.3 0.1 reshape.97
  16.6 9.2 %multiply_convert_fusion = (bf16[512,1024]{1,0:T(8,128)(2,1)S(1)}, bf16[512,1024]{1,0:T(8,128)(2,1)S(1)}) fusion(f32[512]{0:T(512)S(1)} %neg.8, s32[512]{0:T(512)S(1)} %reshape.97, f32[512]{0:T(512)S(1)} %mul.137), kind=kLoop, calls=%fused_computation.6 | loop fusion | flops 9437184 | bytes 2103296 | tf_op jit(solution)/shard_map/convert_element_type | solution.py:255
  25.8 2.1 %collective-permute-done.4.x_mine = bf16[16,240,128]{2,1,0:T(8,128)(2,1)} collective-permute-done((bf16[16,240,128]{2,1,0:T(8,128)(2,1)}, bf16[16,240,128]{2,1,0:T(8,128)(2,1)}, u32[]{:S(2)}, u32[]{:S(2)}) %collective-permute-start.4) | collective-permute-done | bytes 983072 | tf_op jit(solution)/shard_map/ppermute | solution.py:20
  27.9 1.5 collective-permute-done.5.y_mine
  29.4 1.8 shard_map.28
  31.2 0.8 collective-permute-start.24
  32.0 1.5 collective-permute-start.25
  33.5 0.2 collective-permute-done.7.last_other
  33.8 4.9 %shard_map.29 = bf16[4,2,2,16,16,128]{5,4,3,2,1,0:T(8,128)(2,1)S(1)} custom-call(s32[4]{0:T(128)S(1)} %get-tuple-element.64.scalars, bf16[128,240,128]{2,1,0:T(8,128)(2,1)} %bitcast.34, bf16[16,240,128]{2,1,0:T(8,128)(2,1)} %collective-permute-done.4.x_mine, bf16[16,240,128]{2,1,0:T(8,128)(2,1)} %collective-permute-done.5.y_mine, ...), custom_call_target="tpu_custom_call" | custom-call | flops 503316480 | bytes 5963776 | tf_op jit(solution)/shard_map/pallas_call | solution.py:119
  38.7 1.0 copy-done.2
  39.6 4.9 %all-to-all-start = ((bf16[4,2,2,16,16,128]{5,4,3,2,1,0:T(8,128)(2,1)}), bf16[4,2,2,16,16,128]{5,4,3,2,1,0:T(8,128)(2,1)}, u32[]{:S(2)}, u32[]{:S(2)}) async-start(bf16[4,2,2,16,16,128]{5,4,3,2,1,0:T(8,128)(2,1)} %copy-done.2), calls=%async_computation | async-start | bytes 2097152 | tf_op jit(solution)/shard_map/all_to_all | solution.py:308
  44.5 11.2 %collective-permute-done.24.x_mine = bf16[16,240,128]{2,1,0:T(8,128)(2,1)} collective-permute-done((bf16[16,240,128]{2,1,0:T(8,128)(2,1)}, bf16[16,240,128]{2,1,0:T(8,128)(2,1)}, u32[]{:S(2)}, u32[]{:S(2)}) %collective-permute-start.24) | collective-permute-done | bytes 983072 | tf_op jit(solution)/shard_map/ppermute | solution.py:20
  55.8 1.3 broadcast_select_fusion
  57.1 0.5 collective-permute-start.27
  57.6 1.3 collective-permute-start.14
  58.9 1.5 collective-permute-start.15
  60.4 4.9 %shard_map.33 = bf16[4,2,2,16,16,128]{5,4,3,2,1,0:T(8,128)(2,1)S(1)} custom-call(s32[4]{0:T(128)S(1)} %get-tuple-element.47.scalars, bf16[128,240,128]{2,1,0:T(8,128)(2,1)} %bitcast.35, bf16[16,240,128]{2,1,0:T(8,128)(2,1)} %collective-permute-done.24.x_mine, bf16[16,240,128]{2,1,0:T(8,128)(2,1)} %collective-permute-done.25.y_mine, ...), custom_call_target="tpu_custom_call" | custom-call | flops 503316480 | bytes 5963776 | tf_op jit(solution)/shard_map/pallas_call | solution.py:119
  65.3 1.0 copy-done.1
  66.3 4.3 %all-to-all-done = bf16[4,2,2,16,16,128]{5,4,3,2,1,0:T(8,128)(2,1)} async-done(((bf16[4,2,2,16,16,128]{5,4,3,2,1,0:T(8,128)(2,1)}), bf16[4,2,2,16,16,128]{5,4,3,2,1,0:T(8,128)(2,1)}, u32[]{:S(2)}, u32[]{:S(2)}) %all-to-all-start) | async-done | bytes 1048608 | tf_op jit(solution)/shard_map/all_to_all | solution.py:308
  70.6 4.3 %all-to-all-start.2 = ((bf16[4,2,2,16,16,128]{5,4,3,2,1,0:T(8,128)(2,1)}), bf16[4,2,2,16,16,128]{5,4,3,2,1,0:T(8,128)(2,1)}, u32[]{:S(2)}, u32[]{:S(2)}) async-start(bf16[4,2,2,16,16,128]{5,4,3,2,1,0:T(8,128)(2,1)} %copy-done.1), calls=%async_computation.2 | async-start | bytes 2097152 | tf_op jit(solution)/shard_map/all_to_all | solution.py:308
  74.9 6.8 %collective-permute-done.14.x_mine = bf16[16,240,128]{2,1,0:T(8,128)(2,1)} collective-permute-done((bf16[16,240,128]{2,1,0:T(8,128)(2,1)}, bf16[16,240,128]{2,1,0:T(8,128)(2,1)}, u32[]{:S(2)}, u32[]{:S(2)}) %collective-permute-start.14) | collective-permute-done | bytes 983072 | tf_op jit(solution)/shard_map/ppermute | solution.py:20
  81.7 1.4 collective-permute-done.15.y_mine
  83.1 1.3 broadcast_select_fusion.1
  84.5 0.8 collective-permute-start
  85.2 1.5 collective-permute-start.1
  86.8 0.2 collective-permute-done.17.last_other
  87.0 4.9 %shard_map.31 = bf16[4,2,2,16,16,128]{5,4,3,2,1,0:T(8,128)(2,1)S(1)} custom-call(s32[4]{0:T(128)S(1)} %get-tuple-element.63.scalars, bf16[128,240,128]{2,1,0:T(8,128)(2,1)} %bitcast.36, bf16[16,240,128]{2,1,0:T(8,128)(2,1)} %collective-permute-done.14.x_mine, bf16[16,240,128]{2,1,0:T(8,128)(2,1)} %collective-permute-done.15.y_mine, ...), custom_call_target="tpu_custom_call" | custom-call | flops 503316480 | bytes 5963776 | tf_op jit(solution)/shard_map/pallas_call | solution.py:119
  91.9 1.0 copy-done
  92.9 7.4 %all-to-all-done.2 = bf16[4,2,2,16,16,128]{5,4,3,2,1,0:T(8,128)(2,1)} async-done(((bf16[4,2,2,16,16,128]{5,4,3,2,1,0:T(8,128)(2,1)}), bf16[4,2,2,16,16,128]{5,4,3,2,1,0:T(8,128)(2,1)}, u32[]{:S(2)}, u32[]{:S(2)}) %all-to-all-start.2) | async-done | bytes 1048608 | tf_op jit(solution)/shard_map/all_to_all | solution.py:308
  100.2 4.3 %all-to-all-start.1 = ((bf16[4,2,2,16,16,128]{5,4,3,2,1,0:T(8,128)(2,1)}), bf16[4,2,2,16,16,128]{5,4,3,2,1,0:T(8,128)(2,1)}, u32[]{:S(2)}, u32[]{:S(2)}) async-start(bf16[4,2,2,16,16,128]{5,4,3,2,1,0:T(8,128)(2,1)} %copy-done), calls=%async_computation.1 | async-start | bytes 2097152 | tf_op jit(solution)/shard_map/all_to_all | solution.py:308
  104.5 4.4 %collective-permute-done.x_mine = bf16[16,240,128]{2,1,0:T(8,128)(2,1)} collective-permute-done((bf16[16,240,128]{2,1,0:T(8,128)(2,1)}, bf16[16,240,128]{2,1,0:T(8,128)(2,1)}, u32[]{:S(2)}, u32[]{:S(2)}) %collective-permute-start) | collective-permute-done | bytes 983072 | tf_op jit(solution)/shard_map/ppermute | solution.py:20
  108.9 1.3 broadcast_select_fusion.2
  110.3 1.4 slice_bitcast_fusion.2
  111.8 0.9 collective-permute-start.8
  112.7 3.6 %collective-permute-start.9 = (bf16[4,2,16,16,128]{4,3,2,1,0:T(8,128)(2,1)S(1)}, bf16[4,2,16,16,128]{4,3,2,1,0:T(8,128)(2,1)S(1)}, u32[]{:S(2)}, u32[]{:S(2)}) collective-permute-start(bf16[4,2,16,16,128]{4,3,2,1,0:T(8,128)(2,1)S(1)} %get-tuple-element.59), channel_id=1, source_target_pairs={{0,16},{4,20},{8,8},{12,12},{16,0},{20,4},{24,24},{28,28},{1,17},{... | collective-permute-start | bytes 1572872 | tf_op jit(solution)/shard_map/ppermute | solution.py:20
  116.2 2.4 %slice_bitcast_fusion = (bf16[4,2,16,16,128]{4,3,2,1,0:T(8,128)(2,1)}, bf16[4,2,16,16,128]{4,3,2,1,0:T(8,128)(2,1)}) fusion(bf16[4,2,2,16,16,128]{5,4,3,2,1,0:T(8,128)(2,1)} %all-to-all-done.2), kind=kLoop, calls=%fused_computation.16 | loop fusion | bytes 2097152 | tf_op jit(solution)/shard_map/squeeze | solution.py:311
  118.6 2.3 %collective-permute-start.29 = (bf16[4,2,16,16,128]{4,3,2,1,0:T(8,128)(2,1)}, bf16[4,2,16,16,128]{4,3,2,1,0:T(8,128)(2,1)}, u32[]{:S(2)}, u32[]{:S(2)}) collective-permute-start(bf16[4,2,16,16,128]{4,3,2,1,0:T(8,128)(2,1)} %get-tuple-element.57), channel_id=1, source_target_pairs={{0,16},{4,20},{8,8},{12,12},{16,0},{20,4},{24,24},{28,28},{1,17},{... | collective-permute-start | bytes 1572872 | tf_op jit(solution)/shard_map/ppermute | solution.py:20
  120.9 5.6 %collective-permute-done.8.refs_0_ = bf16[4,2,16,16,128]{4,3,2,1,0:T(8,128)(2,1)S(1)} collective-permute-done((bf16[4,2,16,16,128]{4,3,2,1,0:T(8,128)(2,1)S(1)}, bf16[4,2,16,16,128]{4,3,2,1,0:T(8,128)(2,1)S(1)}, u32[]{:S(2)}, u32[]{:S(2)}) %collective-permute-start.8) | collective-permute-done | bytes 524320 | tf_op jit(solution)/shard_map/ppermute | solution.py:20
  126.6 2.8 %collective-permute-done.9.refs_1_ = bf16[4,2,16,16,128]{4,3,2,1,0:T(8,128)(2,1)S(1)} collective-permute-done((bf16[4,2,16,16,128]{4,3,2,1,0:T(8,128)(2,1)S(1)}, bf16[4,2,16,16,128]{4,3,2,1,0:T(8,128)(2,1)S(1)}, u32[]{:S(2)}, u32[]{:S(2)}) %collective-permute-start.9) | collective-permute-done | bytes 524320 | tf_op jit(solution)/shard_map/ppermute | solution.py:20
  129.4 4.8 %shard_map.30 = (bf16[2,16,16,128]{3,2,1,0:T(8,128)(2,1)S(1)}, bf16[2,16,16,128]{3,2,1,0:T(8,128)(2,1)S(1)}, bf16[2,16,16,128]{3,2,1,0:T(8,128)(2,1)S(1)}, bf16[...) custom-call(s32[4]{0:T(128)S(1)} %get-tuple-element.65.scalars, ...), custom_call_target="tpu_custom_call" | custom-call | flops 503316480 | bytes 5963776 | tf_op jit(solution)/shard_map/pallas_call | solution.py:119
  134.2 0.6 copy-done.3
  134.9 0.6 copy-done.4
  135.5 0.6 copy-done.5
  136.2 0.7 copy-done.6
  136.8 0.6 copy-done.7
  137.5 1.3 shard_map.32
  138.9 3.6 %collective-permute-start.19 = (bf16[4,2,16,16,128]{4,3,2,1,0:T(8,128)(2,1)S(1)}, bf16[4,2,16,16,128]{4,3,2,1,0:T(8,128)(2,1)S(1)}, u32[]{:S(2)}, u32[]{:S(2)}) collective-permute-start(bf16[4,2,16,16,128]{4,3,2,1,0:T(8,128)(2,1)S(1)} %get-tuple-element.43), channel_id=1, source_target_pairs={{0,16},{4,20},{8,8},{12,12},{16,0},{20,4},{24,24},{28,28},{1,17},{... | collective-permute-start | bytes 1572872 | tf_op jit(solution)/shard_map/ppermute | solution.py:20
  142.4 2.3 %collective-permute-start.10 = (bf16[2,16,16,128]{3,2,1,0:T(8,128)(2,1)}, bf16[2,16,16,128]{3,2,1,0:T(8,128)(2,1)S(1)}, u32[]{:S(2)}, u32[]{:S(2)}) collective-permute-start(bf16[2,16,16,128]{3,2,1,0:T(8,128)(2,1)} %copy-done.7), channel_id=1, source_target_pairs={{0,16},{1,17},{2,18},{3,19},{4,20},{5,21},{6,22},{7,23},{8,8},{9,9... | collective-permute-start | bytes 393224 | tf_op jit(solution)/shard_map/ppermute | solution.py:25
  144.7 2.7 %collective-permute-start.11 = (bf16[2,16,16,128]{3,2,1,0:T(8,128)(2,1)}, bf16[2,16,16,128]{3,2,1,0:T(8,128)(2,1)S(1)}, u32[]{:S(2)}, u32[]{:S(2)}) collective-permute-start(bf16[2,16,16,128]{3,2,1,0:T(8,128)(2,1)} %copy-done.6), channel_id=1, source_target_pairs={{0,17},{1,18},{2,19},{3,16},{4,21},{5,22},{6,23},{7,20},{8,9},{9,1... | collective-permute-start | bytes 393224 | tf_op jit(solution)/shard_map/ppermute | solution.py:25
  147.5 2.5 %collective-permute-start.12 = (bf16[2,16,16,128]{3,2,1,0:T(8,128)(2,1)}, bf16[2,16,16,128]{3,2,1,0:T(8,128)(2,1)S(1)}, u32[]{:S(2)}, u32[]{:S(2)}) collective-permute-start(bf16[2,16,16,128]{3,2,1,0:T(8,128)(2,1)} %copy-done.5), channel_id=1, source_target_pairs={{0,18},{1,19},{2,16},{3,17},{4,22},{5,23},{6,20},{7,21},{8,10},{9,... | collective-permute-start | bytes 393224 | tf_op jit(solution)/shard_map/ppermute | solution.py:25
  150.0 10.7 %collective-permute-done.10.refs_0_ = bf16[2,16,16,128]{3,2,1,0:T(8,128)(2,1)S(1)} collective-permute-done((bf16[2,16,16,128]{3,2,1,0:T(8,128)(2,1)}, bf16[2,16,16,128]{3,2,1,0:T(8,128)(2,1)S(1)}, u32[]{:S(2)}, u32[]{:S(2)}) %collective-permute-start.10) | collective-permute-done | bytes 131104 | tf_op jit(solution)/shard_map/ppermute | solution.py:25
  160.7 4.7 %collective-permute-start.13 = (bf16[2,16,16,128]{3,2,1,0:T(8,128)(2,1)}, bf16[2,16,16,128]{3,2,1,0:T(8,128)(2,1)S(1)}, u32[]{:S(2)}, u32[]{:S(2)}) collective-permute-start(bf16[2,16,16,128]{3,2,1,0:T(8,128)(2,1)} %copy-done.4), channel_id=1, source_target_pairs={{0,19},{1,16},{2,17},{3,18},{4,23},{5,20},{6,21},{7,22},{8,11},{9,... | collective-permute-start | bytes 393224 | tf_op jit(solution)/shard_map/ppermute | solution.py:25
  165.5 4.0 %collective-permute-done.13.refs_3_ = bf16[2,16,16,128]{3,2,1,0:T(8,128)(2,1)S(1)} collective-permute-done((bf16[2,16,16,128]{3,2,1,0:T(8,128)(2,1)}, bf16[2,16,16,128]{3,2,1,0:T(8,128)(2,1)S(1)}, u32[]{:S(2)}, u32[]{:S(2)}) %collective-permute-start.13) | collective-permute-done | bytes 131104 | tf_op jit(solution)/shard_map/ppermute | solution.py:25
  169.5 5.1 %collective-permute-done.20.refs_6_ = bf16[2,16,16,128]{3,2,1,0:T(8,128)(2,1)S(1)} collective-permute-done((bf16[2,16,16,128]{3,2,1,0:T(8,128)(2,1)S(1)}, bf16[2,16,16,128]{3,2,1,0:T(8,128)(2,1)S(1)}, u32[]{:S(2)}, u32[]{:S(2)}) %collective-permute-start.20) | collective-permute-done | bytes 131104 | tf_op jit(solution)/shard_map/ppermute | solution.py:25
  174.6 6.4 %shard_map.34.refs_12_ = f32[2,1,1024,1024]{3,2,1,0:T(8,128)} custom-call(bf16[4,2,16,16,128]{4,3,2,1,0:T(8,128)(2,1)S(1)} %collective-permute-done.8.refs_0_, bf16[4,2,16,16,128]{4,3,2,1,0:T(8,128)(2,1)S(1)} %collective-permute-done.9.refs_1_, bf16[4,2,16,16,128]{4,3,2,1,0:T(8,128)(2,1)} %collective-permute-done.28.refs_2_, ...), custom_call_target="tpu_custom_call" | custom-call | flops 2147483648 | bytes 7340032 | tf_op jit(solution)/shard_map/pallas_call | solution.py:218
  181.0 7.3 %shard_map.35 = bf16[2,1,1024,1024]{3,2,1,0:T(8,128)(2,1)} custom-call(bf16[2,16,16,128]{3,2,1,0:T(8,128)(2,1)S(1)} %collective-permute-done.10.refs_0_, bf16[2,16,16,128]{3,2,1,0:T(8,128)(2,1)S(1)} %collective-permute-done.11.refs_1_, bf16[2,16,16,128]{3,2,1,0:T(8,128)(2,1)S(1)} %collective-permute-done.12.refs_2_, ...), custom_call_target="tpu_custom_call" | custom-call | flops 2147483648 | bytes 7340032 | tf_op jit(solution)/shard_map/pallas_call | solution.py:218
  (53 shorter events, 0.8 us)
Async XLA Ops:
  2.9 25.0 %collective-permute-start.4 = (bf16[16,240,128]{2,1,0:T(8,128)(2,1)}, bf16[16,240,128]{2,1,0:T(8,128)(2,1)}, u32[]{:S(2)}, u32[]{:S(2)}) collective-permute-start(bf16[16,240,128]{2,1,0:T(8,128)(2,1)} %get-tuple-element.31), channel_id=1, source_target_pairs={{0,8},{4,12},{8,0},{12,4},{16,24},{20,28},{24,16},{28,20},{1,9},{5... | collective-permute-start | bytes 2949128 | tf_op jit(solution)/shard_map/ppermute | solution.py:20
  5.9 23.5 %collective-permute-start.5 = (bf16[16,240,128]{2,1,0:T(8,128)(2,1)}, bf16[16,240,128]{2,1,0:T(8,128)(2,1)}, u32[]{:S(2)}, u32[]{:S(2)}) collective-permute-start(bf16[16,240,128]{2,1,0:T(8,128)(2,1)} %get-tuple-element.32.own), channel_id=1, source_target_pairs={{0,16},{4,20},{8,24},{12,28},{16,0},{20,4},{24,8},{28,12},{1,17},{... | collective-permute-start | bytes 2949128 | tf_op jit(solution)/shard_map/ppermute | solution.py:20
  10.4 3.0 %copy-start.8 = (f32[512]{0:T(512)S(1)}, f32[512]{0:T(512)}, u32[]{:S(2)}) copy-start(f32[512]{0:T(512)} %param.3) | copy-start | bytes 6148
  27.9 5.6 %collective-permute-start.6 = (bf16[16,240,128]{2,1,0:T(8,128)(2,1)}, bf16[16,240,128]{2,1,0:T(8,128)(2,1)S(1)}, u32[]{:S(2)}, u32[]{:S(2)}) collective-permute-start(bf16[16,240,128]{2,1,0:T(8,128)(2,1)} %collective-permute-done.4.x_mine), channel_id=1, source_target_pairs={{0,4},{4,0},{8,12},{12,8},{16,20},{20,16},{24,28},{28,24},{1,5},{5... | collective-permute-start | bytes 2949128 | tf_op jit(solution)/shard_map/ppermute | solution.py:20
  31.2 2.6 %collective-permute-start.7 = (bf16[16,240,128]{2,1,0:T(8,128)(2,1)S(1)}, bf16[16,240,128]{2,1,0:T(8,128)(2,1)S(1)}, u32[]{:S(2)}, u32[]{:S(2)}) collective-permute-start(bf16[16,240,128]{2,1,0:T(8,128)(2,1)S(1)} %shard_map.28), channel_id=1, source_target_pairs={{0,4},{4,0},{8,12},{12,8},{16,20},{20,16},{24,28},{28,24},{1,5},{5... | collective-permute-start | bytes 2949128 | tf_op jit(solution)/shard_map/ppermute | solution.py:20
  31.2 24.5 %collective-permute-start.24 = (bf16[16,240,128]{2,1,0:T(8,128)(2,1)}, bf16[16,240,128]{2,1,0:T(8,128)(2,1)}, u32[]{:S(2)}, u32[]{:S(2)}) collective-permute-start(bf16[16,240,128]{2,1,0:T(8,128)(2,1)} %get-tuple-element.33.refs_0_), channel_id=1, source_target_pairs={{0,8},{4,12},{8,0},{12,4},{16,24},{20,28},{24,16},{28,20},{1,9},{5... | collective-permute-start | bytes 2949128 | tf_op jit(solution)/shard_map/ppermute | solution.py:20
  32.0 23.8 %collective-permute-start.25 = (bf16[16,240,128]{2,1,0:T(8,128)(2,1)}, bf16[16,240,128]{2,1,0:T(8,128)(2,1)}, u32[]{:S(2)}, u32[]{:S(2)}) collective-permute-start(bf16[16,240,128]{2,1,0:T(8,128)(2,1)} %get-tuple-element.34.refs_1_), channel_id=1, source_target_pairs={{0,16},{4,20},{8,24},{12,28},{16,0},{20,4},{24,8},{28,12},{1,17},{... | collective-permute-start | bytes 2949128 | tf_op jit(solution)/shard_map/ppermute | solution.py:20
  38.7 1.0 copy-start.2
  39.6 31.0 %all-to-all-start = ((bf16[4,2,2,16,16,128]{5,4,3,2,1,0:T(8,128)(2,1)}), bf16[4,2,2,16,16,128]{5,4,3,2,1,0:T(8,128)(2,1)}, u32[]{:S(2)}, u32[]{:S(2)}) async-start(bf16[4,2,2,16,16,128]{5,4,3,2,1,0:T(8,128)(2,1)} %copy-done.2), calls=%async_computation | async-start | bytes 2097152 | tf_op jit(solution)/shard_map/all_to_all | solution.py:308
  55.7 4.7 %collective-permute-start.26 = (bf16[16,240,128]{2,1,0:T(8,128)(2,1)}, bf16[16,240,128]{2,1,0:T(8,128)(2,1)S(1)}, u32[]{:S(2)}, u32[]{:S(2)}) collective-permute-start(bf16[16,240,128]{2,1,0:T(8,128)(2,1)} %collective-permute-done.24.x_mine), channel_id=1, source_target_pairs={{0,4},{4,0},{8,12},{12,8},{16,20},{20,16},{24,28},{28,24},{1,5},{5... | collective-permute-start | bytes 2949128 | tf_op jit(solution)/shard_map/ppermute | solution.py:20
  57.1 3.3 %collective-permute-start.27 = (bf16[16,240,128]{2,1,0:T(8,128)(2,1)S(1)}, bf16[16,240,128]{2,1,0:T(8,128)(2,1)S(1)}, u32[]{:S(2)}, u32[]{:S(2)}) collective-permute-start(bf16[16,240,128]{2,1,0:T(8,128)(2,1)S(1)} %broadcast_select_fusion), channel_id=1, source_target_pairs={{0,4},{4,0},{8,12},{12,8},{16,20},{20,16},{24,28},{28,24},{1,5},{5... | collective-permute-start | bytes 2949128 | tf_op jit(solution)/shard_map/ppermute | solution.py:20
  57.6 24.1 %collective-permute-start.14 = (bf16[16,240,128]{2,1,0:T(8,128)(2,1)}, bf16[16,240,128]{2,1,0:T(8,128)(2,1)}, u32[]{:S(2)}, u32[]{:S(2)}) collective-permute-start(bf16[16,240,128]{2,1,0:T(8,128)(2,1)} %get-tuple-element.35.refs_2_), channel_id=1, source_target_pairs={{0,8},{4,12},{8,0},{12,4},{16,24},{20,28},{24,16},{28,20},{1,9},{5... | collective-permute-start | bytes 2949128 | tf_op jit(solution)/shard_map/ppermute | solution.py:20
  58.9 24.1 %collective-permute-start.15 = (bf16[16,240,128]{2,1,0:T(8,128)(2,1)}, bf16[16,240,128]{2,1,0:T(8,128)(2,1)}, u32[]{:S(2)}, u32[]{:S(2)}) collective-permute-start(bf16[16,240,128]{2,1,0:T(8,128)(2,1)} %get-tuple-element.36.refs_3_), channel_id=1, source_target_pairs={{0,16},{4,20},{8,24},{12,28},{16,0},{20,4},{24,8},{28,12},{1,17},{... | collective-permute-start | bytes 2949128 | tf_op jit(solution)/shard_map/ppermute | solution.py:20
  65.3 1.0 copy-start.1
  70.6 29.6 %all-to-all-start.2 = ((bf16[4,2,2,16,16,128]{5,4,3,2,1,0:T(8,128)(2,1)}), bf16[4,2,2,16,16,128]{5,4,3,2,1,0:T(8,128)(2,1)}, u32[]{:S(2)}, u32[]{:S(2)}) async-start(bf16[4,2,2,16,16,128]{5,4,3,2,1,0:T(8,128)(2,1)} %copy-done.1), calls=%async_computation.2 | async-start | bytes 2097152 | tf_op jit(solution)/shard_map/all_to_all | solution.py:308
  81.7 5.1 %collective-permute-start.16 = (bf16[16,240,128]{2,1,0:T(8,128)(2,1)}, bf16[16,240,128]{2,1,0:T(8,128)(2,1)S(1)}, u32[]{:S(2)}, u32[]{:S(2)}) collective-permute-start(bf16[16,240,128]{2,1,0:T(8,128)(2,1)} %collective-permute-done.14.x_mine), channel_id=1, source_target_pairs={{0,4},{4,0},{8,12},{12,8},{16,20},{20,16},{24,28},{28,24},{1,5},{5... | collective-permute-start | bytes 2949128 | tf_op jit(solution)/shard_map/ppermute | solution.py:20
  84.4 2.6 %collective-permute-start.17 = (bf16[16,240,128]{2,1,0:T(8,128)(2,1)S(1)}, bf16[16,240,128]{2,1,0:T(8,128)(2,1)S(1)}, u32[]{:S(2)}, u32[]{:S(2)}) collective-permute-start(bf16[16,240,128]{2,1,0:T(8,128)(2,1)S(1)} %broadcast_select_fusion.1), channel_id=1, source_target_pairs={{0,4},{4,0},{8,12},{12,8},{16,20},{20,16},{24,28},{28,24},{1,5},{5... | collective-permute-start | bytes 2949128 | tf_op jit(solution)/shard_map/ppermute | solution.py:20
  84.5 24.5 %collective-permute-start = (bf16[16,240,128]{2,1,0:T(8,128)(2,1)}, bf16[16,240,128]{2,1,0:T(8,128)(2,1)}, u32[]{:S(2)}, u32[]{:S(2)}) collective-permute-start(bf16[16,240,128]{2,1,0:T(8,128)(2,1)} %get-tuple-element.29.refs_4_), channel_id=1, source_target_pairs={{0,8},{4,12},{8,0},{12,4},{16,24},{20,28},{24,16},{28,20},{1,9},{5... | collective-permute-start | bytes 2949128 | tf_op jit(solution)/shard_map/ppermute | solution.py:20
  85.2 23.7 %collective-permute-start.1 = (bf16[16,240,128]{2,1,0:T(8,128)(2,1)S(1)}, bf16[16,240,128]{2,1,0:T(8,128)(2,1)}, u32[]{:S(2)}, u32[]{:S(2)}) collective-permute-start(bf16[16,240,128]{2,1,0:T(8,128)(2,1)S(1)} %get-tuple-element.30.refs_5_), channel_id=1, source_target_pairs={{0,16},{4,20},{8,24},{12,28},{16,0},{20,4},{24,8},{28,12},{1,17},{... | collective-permute-start | bytes 2949128 | tf_op jit(solution)/shard_map/ppermute | solution.py:20
  91.9 1.0 copy-start
  100.2 37.2 %all-to-all-start.1 = ((bf16[4,2,2,16,16,128]{5,4,3,2,1,0:T(8,128)(2,1)}), bf16[4,2,2,16,16,128]{5,4,3,2,1,0:T(8,128)(2,1)}, u32[]{:S(2)}, u32[]{:S(2)}) async-start(bf16[4,2,2,16,16,128]{5,4,3,2,1,0:T(8,128)(2,1)} %copy-done), calls=%async_computation.1 | async-start | bytes 2097152 | tf_op jit(solution)/shard_map/all_to_all | solution.py:308
  108.9 9.7 %collective-permute-start.2 = (bf16[16,240,128]{2,1,0:T(8,128)(2,1)}, bf16[16,240,128]{2,1,0:T(8,128)(2,1)S(1)}, u32[]{:S(2)}, u32[]{:S(2)}) collective-permute-start(bf16[16,240,128]{2,1,0:T(8,128)(2,1)} %collective-permute-done.x_mine), channel_id=1, source_target_pairs={{0,4},{4,0},{8,12},{12,8},{16,20},{20,16},{24,28},{28,24},{1,5},{5... | collective-permute-start | bytes 2949128 | tf_op jit(solution)/shard_map/ppermute | solution.py:20
  110.3 10.7 %collective-permute-start.3 = (bf16[16,240,128]{2,1,0:T(8,128)(2,1)S(1)}, bf16[16,240,128]{2,1,0:T(8,128)(2,1)S(1)}, u32[]{:S(2)}, u32[]{:S(2)}) collective-permute-start(bf16[16,240,128]{2,1,0:T(8,128)(2,1)S(1)} %broadcast_select_fusion.2), channel_id=1, source_target_pairs={{0,4},{4,0},{8,12},{12,8},{16,20},{20,16},{24,28},{28,24},{1,5},{5... | collective-permute-start | bytes 2949128 | tf_op jit(solution)/shard_map/ppermute | solution.py:20
  111.8 14.8 %collective-permute-start.8 = (bf16[4,2,16,16,128]{4,3,2,1,0:T(8,128)(2,1)S(1)}, bf16[4,2,16,16,128]{4,3,2,1,0:T(8,128)(2,1)S(1)}, u32[]{:S(2)}, u32[]{:S(2)}) collective-permute-start(bf16[4,2,16,16,128]{4,3,2,1,0:T(8,128)(2,1)S(1)} %get-tuple-element.60), channel_id=1, source_target_pairs={{0,8},{4,12},{8,0},{12,4},{16,24},{20,28},{24,16},{28,20},{1,9},{5... | collective-permute-start | bytes 1572872 | tf_op jit(solution)/shard_map/ppermute | solution.py:20
  112.7 16.7 %collective-permute-start.9 = (bf16[4,2,16,16,128]{4,3,2,1,0:T(8,128)(2,1)S(1)}, bf16[4,2,16,16,128]{4,3,2,1,0:T(8,128)(2,1)S(1)}, u32[]{:S(2)}, u32[]{:S(2)}) collective-permute-start(bf16[4,2,16,16,128]{4,3,2,1,0:T(8,128)(2,1)S(1)} %get-tuple-element.59), channel_id=1, source_target_pairs={{0,16},{4,20},{8,8},{12,12},{16,0},{20,4},{24,24},{28,28},{1,17},{... | collective-permute-start | bytes 1572872 | tf_op jit(solution)/shard_map/ppermute | solution.py:20
  118.6 26.1 %collective-permute-start.28 = (bf16[4,2,16,16,128]{4,3,2,1,0:T(8,128)(2,1)}, bf16[4,2,16,16,128]{4,3,2,1,0:T(8,128)(2,1)}, u32[]{:S(2)}, u32[]{:S(2)}) collective-permute-start(bf16[4,2,16,16,128]{4,3,2,1,0:T(8,128)(2,1)} %get-tuple-element.58), channel_id=1, source_target_pairs={{0,8},{4,12},{8,0},{12,4},{16,24},{20,28},{24,16},{28,20},{1,9},{5... | collective-permute-start | bytes 1572872 | tf_op jit(solution)/shard_map/ppermute | solution.py:20
  118.6 28.8 %collective-permute-start.29 = (bf16[4,2,16,16,128]{4,3,2,1,0:T(8,128)(2,1)}, bf16[4,2,16,16,128]{4,3,2,1,0:T(8,128)(2,1)}, u32[]{:S(2)}, u32[]{:S(2)}) collective-permute-start(bf16[4,2,16,16,128]{4,3,2,1,0:T(8,128)(2,1)} %get-tuple-element.57), channel_id=1, source_target_pairs={{0,16},{4,20},{8,8},{12,12},{16,0},{20,4},{24,24},{28,28},{1,17},{... | collective-permute-start | bytes 1572872 | tf_op jit(solution)/shard_map/ppermute | solution.py:20
  134.2 0.6 copy-start.3
  134.9 0.6 copy-start.4
  135.5 0.7 copy-start.5
  136.2 0.7 copy-start.6
  136.8 0.6 copy-start.7
  138.8 42.2 %collective-permute-start.18 = (bf16[4,2,16,16,128]{4,3,2,1,0:T(8,128)(2,1)S(1)}, bf16[4,2,16,16,128]{4,3,2,1,0:T(8,128)(2,1)S(1)}, u32[]{:S(2)}, u32[]{:S(2)}) collective-permute-start(bf16[4,2,16,16,128]{4,3,2,1,0:T(8,128)(2,1)S(1)} %get-tuple-element.42), channel_id=1, source_target_pairs={{0,8},{4,12},{8,0},{12,4},{16,24},{20,28},{24,16},{28,20},{1,9},{5... | collective-permute-start | bytes 1572872 | tf_op jit(solution)/shard_map/ppermute | solution.py:20
  138.9 42.1 %collective-permute-start.19 = (bf16[4,2,16,16,128]{4,3,2,1,0:T(8,128)(2,1)S(1)}, bf16[4,2,16,16,128]{4,3,2,1,0:T(8,128)(2,1)S(1)}, u32[]{:S(2)}, u32[]{:S(2)}) collective-permute-start(bf16[4,2,16,16,128]{4,3,2,1,0:T(8,128)(2,1)S(1)} %get-tuple-element.43), channel_id=1, source_target_pairs={{0,16},{4,20},{8,8},{12,12},{16,0},{20,4},{24,24},{28,28},{1,17},{... | collective-permute-start | bytes 1572872 | tf_op jit(solution)/shard_map/ppermute | solution.py:20
  142.4 18.3 %collective-permute-start.10 = (bf16[2,16,16,128]{3,2,1,0:T(8,128)(2,1)}, bf16[2,16,16,128]{3,2,1,0:T(8,128)(2,1)S(1)}, u32[]{:S(2)}, u32[]{:S(2)}) collective-permute-start(bf16[2,16,16,128]{3,2,1,0:T(8,128)(2,1)} %copy-done.7), channel_id=1, source_target_pairs={{0,16},{1,17},{2,18},{3,19},{4,20},{5,21},{6,22},{7,23},{8,8},{9,9... | collective-permute-start | bytes 393224 | tf_op jit(solution)/shard_map/ppermute | solution.py:25
  144.7 20.7 %collective-permute-start.11 = (bf16[2,16,16,128]{3,2,1,0:T(8,128)(2,1)}, bf16[2,16,16,128]{3,2,1,0:T(8,128)(2,1)S(1)}, u32[]{:S(2)}, u32[]{:S(2)}) collective-permute-start(bf16[2,16,16,128]{3,2,1,0:T(8,128)(2,1)} %copy-done.6), channel_id=1, source_target_pairs={{0,17},{1,18},{2,19},{3,16},{4,21},{5,22},{6,23},{7,20},{8,9},{9,1... | collective-permute-start | bytes 393224 | tf_op jit(solution)/shard_map/ppermute | solution.py:25
  147.5 18.0 %collective-permute-start.12 = (bf16[2,16,16,128]{3,2,1,0:T(8,128)(2,1)}, bf16[2,16,16,128]{3,2,1,0:T(8,128)(2,1)S(1)}, u32[]{:S(2)}, u32[]{:S(2)}) collective-permute-start(bf16[2,16,16,128]{3,2,1,0:T(8,128)(2,1)} %copy-done.5), channel_id=1, source_target_pairs={{0,18},{1,19},{2,16},{3,17},{4,22},{5,23},{6,20},{7,21},{8,10},{9,... | collective-permute-start | bytes 393224 | tf_op jit(solution)/shard_map/ppermute | solution.py:25
  160.7 8.8 %collective-permute-start.13 = (bf16[2,16,16,128]{3,2,1,0:T(8,128)(2,1)}, bf16[2,16,16,128]{3,2,1,0:T(8,128)(2,1)S(1)}, u32[]{:S(2)}, u32[]{:S(2)}) collective-permute-start(bf16[2,16,16,128]{3,2,1,0:T(8,128)(2,1)} %copy-done.4), channel_id=1, source_target_pairs={{0,19},{1,16},{2,17},{3,18},{4,23},{5,20},{6,21},{7,22},{8,11},{9,... | collective-permute-start | bytes 393224 | tf_op jit(solution)/shard_map/ppermute | solution.py:25
  165.4 9.1 %collective-permute-start.20 = (bf16[2,16,16,128]{3,2,1,0:T(8,128)(2,1)S(1)}, bf16[2,16,16,128]{3,2,1,0:T(8,128)(2,1)S(1)}, u32[]{:S(2)}, u32[]{:S(2)}) collective-permute-start(bf16[2,16,16,128]{3,2,1,0:T(8,128)(2,1)S(1)} %get-tuple-element.41.refs_0_), channel_id=1, source_target_pairs={{0,8},{1,9},{2,10},{3,11},{4,12},{5,13},{6,14},{7,15},{8,0},{9,1},... | collective-permute-start | bytes 393224 | tf_op jit(solution)/shard_map/ppermute | solution.py:25
  165.4 15.6 %collective-permute-start.21 = (bf16[2,16,16,128]{3,2,1,0:T(8,128)(2,1)}, bf16[2,16,16,128]{3,2,1,0:T(8,128)(2,1)S(1)}, u32[]{:S(2)}, u32[]{:S(2)}) collective-permute-start(bf16[2,16,16,128]{3,2,1,0:T(8,128)(2,1)} %copy-done.3), channel_id=1, source_target_pairs={{0,9},{1,10},{2,11},{3,8},{4,13},{5,14},{6,15},{7,12},{8,1},{9,2},... | collective-permute-start | bytes 393224 | tf_op jit(solution)/shard_map/ppermute | solution.py:25
  169.5 11.5 %collective-permute-start.22 = (bf16[2,16,16,128]{3,2,1,0:T(8,128)(2,1)S(1)}, bf16[2,16,16,128]{3,2,1,0:T(8,128)(2,1)S(1)}, u32[]{:S(2)}, u32[]{:S(2)}) collective-permute-start(bf16[2,16,16,128]{3,2,1,0:T(8,128)(2,1)S(1)} %get-tuple-element.45), channel_id=1, source_target_pairs={{0,10},{1,11},{2,8},{3,9},{4,14},{5,15},{6,12},{7,13},{8,2},{9,3},... | collective-permute-start | bytes 393224 | tf_op jit(solution)/shard_map/ppermute | solution.py:25
  174.6 6.4 %collective-permute-start.23 = (bf16[2,16,16,128]{3,2,1,0:T(8,128)(2,1)S(1)}, bf16[2,16,16,128]{3,2,1,0:T(8,128)(2,1)S(1)}, u32[]{:S(2)}, u32[]{:S(2)}) collective-permute-start(bf16[2,16,16,128]{3,2,1,0:T(8,128)(2,1)S(1)} %get-tuple-element.46), channel_id=1, source_target_pairs={{0,11},{1,8},{2,9},{3,10},{4,15},{5,12},{6,13},{7,14},{8,3},{9,0},... | collective-permute-start | bytes 393224 | tf_op jit(solution)/shard_map/ppermute | solution.py:25

commit v3 on v2

--- a/solution.py
+++ b/solution.py
@@ -126,7 +126,7 @@
                 pl.BlockSpec(block, lambda step, scalars: (scalars[2] * (freqs // step_freqs) + step, 0, 0))
             ]
             + [plain] * 4
-            + in_hbm(len(earlier)),
+            + anywhere(len(earlier)),
             out_specs=[pl.BlockSpec(out_shape, lambda step, scalars: (0,) * len(out_shape))] * count,
             scratch_shapes=[pltpu.VMEM((2 * ROUNDS * half * freqs, width), jnp.float32)],
         ),
@@ -139,8 +139,8 @@
     )(scalars, spectra, x_mine, y_mine, x_other, last_other, *earlier)
 
 
-def in_hbm(count):
-    return [pl.BlockSpec(memory_space=pltpu.HBM)] * count
+def anywhere(count):
+    return [pl.BlockSpec(memory_space=pl.ANY)] * count
 
 
 def last_body(scalars, own, y_mine, *refs):
@@ -153,7 +153,7 @@
         out_shape=jax.ShapeDtypeStruct(y_mine.shape, jnp.bfloat16),
         in_specs=[pl.BlockSpec(memory_space=pltpu.SMEM)]
         + [pl.BlockSpec(memory_space=pltpu.VMEM)] * 2
-        + in_hbm(len(waits)),
+        + anywhere(len(waits)),
         out_specs=pl.BlockSpec(memory_space=pltpu.VMEM),
         compiler_params=pltpu.CompilerParams(vmem_limit_bytes=LITTLE),
         cost_estimate=pl.CostEstimate(flops=0, bytes_accessed=6 * y_mine.size, transcendentals=0),
@@ -170,7 +170,7 @@
     return pl.pallas_call(
         bundles_body,
         out_shape=[shape] * 2,
-        in_specs=[pl.BlockSpec(memory_space=pltpu.VMEM)] + in_hbm(len(waits)),
+        in_specs=[pl.BlockSpec(memory_space=pltpu.VMEM)] + anywhere(len(waits)),
         out_specs=[pl.BlockSpec(memory_space=pltpu.VMEM)] * 2,
         compiler_params=pltpu.CompilerParams(vmem_limit_bytes=LITTLE),
         cost_estimate=pl.CostEstimate(flops=0, bytes_accessed=4 * spread.size, transcendentals=0),
@@ -180,7 +180,7 @@
 def lag_body(order, *refs):
     count = len(order)
     blocks = [refs[order.index(at)] for at in range(count)]
-    cosines, sines, *partial, out = refs[count:]
+    cosines, sines, out = refs[count:]
     stations, _, width = blocks[0].shape[-3:]
     half = width // 2
     real, imag = [], []
@@ -196,16 +196,13 @@
         imag.append(turned[half:])
     lagged = jnp.dot(jnp.concatenate(real, 0), cosines[...], preferred_element_type=jnp.float32)
     lagged += jnp.dot(jnp.concatenate(imag, 0), sines[...], preferred_element_type=jnp.float32)
-    if partial:
-        lagged += partial[0][0, 0]
     out[0, 0] = lagged.astype(out.dtype)
 
 
-def to_lags(blocks, order, cosines, sines, part, partial, kind):
+def to_lags(blocks, order, cosines, sines):
     rounds, stations, freqs, width = blocks[0].shape[-4:]
     half = width // 2
-    rows = sum(block.size for block in blocks) // (rounds * stations * width)
-    lags = cosines.shape[1]
+    bins, lags = cosines.shape
     step = math.gcd(stations, 8)
 
     def spec(block):
@@ -213,21 +210,20 @@
             return pl.BlockSpec((1, step, freqs, width), lambda turn, at: (turn, at, 0, 0))
         return pl.BlockSpec((block.shape[0], 1, step, freqs, width), lambda turn, at: (0, turn, at, 0, 0))
 
-    table = pl.BlockSpec((rows, lags), lambda turn, at: (part, 0))
-    lagged = pl.BlockSpec((1, 1, step * half, lags), lambda turn, at: (turn, 0, at, 0))
+    table = pl.BlockSpec((bins, lags), lambda turn, at: (0, 0))
     return pl.pallas_call(
         functools.partial(lag_body, order),
-        out_shape=jax.ShapeDtypeStruct((rounds, 1, stations * half, lags), kind),
+        out_shape=jax.ShapeDtypeStruct((rounds, 1, stations * half, lags), jnp.bfloat16),
         grid=(rounds, stations // step),
-        in_specs=[spec(blocks[at]) for at in order] + [table] * 2 + [lagged] * len(partial),
-        out_specs=lagged,
+        in_specs=[spec(blocks[at]) for at in order] + [table] * 2,
+        out_specs=pl.BlockSpec((1, 1, step * half, lags), lambda turn, at: (turn, 0, at, 0)),
         compiler_params=pltpu.CompilerParams(vmem_limit_bytes=VMEM),
         cost_estimate=pl.CostEstimate(
-            flops=2 * rounds * stations * half * 2 * rows * lags,
-            bytes_accessed=2 * (rounds * stations * half * (2 * rows + lags) + 2 * rows * lags),
+            flops=2 * rounds * stations * half * 2 * bins * lags,
+            bytes_accessed=2 * (rounds * stations * half * (2 * bins + lags) + 2 * bins * lags),
             transcendentals=0,
         ),
-    )(*[blocks[at] for at in order], cosines, sines, *partial)
+    )(*[blocks[at] for at in order], cosines, sines)
 
 
 def inverse_table(band_weight, shard, odd, chunks, straight):
@@ -309,15 +305,15 @@
             spreads.append(spread)
             if chunk + 1 < chunks - straight:
                 blocks[chunk] = [permuted(spread[:, 0], to_x), permuted(spread[:, 1], to_b)]
-    partial, part = [], 0
-    if chunks == 4:
-        early = blocks[0] + blocks[1]
-        partial = [to_lags(early, range(len(early)), cosines, sines, 0, [], jnp.float32)]
-        blocks, part = blocks[2:], 1
-    beside = [at + len(sum(blocks[:-1], [])) for at in range(shards, 2 * shards)]
-    over = [at - shards for at in beside]
-    order = beside + list(range(over[0])) + over
-    return to_lags(sum(blocks, []), order, cosines, sines, part, partial, jnp.bfloat16)
+    blocks = sum(blocks, [])
+
+    before = len(blocks) - 2 * shards * straight
+    far_first = sorted(range(shards), key=lambda distance: -min(distance, shards - distance))
+    order = list(range(before))
+    for first in range(before, len(blocks), 2 * shards):
+        order += [first + bundle * shards + distance for bundle in range(2) for distance in far_first[:-1]]
+        order += [first + bundle * shards + far_first[-1] for bundle in range(2)]
+    return to_lags(blocks, order, cosines, sines)
 
 
 def solution(mesh):

time: 190 us -> 180 us (0.947)
  Pallas kernels: 36.2 us -> 30.5 us
  starting transfers between devices: 48.7 us -> 51.5 us
  other arithmetic: 13.4 us -> 11.1 us
  waiting for transfers between devices: 68 us -> 65.8 us
    pallas_call x2 -> x1, Pallas kernels: 13.7 us -> 7.73 us  [to_lags(): pl.pallas_call(functools.partial(lag_body, order), out_shape=jax.ShapeDty...]
    ppermute x8, starting transfers between devices: 12.3 us -> 14.9 us  [permuted_far(): lax.ppermute(value, ('grp', 'frq'), [(group * shards + shard, target(grou...]
    select_n x3, other arithmetic: 3.92 us -> 1.54 us  [local(): last = jnp.where(odd == core, y_mine, own)]
    ppermute x22, waiting for transfers between devices: 36.4 us -> 34.3 us  [permuted(): lax.ppermute(value, 'grp', [(source, target(source) % count) for source i...]
    unnamed x18 -> x24, local copies, waits for them, and re-layouts: 6.13 us -> 4.95 us
  transfers between devices with their start and end apart: 33 -> 33, of which waited for: 16 -> 16; matrix products, arithmetic and copies ran while one was open for 14% -> 13% of each run, Pallas kernels for 15% -> 13%
where the time goes in v3:
time: 180 us; the launch traced here: 179 us
  waiting for transfers between devices  65.8 us (37%)
  starting transfers between devices  51.5 us (29%)
  Pallas kernels  30.5 us (17%)
  local copies, waits for them, and re-layouts  19.9 us (11%)
  other arithmetic  11.1 us (6%)
    ppermute x22, waiting for transfers between devices, permuted(): lax.ppermute(value, 'grp', [(source, target(source) % count) for source i...  34.3 us
    ppermute x22, starting transfers between devices, permuted(): lax.ppermute(value, 'grp', [(source, target(source) % count) for source i...  24 us
    pallas_call x4, Pallas kernels, cross_spectra(): pl.pallas_call(functools.partial(cross_body, shards, step_freqs, len(earl...  21 us
    ppermute x8, waiting for transfers between devices, permuted_far(): lax.ppermute(value, ('grp', 'frq'), [(group * shards + shard, target(grou...  18.6 us
    ppermute x8, starting transfers between devices, permuted_far(): lax.ppermute(value, ('grp', 'frq'), [(group * shards + shard, target(grou...  14.9 us
    all_to_all x3, waiting for transfers between devices, local(): lax.all_to_all(results[0], 'frq', split_axis=0, concat_axis=0, tiled=True)  12.9 us
    all_to_all x3, starting transfers between devices, local(): lax.all_to_all(results[0], 'frq', split_axis=0, concat_axis=0, tiled=True)  12.6 us
    dynamic_slice x4, local copies, waits for them, and re-layouts, piece(): lax.dynamic_slice_in_dim(source, (half * chunks + chunk) * size, size, 0)  10.8 us
  transfers between devices with their start and end apart: 33, of which 16 were waited for; matrix products, arithmetic and copies ran while one was open for 13% of the time, Pallas kernels for 13%

profile of v3, /device:TPU:0, one launch (start us, length us, event | category | flops | bytes accessed | tf_op | source)
XLA Modules:
  0.0 179.1 jit_solution(4702602441434887143)
XLA Ops:
  0.0 2.9 %dynamic-slice_bitcast_fusion = (bf16[16,240,128]{2,1,0:T(8,128)(2,1)}, bf16[16,240,128]{2,1,0:T(8,128)(2,1)}) fusion(bf16[1,128,240,128]{3,2,1,0:T(8,128)(2,1)} %param.2, s32[]{:T(128)S(6)} %select_n.79, s32[]{:T(128)S(6)} %select_n.78), kind=kLoop, calls=%fused_computation.11 | loop fusion | bytes 3932168 | tf_op jit(solution)/shard_map/dynamic_slice | solution.py:268
  2.9 2.9 %collective-permute-start = (bf16[16,240,128]{2,1,0:T(8,128)(2,1)}, bf16[16,240,128]{2,1,0:T(8,128)(2,1)}, u32[]{:S(2)}, u32[]{:S(2)}) collective-permute-start(bf16[16,240,128]{2,1,0:T(8,128)(2,1)} %get-tuple-element.26), channel_id=1, source_target_pairs={{0,8},{4,12},{8,0},{12,4},{16,24},{20,28},{24,16},{28,20},{1,9},{5... | collective-permute-start | bytes 2949128 | tf_op jit(solution)/shard_map/ppermute | solution.py:20
  5.8 1.5 collective-permute-start.1
  7.4 2.7 %constant_dynamic-slice_fusion.4 = (bf16[16,240,128]{2,1,0:T(8,128)(2,1)S(1)}, bf16[16,240,128]{2,1,0:T(8,128)(2,1)}) fusion(bf16[128,240,128]{2,1,0:T(8,128)(2,1)} %bitcast.31, s32[]{:T(128)S(6)} %select_n.81, s32[]{:T(128)S(6)} %select_n.80), kind=kLoop, calls=%fused_computation.31 | loop fusion | bytes 3932168 | tf_op jit(solution)/shard_map/dynamic_slice | solution.py:268
  10.1 2.6 %constant_dynamic-slice_fusion.2 = (bf16[16,240,128]{2,1,0:T(8,128)(2,1)S(1)}, bf16[16,240,128]{2,1,0:T(8,128)(2,1)}) fusion(bf16[128,240,128]{2,1,0:T(8,128)(2,1)} %bitcast.32, s32[]{:T(128)S(6)} %select_n.83, s32[]{:T(128)S(6)} %select_n.82), kind=kLoop, calls=%fused_computation.29 | loop fusion | bytes 3932168 | tf_op jit(solution)/shard_map/dynamic_slice | solution.py:268
  12.7 0.1 reshape.90
  12.8 2.6 %constant_dynamic-slice_fusion = (bf16[16,240,128]{2,1,0:T(8,128)(2,1)S(1)}, bf16[16,240,128]{2,1,0:T(8,128)(2,1)}) fusion(bf16[128,240,128]{2,1,0:T(8,128)(2,1)} %bitcast.33, s32[]{:T(128)S(6)} %select_n.85, s32[]{:T(128)S(6)} %select_n.84), kind=kLoop, calls=%fused_computation.27 | loop fusion | bytes 3932168 | tf_op jit(solution)/shard_map/dynamic_slice | solution.py:268
  15.4 0.1 mul.137
  15.5 0.1 multiply_add_fusion
  15.6 0.1 reshape.97
  15.9 9.2 %multiply_convert_fusion = (bf16[512,1024]{1,0:T(8,128)(2,1)S(1)}, bf16[512,1024]{1,0:T(8,128)(2,1)S(1)}) fusion(f32[512]{0:T(512)S(1)} %neg.8, s32[512]{0:T(512)S(1)} %reshape.97, f32[512]{0:T(512)S(1)} %mul.137), kind=kLoop, calls=%fused_computation.6 | loop fusion | flops 9437184 | bytes 2103296 | tf_op jit(solution)/shard_map/convert_element_type | solution.py:251
  25.1 2.8 %collective-permute-done.x_mine = bf16[16,240,128]{2,1,0:T(8,128)(2,1)} collective-permute-done((bf16[16,240,128]{2,1,0:T(8,128)(2,1)}, bf16[16,240,128]{2,1,0:T(8,128)(2,1)}, u32[]{:S(2)}, u32[]{:S(2)}) %collective-permute-start) | collective-permute-done | bytes 983072 | tf_op jit(solution)/shard_map/ppermute | solution.py:20
  27.9 1.5 collective-permute-done.1.y_mine
  29.4 1.8 shard_map.28
  31.2 0.8 collective-permute-start.6
  32.0 1.5 collective-permute-start.7
  33.5 0.2 collective-permute-done.3.last_other
  33.8 4.9 %shard_map.29 = bf16[4,2,2,16,16,128]{5,4,3,2,1,0:T(8,128)(2,1)S(1)} custom-call(s32[4]{0:T(128)S(1)} %get-tuple-element.65.scalars, bf16[128,240,128]{2,1,0:T(8,128)(2,1)} %bitcast.34, bf16[16,240,128]{2,1,0:T(8,128)(2,1)} %collective-permute-done.x_mine, bf16[16,240,128]{2,1,0:T(8,128)(2,1)} %collective-permute-done.1.y_mine, ...), custom_call_target="tpu_custom_call" | custom-call | flops 503316480 | bytes 5963776 | tf_op jit(solution)/shard_map/pallas_call | solution.py:119
  38.7 1.0 copy-done
  39.7 4.9 %all-to-all-start = ((bf16[4,2,2,16,16,128]{5,4,3,2,1,0:T(8,128)(2,1)}), bf16[4,2,2,16,16,128]{5,4,3,2,1,0:T(8,128)(2,1)}, u32[]{:S(2)}, u32[]{:S(2)}) async-start(bf16[4,2,2,16,16,128]{5,4,3,2,1,0:T(8,128)(2,1)} %copy-done), calls=%async_computation | async-start | bytes 2097152 | tf_op jit(solution)/shard_map/all_to_all | solution.py:304
  44.5 11.2 %collective-permute-done.6.x_mine = bf16[16,240,128]{2,1,0:T(8,128)(2,1)} collective-permute-done((bf16[16,240,128]{2,1,0:T(8,128)(2,1)}, bf16[16,240,128]{2,1,0:T(8,128)(2,1)}, u32[]{:S(2)}, u32[]{:S(2)}) %collective-permute-start.6) | collective-permute-done | bytes 983072 | tf_op jit(solution)/shard_map/ppermute | solution.py:20
  55.7 1.3 broadcast_select_fusion.2
  57.2 0.9 collective-permute-start.12
  58.0 1.7 collective-permute-start.13
  59.7 5.8 %shard_map.30 = bf16[4,2,2,16,16,128]{5,4,3,2,1,0:T(8,128)(2,1)} custom-call(s32[4]{0:T(128)S(1)} %get-tuple-element.64.scalars, bf16[128,240,128]{2,1,0:T(8,128)(2,1)} %bitcast.35, bf16[16,240,128]{2,1,0:T(8,128)(2,1)} %collective-permute-done.6.x_mine, bf16[16,240,128]{2,1,0:T(8,128)(2,1)} %collective-permute-done.7.y_mine, ...), custom_call_target="tpu_custom_call" | custom-call | flops 503316480 | bytes 5963776 | tf_op jit(solution)/shard_map/pallas_call | solution.py:119
  65.5 5.1 %all-to-all-done = bf16[4,2,2,16,16,128]{5,4,3,2,1,0:T(8,128)(2,1)} async-done(((bf16[4,2,2,16,16,128]{5,4,3,2,1,0:T(8,128)(2,1)}), bf16[4,2,2,16,16,128]{5,4,3,2,1,0:T(8,128)(2,1)}, u32[]{:S(2)}, u32[]{:S(2)}) %all-to-all-start) | async-done | bytes 1048608 | tf_op jit(solution)/shard_map/all_to_all | solution.py:304
  70.7 4.2 %all-to-all-start.1 = ((bf16[4,2,2,16,16,128]{5,4,3,2,1,0:T(8,128)(2,1)}), bf16[4,2,2,16,16,128]{5,4,3,2,1,0:T(8,128)(2,1)}, u32[]{:S(2)}, u32[]{:S(2)}) async-start(bf16[4,2,2,16,16,128]{5,4,3,2,1,0:T(8,128)(2,1)} %shard_map.30), calls=%async_computation.1 | async-start | bytes 2097152 | tf_op jit(solution)/shard_map/all_to_all | solution.py:304
  74.9 6.7 %collective-permute-done.12.x_mine = bf16[16,240,128]{2,1,0:T(8,128)(2,1)} collective-permute-done((bf16[16,240,128]{2,1,0:T(8,128)(2,1)}, bf16[16,240,128]{2,1,0:T(8,128)(2,1)}, u32[]{:S(2)}, u32[]{:S(2)}) %collective-permute-start.12) | collective-permute-done | bytes 983072 | tf_op jit(solution)/shard_map/ppermute | solution.py:20
  81.7 0.1 broadcast_select_fusion.1
  81.8 0.6 collective-permute-start.15
  82.3 0.3 copy-done.6
  82.6 1.4 collective-permute-start.16
  84.0 1.5 collective-permute-start.17
  85.6 1.2 copy-done.7
  86.8 5.6 %shard_map.31 = bf16[4,2,2,16,16,128]{5,4,3,2,1,0:T(8,128)(2,1)} custom-call(s32[4]{0:T(128)S(1)} %get-tuple-element.63.scalars, bf16[128,240,128]{2,1,0:T(8,128)(2,1)} %bitcast.36, bf16[16,240,128]{2,1,0:T(8,128)(2,1)} %collective-permute-done.12.x_mine, bf16[16,240,128]{2,1,0:T(8,128)(2,1)S(1)} %copy-done.7, ...), custom_call_target="tpu_custom_call" | custom-call | flops 503316480 | bytes 5963776 | tf_op jit(solution)/shard_map/pallas_call | solution.py:119
  92.4 7.8 %all-to-all-done.1 = bf16[4,2,2,16,16,128]{5,4,3,2,1,0:T(8,128)(2,1)} async-done(((bf16[4,2,2,16,16,128]{5,4,3,2,1,0:T(8,128)(2,1)}), bf16[4,2,2,16,16,128]{5,4,3,2,1,0:T(8,128)(2,1)}, u32[]{:S(2)}, u32[]{:S(2)}) %all-to-all-start.1) | async-done | bytes 1048608 | tf_op jit(solution)/shard_map/all_to_all | solution.py:304
  100.2 3.5 %all-to-all-start.2 = ((bf16[4,2,2,16,16,128]{5,4,3,2,1,0:T(8,128)(2,1)}), bf16[4,2,2,16,16,128]{5,4,3,2,1,0:T(8,128)(2,1)S(1)}, u32[]{:S(2)}, u32[]{:S(2)}) async-start(bf16[4,2,2,16,16,128]{5,4,3,2,1,0:T(8,128)(2,1)} %shard_map.31), calls=%async_computation.2 | async-start | bytes 2097152 | tf_op jit(solution)/shard_map/all_to_all | solution.py:304
  103.8 3.3 %collective-permute-done.16.x_mine = bf16[16,240,128]{2,1,0:T(8,128)(2,1)} collective-permute-done((bf16[16,240,128]{2,1,0:T(8,128)(2,1)}, bf16[16,240,128]{2,1,0:T(8,128)(2,1)}, u32[]{:S(2)}, u32[]{:S(2)}) %collective-permute-start.16) | collective-permute-done | bytes 983072 | tf_op jit(solution)/shard_map/ppermute | solution.py:20
  107.1 0.1 broadcast_select_fusion
  107.2 0.5 collective-permute-start.19
  107.8 1.4 slice_bitcast_fusion.2
  109.2 1.2 collective-permute-start.4
  110.4 3.4 %collective-permute-start.5 = (bf16[4,2,16,16,128]{4,3,2,1,0:T(8,128)(2,1)S(1)}, bf16[4,2,16,16,128]{4,3,2,1,0:T(8,128)(2,1)S(1)}, u32[]{:S(2)}, u32[]{:S(2)}) collective-permute-start(bf16[4,2,16,16,128]{4,3,2,1,0:T(8,128)(2,1)S(1)} %get-tuple-element.59), channel_id=1, source_target_pairs={{0,16},{4,20},{8,8},{12,12},{16,0},{20,4},{24,24},{28,28},{1,17},{... | collective-permute-start | bytes 1572872 | tf_op jit(solution)/shard_map/ppermute | solution.py:20
  113.8 2.4 %slice_bitcast_fusion = (bf16[4,2,16,16,128]{4,3,2,1,0:T(8,128)(2,1)}, bf16[4,2,16,16,128]{4,3,2,1,0:T(8,128)(2,1)}) fusion(bf16[4,2,2,16,16,128]{5,4,3,2,1,0:T(8,128)(2,1)} %all-to-all-done.1), kind=kLoop, calls=%fused_computation.16 | loop fusion | bytes 2097152 | tf_op jit(solution)/shard_map/squeeze | solution.py:307
  116.3 2.4 %collective-permute-start.11 = (bf16[4,2,16,16,128]{4,3,2,1,0:T(8,128)(2,1)}, bf16[4,2,16,16,128]{4,3,2,1,0:T(8,128)(2,1)}, u32[]{:S(2)}, u32[]{:S(2)}) collective-permute-start(bf16[4,2,16,16,128]{4,3,2,1,0:T(8,128)(2,1)} %get-tuple-element.57), channel_id=1, source_target_pairs={{0,16},{4,20},{8,8},{12,12},{16,0},{20,4},{24,24},{28,28},{1,17},{... | collective-permute-start | bytes 1572872 | tf_op jit(solution)/shard_map/ppermute | solution.py:20
  118.7 5.4 %collective-permute-done.4.refs_0_ = bf16[4,2,16,16,128]{4,3,2,1,0:T(8,128)(2,1)S(1)} collective-permute-done((bf16[4,2,16,16,128]{4,3,2,1,0:T(8,128)(2,1)S(1)}, bf16[4,2,16,16,128]{4,3,2,1,0:T(8,128)(2,1)S(1)}, u32[]{:S(2)}, u32[]{:S(2)}) %collective-permute-start.4) | collective-permute-done | bytes 524320 | tf_op jit(solution)/shard_map/ppermute | solution.py:20
  124.0 3.0 %collective-permute-done.5.refs_1_ = bf16[4,2,16,16,128]{4,3,2,1,0:T(8,128)(2,1)S(1)} collective-permute-done((bf16[4,2,16,16,128]{4,3,2,1,0:T(8,128)(2,1)S(1)}, bf16[4,2,16,16,128]{4,3,2,1,0:T(8,128)(2,1)S(1)}, u32[]{:S(2)}, u32[]{:S(2)}) %collective-permute-start.5) | collective-permute-done | bytes 524320 | tf_op jit(solution)/shard_map/ppermute | solution.py:20
  127.1 4.7 %shard_map.32 = (bf16[2,16,16,128]{3,2,1,0:T(8,128)(2,1)S(1)}, bf16[2,16,16,128]{3,2,1,0:T(8,128)(2,1)S(1)}, bf16[2,16,16,128]{3,2,1,0:T(8,128)(2,1)S(1)}, bf16[...) custom-call(s32[4]{0:T(128)S(1)} %get-tuple-element.47.scalars, ...), custom_call_target="tpu_custom_call" | custom-call | flops 503316480 | bytes 5963776 | tf_op jit(solution)/shard_map/pallas_call | solution.py:119
  131.7 0.8 copy-done.8
  132.5 0.7 copy-done.10
  133.3 3.5 %collective-permute-start.21 = (bf16[4,2,16,16,128]{4,3,2,1,0:T(8,128)(2,1)S(1)}, bf16[4,2,16,16,128]{4,3,2,1,0:T(8,128)(2,1)S(1)}, u32[]{:S(2)}, u32[]{:S(2)}) collective-permute-start(bf16[4,2,16,16,128]{4,3,2,1,0:T(8,128)(2,1)S(1)} %get-tuple-element.39), channel_id=1, source_target_pairs={{0,16},{4,20},{8,8},{12,12},{16,0},{20,4},{24,24},{28,28},{1,17},{... | collective-permute-start | bytes 1572872 | tf_op jit(solution)/shard_map/ppermute | solution.py:20
  136.8 1.4 collective-permute-start.22
  138.2 3.8 %collective-permute-start.23 = (bf16[2,16,16,128]{3,2,1,0:T(8,128)(2,1)S(1)}, bf16[2,16,16,128]{3,2,1,0:T(8,128)(2,1)S(1)}, u32[]{:S(2)}, u32[]{:S(2)}) collective-permute-start(bf16[2,16,16,128]{3,2,1,0:T(8,128)(2,1)S(1)} %get-tuple-element.41), channel_id=1, source_target_pairs={{0,9},{1,10},{2,11},{3,8},{4,13},{5,14},{6,15},{7,12},{8,1},{9,2},... | collective-permute-start | bytes 393224 | tf_op jit(solution)/shard_map/ppermute | solution.py:25
  141.9 1.0 collective-permute-start.24
  142.9 9.1 %collective-permute-done.22.refs_6_ = bf16[2,16,16,128]{3,2,1,0:T(8,128)(2,1)S(1)} collective-permute-done((bf16[2,16,16,128]{3,2,1,0:T(8,128)(2,1)}, bf16[2,16,16,128]{3,2,1,0:T(8,128)(2,1)S(1)}, u32[]{:S(2)}, u32[]{:S(2)}) %collective-permute-start.22) | collective-permute-done | bytes 131104 | tf_op jit(solution)/shard_map/ppermute | solution.py:25
  152.0 4.1 %collective-permute-start.26 = (bf16[2,16,16,128]{3,2,1,0:T(8,128)(2,1)S(1)}, bf16[2,16,16,128]{3,2,1,0:T(8,128)(2,1)S(1)}, u32[]{:S(2)}, u32[]{:S(2)}) collective-permute-start(bf16[2,16,16,128]{3,2,1,0:T(8,128)(2,1)S(1)} %get-tuple-element.44), channel_id=1, source_target_pairs={{0,17},{1,18},{2,19},{3,16},{4,21},{5,22},{6,23},{7,20},{8,9},{9,1... | collective-permute-start | bytes 393224 | tf_op jit(solution)/shard_map/ppermute | solution.py:25
  156.1 0.3 collective-permute-start.28
  156.4 5.4 %collective-permute-done.25.refs_9_ = bf16[2,16,16,128]{3,2,1,0:T(8,128)(2,1)S(1)} collective-permute-done((bf16[2,16,16,128]{3,2,1,0:T(8,128)(2,1)S(1)}, bf16[2,16,16,128]{3,2,1,0:T(8,128)(2,1)S(1)}, u32[]{:S(2)}, u32[]{:S(2)}) %collective-permute-start.25) | collective-permute-done | bytes 131104 | tf_op jit(solution)/shard_map/ppermute | solution.py:25
  161.8 1.6 collective-permute-start.27
  163.4 2.8 %collective-permute-start.29 = (bf16[2,16,16,128]{3,2,1,0:T(8,128)(2,1)S(1)}, bf16[2,16,16,128]{3,2,1,0:T(8,128)(2,1)S(1)}, u32[]{:S(2)}, u32[]{:S(2)}) collective-permute-start(bf16[2,16,16,128]{3,2,1,0:T(8,128)(2,1)S(1)} %get-tuple-element.46), channel_id=1, source_target_pairs={{0,16},{1,17},{2,18},{3,19},{4,20},{5,21},{6,22},{7,23},{8,8},{9,9... | collective-permute-start | bytes 393224 | tf_op jit(solution)/shard_map/ppermute | solution.py:25
  166.2 1.5 collective-permute-done.27.refs_11_
  167.7 2.6 %collective-permute-done.29.refs_13_ = bf16[2,16,16,128]{3,2,1,0:T(8,128)(2,1)S(1)} collective-permute-done((bf16[2,16,16,128]{3,2,1,0:T(8,128)(2,1)S(1)}, bf16[2,16,16,128]{3,2,1,0:T(8,128)(2,1)S(1)}, u32[]{:S(2)}, u32[]{:S(2)}) %collective-permute-start.29) | collective-permute-done | bytes 131104 | tf_op jit(solution)/shard_map/ppermute | solution.py:25
  170.3 1.0 copy-done.9
  171.3 7.7 %shard_map.34 = bf16[2,1,1024,1024]{3,2,1,0:T(8,128)(2,1)} custom-call(bf16[4,2,16,16,128]{4,3,2,1,0:T(8,128)(2,1)S(1)} %collective-permute-done.4.refs_0_, bf16[4,2,16,16,128]{4,3,2,1,0:T(8,128)(2,1)S(1)} %copy-done.9, bf16[4,2,16,16,128]{4,3,2,1,0:T(8,128)(2,1)} %collective-permute-done.10.refs_2_, ...), custom_call_target="tpu_custom_call" | custom-call | flops 4294967296 | bytes 10485760 | tf_op jit(solution)/shard_map/pallas_call | solution.py:214
  (58 shorter events, 0.7 us)
Async XLA Ops:
  2.9 25.0 %collective-permute-start = (bf16[16,240,128]{2,1,0:T(8,128)(2,1)}, bf16[16,240,128]{2,1,0:T(8,128)(2,1)}, u32[]{:S(2)}, u32[]{:S(2)}) collective-permute-start(bf16[16,240,128]{2,1,0:T(8,128)(2,1)} %get-tuple-element.26), channel_id=1, source_target_pairs={{0,8},{4,12},{8,0},{12,4},{16,24},{20,28},{24,16},{28,20},{1,9},{5... | collective-permute-start | bytes 2949128 | tf_op jit(solution)/shard_map/ppermute | solution.py:20
  5.8 23.5 %collective-permute-start.1 = (bf16[16,240,128]{2,1,0:T(8,128)(2,1)}, bf16[16,240,128]{2,1,0:T(8,128)(2,1)}, u32[]{:S(2)}, u32[]{:S(2)}) collective-permute-start(bf16[16,240,128]{2,1,0:T(8,128)(2,1)} %get-tuple-element.27.own), channel_id=1, source_target_pairs={{0,16},{4,20},{8,24},{12,28},{16,0},{20,4},{24,8},{28,12},{1,17},{... | collective-permute-start | bytes 2949128 | tf_op jit(solution)/shard_map/ppermute | solution.py:20
  10.1 2.6 %copy-start.11 = (f32[512]{0:T(512)S(1)}, f32[512]{0:T(512)}, u32[]{:S(2)}) copy-start(f32[512]{0:T(512)} %param.3) | copy-start | bytes 6148
  25.1 6.1 %copy-start.1 = (bf16[512,1024]{1,0:T(8,128)(2,1)}, bf16[512,1024]{1,0:T(8,128)(2,1)S(1)}, u32[]{:S(2)}) copy-start(bf16[512,1024]{1,0:T(8,128)(2,1)S(1)} %get-tuple-element.61.refs_7_.refs_15_) | copy-start | bytes 3145732
  25.1 6.1 %copy-start.2 = (bf16[512,1024]{1,0:T(8,128)(2,1)}, bf16[512,1024]{1,0:T(8,128)(2,1)S(1)}, u32[]{:S(2)}) copy-start(bf16[512,1024]{1,0:T(8,128)(2,1)S(1)} %get-tuple-element.62.refs_6_.refs_14_) | copy-start | bytes 3145732
  27.9 5.6 %collective-permute-start.2 = (bf16[16,240,128]{2,1,0:T(8,128)(2,1)}, bf16[16,240,128]{2,1,0:T(8,128)(2,1)S(1)}, u32[]{:S(2)}, u32[]{:S(2)}) collective-permute-start(bf16[16,240,128]{2,1,0:T(8,128)(2,1)} %collective-permute-done.x_mine), channel_id=1, source_target_pairs={{0,4},{4,0},{8,12},{12,8},{16,20},{20,16},{24,28},{28,24},{1,5},{5... | collective-permute-start | bytes 2949128 | tf_op jit(solution)/shard_map/ppermute | solution.py:20
  31.2 2.6 %collective-permute-start.3 = (bf16[16,240,128]{2,1,0:T(8,128)(2,1)S(1)}, bf16[16,240,128]{2,1,0:T(8,128)(2,1)S(1)}, u32[]{:S(2)}, u32[]{:S(2)}) collective-permute-start(bf16[16,240,128]{2,1,0:T(8,128)(2,1)S(1)} %shard_map.28), channel_id=1, source_target_pairs={{0,4},{4,0},{8,12},{12,8},{16,20},{20,16},{24,28},{28,24},{1,5},{5... | collective-permute-start | bytes 2949128 | tf_op jit(solution)/shard_map/ppermute | solution.py:20
  31.2 24.5 %collective-permute-start.6 = (bf16[16,240,128]{2,1,0:T(8,128)(2,1)}, bf16[16,240,128]{2,1,0:T(8,128)(2,1)}, u32[]{:S(2)}, u32[]{:S(2)}) collective-permute-start(bf16[16,240,128]{2,1,0:T(8,128)(2,1)} %get-tuple-element.29.refs_0_), channel_id=1, source_target_pairs={{0,8},{4,12},{8,0},{12,4},{16,24},{20,28},{24,16},{28,20},{1,9},{5... | collective-permute-start | bytes 2949128 | tf_op jit(solution)/shard_map/ppermute | solution.py:20
  32.0 23.7 %collective-permute-start.7 = (bf16[16,240,128]{2,1,0:T(8,128)(2,1)S(1)}, bf16[16,240,128]{2,1,0:T(8,128)(2,1)}, u32[]{:S(2)}, u32[]{:S(2)}) collective-permute-start(bf16[16,240,128]{2,1,0:T(8,128)(2,1)S(1)} %get-tuple-element.30.refs_1_), channel_id=1, source_target_pairs={{0,16},{4,20},{8,24},{12,28},{16,0},{20,4},{24,8},{28,12},{1,17},{... | collective-permute-start | bytes 2949128 | tf_op jit(solution)/shard_map/ppermute | solution.py:20
  38.7 1.0 copy-start
  39.7 31.0 %all-to-all-start = ((bf16[4,2,2,16,16,128]{5,4,3,2,1,0:T(8,128)(2,1)}), bf16[4,2,2,16,16,128]{5,4,3,2,1,0:T(8,128)(2,1)}, u32[]{:S(2)}, u32[]{:S(2)}) async-start(bf16[4,2,2,16,16,128]{5,4,3,2,1,0:T(8,128)(2,1)} %copy-done), calls=%async_computation | async-start | bytes 2097152 | tf_op jit(solution)/shard_map/all_to_all | solution.py:304
  55.7 4.0 %collective-permute-start.8 = (bf16[16,240,128]{2,1,0:T(8,128)(2,1)}, bf16[16,240,128]{2,1,0:T(8,128)(2,1)S(1)}, u32[]{:S(2)}, u32[]{:S(2)}) collective-permute-start(bf16[16,240,128]{2,1,0:T(8,128)(2,1)} %collective-permute-done.6.x_mine), channel_id=1, source_target_pairs={{0,4},{4,0},{8,12},{12,8},{16,20},{20,16},{24,28},{28,24},{1,5},{5... | collective-permute-start | bytes 2949128 | tf_op jit(solution)/shard_map/ppermute | solution.py:20
  57.1 2.6 %collective-permute-start.9 = (bf16[16,240,128]{2,1,0:T(8,128)(2,1)S(1)}, bf16[16,240,128]{2,1,0:T(8,128)(2,1)S(1)}, u32[]{:S(2)}, u32[]{:S(2)}) collective-permute-start(bf16[16,240,128]{2,1,0:T(8,128)(2,1)S(1)} %broadcast_select_fusion.2), channel_id=1, source_target_pairs={{0,4},{4,0},{8,12},{12,8},{16,20},{20,16},{24,28},{28,24},{1,5},{5... | collective-permute-start | bytes 2949128 | tf_op jit(solution)/shard_map/ppermute | solution.py:20
  57.2 24.5 %collective-permute-start.12 = (bf16[16,240,128]{2,1,0:T(8,128)(2,1)}, bf16[16,240,128]{2,1,0:T(8,128)(2,1)}, u32[]{:S(2)}, u32[]{:S(2)}) collective-permute-start(bf16[16,240,128]{2,1,0:T(8,128)(2,1)} %get-tuple-element.32.refs_2_), channel_id=1, source_target_pairs={{0,8},{4,12},{8,0},{12,4},{16,24},{20,28},{24,16},{28,20},{1,9},{5... | collective-permute-start | bytes 2949128 | tf_op jit(solution)/shard_map/ppermute | solution.py:20
  58.0 23.6 %collective-permute-start.13 = (bf16[16,240,128]{2,1,0:T(8,128)(2,1)S(1)}, bf16[16,240,128]{2,1,0:T(8,128)(2,1)S(1)}, u32[]{:S(2)}, u32[]{:S(2)}) collective-permute-start(bf16[16,240,128]{2,1,0:T(8,128)(2,1)S(1)} %get-tuple-element.33.refs_3_), channel_id=1, source_target_pairs={{0,16},{4,20},{8,24},{12,28},{16,0},{20,4},{24,8},{28,12},{1,17},{... | collective-permute-start | bytes 2949128 | tf_op jit(solution)/shard_map/ppermute | solution.py:20
  70.7 29.6 %all-to-all-start.1 = ((bf16[4,2,2,16,16,128]{5,4,3,2,1,0:T(8,128)(2,1)}), bf16[4,2,2,16,16,128]{5,4,3,2,1,0:T(8,128)(2,1)}, u32[]{:S(2)}, u32[]{:S(2)}) async-start(bf16[4,2,2,16,16,128]{5,4,3,2,1,0:T(8,128)(2,1)} %shard_map.30), calls=%async_computation.1 | async-start | bytes 2097152 | tf_op jit(solution)/shard_map/all_to_all | solution.py:304
  81.6 3.9 %collective-permute-start.14 = (bf16[16,240,128]{2,1,0:T(8,128)(2,1)}, bf16[16,240,128]{2,1,0:T(8,128)(2,1)S(1)}, u32[]{:S(2)}, u32[]{:S(2)}) collective-permute-start(bf16[16,240,128]{2,1,0:T(8,128)(2,1)} %collective-permute-done.12.x_mine), channel_id=1, source_target_pairs={{0,4},{4,0},{8,12},{12,8},{16,20},{20,16},{24,28},{28,24},{1,5},{5... | collective-permute-start | bytes 2949128 | tf_op jit(solution)/shard_map/ppermute | solution.py:20
  81.6 0.9 copy-start.6
  81.8 3.8 %collective-permute-start.15 = (bf16[16,240,128]{2,1,0:T(8,128)(2,1)S(1)}, bf16[16,240,128]{2,1,0:T(8,128)(2,1)S(1)}, u32[]{:S(2)}, u32[]{:S(2)}) collective-permute-start(bf16[16,240,128]{2,1,0:T(8,128)(2,1)S(1)} %broadcast_select_fusion.1), channel_id=1, source_target_pairs={{0,4},{4,0},{8,12},{12,8},{16,20},{20,16},{24,28},{28,24},{1,5},{5... | collective-permute-start | bytes 2949128 | tf_op jit(solution)/shard_map/ppermute | solution.py:20
  82.6 24.5 %collective-permute-start.16 = (bf16[16,240,128]{2,1,0:T(8,128)(2,1)}, bf16[16,240,128]{2,1,0:T(8,128)(2,1)}, u32[]{:S(2)}, u32[]{:S(2)}) collective-permute-start(bf16[16,240,128]{2,1,0:T(8,128)(2,1)} %get-tuple-element.35.refs_4_), channel_id=1, source_target_pairs={{0,8},{4,12},{8,0},{12,4},{16,24},{20,28},{24,16},{28,20},{1,9},{5... | collective-permute-start | bytes 2949128 | tf_op jit(solution)/shard_map/ppermute | solution.py:20
  84.0 23.1 %collective-permute-start.17 = (bf16[16,240,128]{2,1,0:T(8,128)(2,1)S(1)}, bf16[16,240,128]{2,1,0:T(8,128)(2,1)S(1)}, u32[]{:S(2)}, u32[]{:S(2)}) collective-permute-start(bf16[16,240,128]{2,1,0:T(8,128)(2,1)S(1)} %get-tuple-element.36.refs_5_), channel_id=1, source_target_pairs={{0,16},{4,20},{8,24},{12,28},{16,0},{20,4},{24,8},{28,12},{1,17},{... | collective-permute-start | bytes 2949128 | tf_op jit(solution)/shard_map/ppermute | solution.py:20
  85.6 1.2 copy-start.7
  100.2 33.0 %all-to-all-start.2 = ((bf16[4,2,2,16,16,128]{5,4,3,2,1,0:T(8,128)(2,1)}), bf16[4,2,2,16,16,128]{5,4,3,2,1,0:T(8,128)(2,1)S(1)}, u32[]{:S(2)}, u32[]{:S(2)}) async-start(bf16[4,2,2,16,16,128]{5,4,3,2,1,0:T(8,128)(2,1)} %shard_map.31), calls=%async_computation.2 | async-start | bytes 2097152 | tf_op jit(solution)/shard_map/all_to_all | solution.py:304
  107.1 9.2 %collective-permute-start.18 = (bf16[16,240,128]{2,1,0:T(8,128)(2,1)}, bf16[16,240,128]{2,1,0:T(8,128)(2,1)S(1)}, u32[]{:S(2)}, u32[]{:S(2)}) collective-permute-start(bf16[16,240,128]{2,1,0:T(8,128)(2,1)} %collective-permute-done.16.x_mine), channel_id=1, source_target_pairs={{0,4},{4,0},{8,12},{12,8},{16,20},{20,16},{24,28},{28,24},{1,5},{5... | collective-permute-start | bytes 2949128 | tf_op jit(solution)/shard_map/ppermute | solution.py:20
  107.1 2.1 %copy-start.4 = (bf16[16,240,128]{2,1,0:T(8,128)(2,1)}, bf16[16,240,128]{2,1,0:T(8,128)(2,1)S(1)}, u32[]{:S(2)}) copy-start(bf16[16,240,128]{2,1,0:T(8,128)(2,1)S(1)} %collective-permute-done.17.y_mine) | copy-start | bytes 2949124
  107.2 11.4 %collective-permute-start.19 = (bf16[16,240,128]{2,1,0:T(8,128)(2,1)S(1)}, bf16[16,240,128]{2,1,0:T(8,128)(2,1)S(1)}, u32[]{:S(2)}, u32[]{:S(2)}) collective-permute-start(bf16[16,240,128]{2,1,0:T(8,128)(2,1)S(1)} %broadcast_select_fusion), channel_id=1, source_target_pairs={{0,4},{4,0},{8,12},{12,8},{16,20},{20,16},{24,28},{28,24},{1,5},{5... | collective-permute-start | bytes 2949128 | tf_op jit(solution)/shard_map/ppermute | solution.py:20
  109.2 17.8 %copy-start.5 = (bf16[16,240,128]{2,1,0:T(8,128)(2,1)S(1)}, bf16[16,240,128]{2,1,0:T(8,128)(2,1)}, u32[]{:S(2)}) copy-start(bf16[16,240,128]{2,1,0:T(8,128)(2,1)} %copy-done.4) | copy-start | bytes 2949124
  109.2 14.8 %collective-permute-start.4 = (bf16[4,2,16,16,128]{4,3,2,1,0:T(8,128)(2,1)S(1)}, bf16[4,2,16,16,128]{4,3,2,1,0:T(8,128)(2,1)S(1)}, u32[]{:S(2)}, u32[]{:S(2)}) collective-permute-start(bf16[4,2,16,16,128]{4,3,2,1,0:T(8,128)(2,1)S(1)} %get-tuple-element.60), channel_id=1, source_target_pairs={{0,8},{4,12},{8,0},{12,4},{16,24},{20,28},{24,16},{28,20},{1,9},{5... | collective-permute-start | bytes 1572872 | tf_op jit(solution)/shard_map/ppermute | solution.py:20
  110.4 16.7 %collective-permute-start.5 = (bf16[4,2,16,16,128]{4,3,2,1,0:T(8,128)(2,1)S(1)}, bf16[4,2,16,16,128]{4,3,2,1,0:T(8,128)(2,1)S(1)}, u32[]{:S(2)}, u32[]{:S(2)}) collective-permute-start(bf16[4,2,16,16,128]{4,3,2,1,0:T(8,128)(2,1)S(1)} %get-tuple-element.59), channel_id=1, source_target_pairs={{0,16},{4,20},{8,8},{12,12},{16,0},{20,4},{24,24},{28,28},{1,17},{... | collective-permute-start | bytes 1572872 | tf_op jit(solution)/shard_map/ppermute | solution.py:20
  116.3 21.9 %collective-permute-start.10 = (bf16[4,2,16,16,128]{4,3,2,1,0:T(8,128)(2,1)}, bf16[4,2,16,16,128]{4,3,2,1,0:T(8,128)(2,1)}, u32[]{:S(2)}, u32[]{:S(2)}) collective-permute-start(bf16[4,2,16,16,128]{4,3,2,1,0:T(8,128)(2,1)} %get-tuple-element.58), channel_id=1, source_target_pairs={{0,8},{4,12},{8,0},{12,4},{16,24},{20,28},{24,16},{28,20},{1,9},{5... | collective-permute-start | bytes 1572872 | tf_op jit(solution)/shard_map/ppermute | solution.py:20
  116.3 25.7 %collective-permute-start.11 = (bf16[4,2,16,16,128]{4,3,2,1,0:T(8,128)(2,1)}, bf16[4,2,16,16,128]{4,3,2,1,0:T(8,128)(2,1)}, u32[]{:S(2)}, u32[]{:S(2)}) collective-permute-start(bf16[4,2,16,16,128]{4,3,2,1,0:T(8,128)(2,1)} %get-tuple-element.57), channel_id=1, source_target_pairs={{0,16},{4,20},{8,8},{12,12},{16,0},{20,4},{24,24},{28,28},{1,17},{... | collective-permute-start | bytes 1572872 | tf_op jit(solution)/shard_map/ppermute | solution.py:20
  127.1 43.2 %copy-start.3 = (bf16[512,1024]{1,0:T(8,128)(2,1)S(1)}, bf16[512,1024]{1,0:T(8,128)(2,1)}, u32[]{:S(2)}) copy-start(bf16[512,1024]{1,0:T(8,128)(2,1)} %copy-done.2) | copy-start | bytes 3145732
  131.7 0.8 copy-start.8
  132.5 0.7 copy-start.10
  133.3 37.0 %collective-permute-start.20 = (bf16[4,2,16,16,128]{4,3,2,1,0:T(8,128)(2,1)S(1)}, bf16[4,2,16,16,128]{4,3,2,1,0:T(8,128)(2,1)S(1)}, u32[]{:S(2)}, u32[]{:S(2)}) collective-permute-start(bf16[4,2,16,16,128]{4,3,2,1,0:T(8,128)(2,1)S(1)} %get-tuple-element.38), channel_id=1, source_target_pairs={{0,8},{4,12},{8,0},{12,4},{16,24},{20,28},{24,16},{28,20},{1,9},{5... | collective-permute-start | bytes 1572872 | tf_op jit(solution)/shard_map/ppermute | solution.py:20
  133.3 36.9 %collective-permute-start.21 = (bf16[4,2,16,16,128]{4,3,2,1,0:T(8,128)(2,1)S(1)}, bf16[4,2,16,16,128]{4,3,2,1,0:T(8,128)(2,1)S(1)}, u32[]{:S(2)}, u32[]{:S(2)}) collective-permute-start(bf16[4,2,16,16,128]{4,3,2,1,0:T(8,128)(2,1)S(1)} %get-tuple-element.39), channel_id=1, source_target_pairs={{0,16},{4,20},{8,8},{12,12},{16,0},{20,4},{24,24},{28,28},{1,17},{... | collective-permute-start | bytes 1572872 | tf_op jit(solution)/shard_map/ppermute | solution.py:20
  136.8 15.2 %collective-permute-start.22 = (bf16[2,16,16,128]{3,2,1,0:T(8,128)(2,1)}, bf16[2,16,16,128]{3,2,1,0:T(8,128)(2,1)S(1)}, u32[]{:S(2)}, u32[]{:S(2)}) collective-permute-start(bf16[2,16,16,128]{3,2,1,0:T(8,128)(2,1)} %copy-done.10), channel_id=1, source_target_pairs={{0,10},{1,11},{2,8},{3,9},{4,14},{5,15},{6,12},{7,13},{8,2},{9,3},... | collective-permute-start | bytes 393224 | tf_op jit(solution)/shard_map/ppermute | solution.py:25
  138.2 13.8 %collective-permute-start.23 = (bf16[2,16,16,128]{3,2,1,0:T(8,128)(2,1)S(1)}, bf16[2,16,16,128]{3,2,1,0:T(8,128)(2,1)S(1)}, u32[]{:S(2)}, u32[]{:S(2)}) collective-permute-start(bf16[2,16,16,128]{3,2,1,0:T(8,128)(2,1)S(1)} %get-tuple-element.41), channel_id=1, source_target_pairs={{0,9},{1,10},{2,11},{3,8},{4,13},{5,14},{6,15},{7,12},{8,1},{9,2},... | collective-permute-start | bytes 393224 | tf_op jit(solution)/shard_map/ppermute | solution.py:25
  141.9 14.2 %collective-permute-start.24 = (bf16[2,16,16,128]{3,2,1,0:T(8,128)(2,1)S(1)}, bf16[2,16,16,128]{3,2,1,0:T(8,128)(2,1)S(1)}, u32[]{:S(2)}, u32[]{:S(2)}) collective-permute-start(bf16[2,16,16,128]{3,2,1,0:T(8,128)(2,1)S(1)} %get-tuple-element.42), channel_id=1, source_target_pairs={{0,11},{1,8},{2,9},{3,10},{4,15},{5,12},{6,13},{7,14},{8,3},{9,0},... | collective-permute-start | bytes 393224 | tf_op jit(solution)/shard_map/ppermute | solution.py:25
  152.0 9.8 %collective-permute-start.25 = (bf16[2,16,16,128]{3,2,1,0:T(8,128)(2,1)S(1)}, bf16[2,16,16,128]{3,2,1,0:T(8,128)(2,1)S(1)}, u32[]{:S(2)}, u32[]{:S(2)}) collective-permute-start(bf16[2,16,16,128]{3,2,1,0:T(8,128)(2,1)S(1)} %get-tuple-element.43), channel_id=1, source_target_pairs={{0,18},{1,19},{2,16},{3,17},{4,22},{5,23},{6,20},{7,21},{8,10},{9,... | collective-permute-start | bytes 393224 | tf_op jit(solution)/shard_map/ppermute | solution.py:25
  152.0 11.4 %collective-permute-start.26 = (bf16[2,16,16,128]{3,2,1,0:T(8,128)(2,1)S(1)}, bf16[2,16,16,128]{3,2,1,0:T(8,128)(2,1)S(1)}, u32[]{:S(2)}, u32[]{:S(2)}) collective-permute-start(bf16[2,16,16,128]{3,2,1,0:T(8,128)(2,1)S(1)} %get-tuple-element.44), channel_id=1, source_target_pairs={{0,17},{1,18},{2,19},{3,16},{4,21},{5,22},{6,23},{7,20},{8,9},{9,1... | collective-permute-start | bytes 393224 | tf_op jit(solution)/shard_map/ppermute | solution.py:25
  156.1 11.6 %collective-permute-start.28 = (bf16[2,16,16,128]{3,2,1,0:T(8,128)(2,1)S(1)}, bf16[2,16,16,128]{3,2,1,0:T(8,128)(2,1)S(1)}, u32[]{:S(2)}, u32[]{:S(2)}) collective-permute-start(bf16[2,16,16,128]{3,2,1,0:T(8,128)(2,1)S(1)} %get-tuple-element.37.refs_0_), channel_id=1, source_target_pairs={{0,8},{1,9},{2,10},{3,11},{4,12},{5,13},{6,14},{7,15},{8,0},{9,1},... | collective-permute-start | bytes 393224 | tf_op jit(solution)/shard_map/ppermute | solution.py:25
  161.8 5.9 %collective-permute-start.27 = (bf16[2,16,16,128]{3,2,1,0:T(8,128)(2,1)S(1)}, bf16[2,16,16,128]{3,2,1,0:T(8,128)(2,1)S(1)}, u32[]{:S(2)}, u32[]{:S(2)}) collective-permute-start(bf16[2,16,16,128]{3,2,1,0:T(8,128)(2,1)S(1)} %get-tuple-element.45), channel_id=1, source_target_pairs={{0,19},{1,16},{2,17},{3,18},{4,23},{5,20},{6,21},{7,22},{8,11},{9,... | collective-permute-start | bytes 393224 | tf_op jit(solution)/shard_map/ppermute | solution.py:25
  163.4 6.9 %collective-permute-start.29 = (bf16[2,16,16,128]{3,2,1,0:T(8,128)(2,1)S(1)}, bf16[2,16,16,128]{3,2,1,0:T(8,128)(2,1)S(1)}, u32[]{:S(2)}, u32[]{:S(2)}) collective-permute-start(bf16[2,16,16,128]{3,2,1,0:T(8,128)(2,1)S(1)} %get-tuple-element.46), channel_id=1, source_target_pairs={{0,16},{1,17},{2,18},{3,19},{4,20},{5,21},{6,22},{7,23},{8,8},{9,9... | collective-permute-start | bytes 393224 | tf_op jit(solution)/shard_map/ppermute | solution.py:25
  170.3 1.0 copy-start.9

commit v4 on v3

--- a/solution.py
+++ b/solution.py
@@ -311,8 +311,7 @@
     far_first = sorted(range(shards), key=lambda distance: -min(distance, shards - distance))
     order = list(range(before))
     for first in range(before, len(blocks), 2 * shards):
-        order += [first + bundle * shards + distance for bundle in range(2) for distance in far_first[:-1]]
-        order += [first + bundle * shards + far_first[-1] for bundle in range(2)]
+        order += [first + bundle * shards + distance for distance in far_first for bundle in range(2)]
     return to_lags(blocks, order, cosines, sines)
 
 

time: 180 us -> 178 us (0.989)
  starting transfers between devices: 51.5 us -> 48.7 us
    ppermute x8, starting transfers between devices: 14.9 us -> 12.1 us  [permuted_far(): lax.ppermute(value, ('grp', 'frq'), [(group * shards + shard, target(grou...]
  transfers between devices with their start and end apart: 33 -> 33, of which waited for: 16 -> 18; matrix products, arithmetic and copies ran while one was open for 13% -> 13% of each run, Pallas kernels for 13% -> 13%
where the time goes in v4:
time: 178 us; the launch traced here: 177 us
  waiting for transfers between devices  66.5 us (37%)
  starting transfers between devices  48.7 us (27%)
  Pallas kernels  30.5 us (17%)
  local copies, waits for them, and re-layouts  19.9 us (11%)
  other arithmetic  11.1 us (6%)
    ppermute x22, waiting for transfers between devices, permuted(): lax.ppermute(value, 'grp', [(source, target(source) % count) for source i...  34.3 us
    ppermute x22, starting transfers between devices, permuted(): lax.ppermute(value, 'grp', [(source, target(source) % count) for source i...  24 us
    pallas_call x4, Pallas kernels, cross_spectra(): pl.pallas_call(functools.partial(cross_body, shards, step_freqs, len(earl...  21 us
    ppermute x8, waiting for transfers between devices, permuted_far(): lax.ppermute(value, ('grp', 'frq'), [(group * shards + shard, target(grou...  19.2 us
    all_to_all x3, waiting for transfers between devices, local(): lax.all_to_all(results[0], 'frq', split_axis=0, concat_axis=0, tiled=True)  12.9 us
    all_to_all x3, starting transfers between devices, local(): lax.all_to_all(results[0], 'frq', split_axis=0, concat_axis=0, tiled=True)  12.6 us
    ppermute x8, starting transfers between devices, permuted_far(): lax.ppermute(value, ('grp', 'frq'), [(group * shards + shard, target(grou...  12.1 us
    dynamic_slice x4, local copies, waits for them, and re-layouts, piece(): lax.dynamic_slice_in_dim(source, (half * chunks + chunk) * size, size, 0)  10.8 us
  transfers between devices with their start and end apart: 33, of which 18 were waited for; matrix products, arithmetic and copies ran while one was open for 13% of the time, Pallas kernels for 13%

profile of v4, /device:TPU:0, one launch (start us, length us, event | category | flops | bytes accessed | tf_op | source)
XLA Modules:
  0.0 177.0 jit_solution(4320904454866601208)
XLA Ops:
  0.0 2.9 %dynamic-slice_bitcast_fusion = (bf16[16,240,128]{2,1,0:T(8,128)(2,1)}, bf16[16,240,128]{2,1,0:T(8,128)(2,1)}) fusion(bf16[1,128,240,128]{3,2,1,0:T(8,128)(2,1)} %param.2, s32[]{:T(128)S(6)} %select_n.79, s32[]{:T(128)S(6)} %select_n.78), kind=kLoop, calls=%fused_computation.11 | loop fusion | bytes 3932168 | tf_op jit(solution)/shard_map/dynamic_slice | solution.py:268
  2.9 2.9 %collective-permute-start = (bf16[16,240,128]{2,1,0:T(8,128)(2,1)}, bf16[16,240,128]{2,1,0:T(8,128)(2,1)}, u32[]{:S(2)}, u32[]{:S(2)}) collective-permute-start(bf16[16,240,128]{2,1,0:T(8,128)(2,1)} %get-tuple-element.26), channel_id=1, source_target_pairs={{0,8},{4,12},{8,0},{12,4},{16,24},{20,28},{24,16},{28,20},{1,9},{5... | collective-permute-start | bytes 2949128 | tf_op jit(solution)/shard_map/ppermute | solution.py:20
  5.8 1.5 collective-permute-start.1
  7.4 2.7 %constant_dynamic-slice_fusion.4 = (bf16[16,240,128]{2,1,0:T(8,128)(2,1)S(1)}, bf16[16,240,128]{2,1,0:T(8,128)(2,1)}) fusion(bf16[128,240,128]{2,1,0:T(8,128)(2,1)} %bitcast.31, s32[]{:T(128)S(6)} %select_n.81, s32[]{:T(128)S(6)} %select_n.80), kind=kLoop, calls=%fused_computation.31 | loop fusion | bytes 3932168 | tf_op jit(solution)/shard_map/dynamic_slice | solution.py:268
  10.1 2.6 %constant_dynamic-slice_fusion.2 = (bf16[16,240,128]{2,1,0:T(8,128)(2,1)S(1)}, bf16[16,240,128]{2,1,0:T(8,128)(2,1)}) fusion(bf16[128,240,128]{2,1,0:T(8,128)(2,1)} %bitcast.32, s32[]{:T(128)S(6)} %select_n.83, s32[]{:T(128)S(6)} %select_n.82), kind=kLoop, calls=%fused_computation.29 | loop fusion | bytes 3932168 | tf_op jit(solution)/shard_map/dynamic_slice | solution.py:268
  12.7 0.1 reshape.90
  12.8 2.6 %constant_dynamic-slice_fusion = (bf16[16,240,128]{2,1,0:T(8,128)(2,1)S(1)}, bf16[16,240,128]{2,1,0:T(8,128)(2,1)}) fusion(bf16[128,240,128]{2,1,0:T(8,128)(2,1)} %bitcast.33, s32[]{:T(128)S(6)} %select_n.85, s32[]{:T(128)S(6)} %select_n.84), kind=kLoop, calls=%fused_computation.27 | loop fusion | bytes 3932168 | tf_op jit(solution)/shard_map/dynamic_slice | solution.py:268
  15.4 0.1 mul.137
  15.6 0.1 reshape.97
  15.9 9.2 %multiply_convert_fusion = (bf16[512,1024]{1,0:T(8,128)(2,1)S(1)}, bf16[512,1024]{1,0:T(8,128)(2,1)S(1)}) fusion(f32[512]{0:T(512)S(1)} %neg.8, s32[512]{0:T(512)S(1)} %reshape.97, f32[512]{0:T(512)S(1)} %mul.137), kind=kLoop, calls=%fused_computation.6 | loop fusion | flops 9437184 | bytes 2103296 | tf_op jit(solution)/shard_map/convert_element_type | solution.py:251
  25.1 2.8 %collective-permute-done.x_mine = bf16[16,240,128]{2,1,0:T(8,128)(2,1)} collective-permute-done((bf16[16,240,128]{2,1,0:T(8,128)(2,1)}, bf16[16,240,128]{2,1,0:T(8,128)(2,1)}, u32[]{:S(2)}, u32[]{:S(2)}) %collective-permute-start) | collective-permute-done | bytes 983072 | tf_op jit(solution)/shard_map/ppermute | solution.py:20
  27.9 1.5 collective-permute-done.1.y_mine
  29.4 1.8 shard_map.28
  31.2 0.8 collective-permute-start.6
  32.0 1.5 collective-permute-start.7
  33.5 0.2 collective-permute-done.3.last_other
  33.8 4.9 %shard_map.29 = bf16[4,2,2,16,16,128]{5,4,3,2,1,0:T(8,128)(2,1)S(1)} custom-call(s32[4]{0:T(128)S(1)} %get-tuple-element.65.scalars, bf16[128,240,128]{2,1,0:T(8,128)(2,1)} %bitcast.34, bf16[16,240,128]{2,1,0:T(8,128)(2,1)} %collective-permute-done.x_mine, bf16[16,240,128]{2,1,0:T(8,128)(2,1)} %collective-permute-done.1.y_mine, ...), custom_call_target="tpu_custom_call" | custom-call | flops 503316480 | bytes 5963776 | tf_op jit(solution)/shard_map/pallas_call | solution.py:119
  38.7 1.0 copy-done
  39.7 4.9 %all-to-all-start = ((bf16[4,2,2,16,16,128]{5,4,3,2,1,0:T(8,128)(2,1)}), bf16[4,2,2,16,16,128]{5,4,3,2,1,0:T(8,128)(2,1)}, u32[]{:S(2)}, u32[]{:S(2)}) async-start(bf16[4,2,2,16,16,128]{5,4,3,2,1,0:T(8,128)(2,1)} %copy-done), calls=%async_computation | async-start | bytes 2097152 | tf_op jit(solution)/shard_map/all_to_all | solution.py:304
  44.5 11.2 %collective-permute-done.6.x_mine = bf16[16,240,128]{2,1,0:T(8,128)(2,1)} collective-permute-done((bf16[16,240,128]{2,1,0:T(8,128)(2,1)}, bf16[16,240,128]{2,1,0:T(8,128)(2,1)}, u32[]{:S(2)}, u32[]{:S(2)}) %collective-permute-start.6) | collective-permute-done | bytes 983072 | tf_op jit(solution)/shard_map/ppermute | solution.py:20
  55.7 1.3 broadcast_select_fusion.2
  57.2 0.9 collective-permute-start.12
  58.0 1.7 collective-permute-start.13
  59.7 5.8 %shard_map.30 = bf16[4,2,2,16,16,128]{5,4,3,2,1,0:T(8,128)(2,1)} custom-call(s32[4]{0:T(128)S(1)} %get-tuple-element.64.scalars, bf16[128,240,128]{2,1,0:T(8,128)(2,1)} %bitcast.35, bf16[16,240,128]{2,1,0:T(8,128)(2,1)} %collective-permute-done.6.x_mine, bf16[16,240,128]{2,1,0:T(8,128)(2,1)} %collective-permute-done.7.y_mine, ...), custom_call_target="tpu_custom_call" | custom-call | flops 503316480 | bytes 5963776 | tf_op jit(solution)/shard_map/pallas_call | solution.py:119
  65.5 5.1 %all-to-all-done = bf16[4,2,2,16,16,128]{5,4,3,2,1,0:T(8,128)(2,1)} async-done(((bf16[4,2,2,16,16,128]{5,4,3,2,1,0:T(8,128)(2,1)}), bf16[4,2,2,16,16,128]{5,4,3,2,1,0:T(8,128)(2,1)}, u32[]{:S(2)}, u32[]{:S(2)}) %all-to-all-start) | async-done | bytes 1048608 | tf_op jit(solution)/shard_map/all_to_all | solution.py:304
  70.7 4.2 %all-to-all-start.1 = ((bf16[4,2,2,16,16,128]{5,4,3,2,1,0:T(8,128)(2,1)}), bf16[4,2,2,16,16,128]{5,4,3,2,1,0:T(8,128)(2,1)}, u32[]{:S(2)}, u32[]{:S(2)}) async-start(bf16[4,2,2,16,16,128]{5,4,3,2,1,0:T(8,128)(2,1)} %shard_map.30), calls=%async_computation.1 | async-start | bytes 2097152 | tf_op jit(solution)/shard_map/all_to_all | solution.py:304
  74.9 6.7 %collective-permute-done.12.x_mine = bf16[16,240,128]{2,1,0:T(8,128)(2,1)} collective-permute-done((bf16[16,240,128]{2,1,0:T(8,128)(2,1)}, bf16[16,240,128]{2,1,0:T(8,128)(2,1)}, u32[]{:S(2)}, u32[]{:S(2)}) %collective-permute-start.12) | collective-permute-done | bytes 983072 | tf_op jit(solution)/shard_map/ppermute | solution.py:20
  81.7 0.1 broadcast_select_fusion.1
  81.8 0.6 collective-permute-start.15
  82.3 0.3 copy-done.6
  82.6 1.4 collective-permute-start.16
  84.0 1.5 collective-permute-start.17
  85.6 1.2 copy-done.7
  86.8 5.6 %shard_map.31 = bf16[4,2,2,16,16,128]{5,4,3,2,1,0:T(8,128)(2,1)} custom-call(s32[4]{0:T(128)S(1)} %get-tuple-element.63.scalars, bf16[128,240,128]{2,1,0:T(8,128)(2,1)} %bitcast.36, bf16[16,240,128]{2,1,0:T(8,128)(2,1)} %collective-permute-done.12.x_mine, bf16[16,240,128]{2,1,0:T(8,128)(2,1)S(1)} %copy-done.7, ...), custom_call_target="tpu_custom_call" | custom-call | flops 503316480 | bytes 5963776 | tf_op jit(solution)/shard_map/pallas_call | solution.py:119
  92.4 7.8 %all-to-all-done.1 = bf16[4,2,2,16,16,128]{5,4,3,2,1,0:T(8,128)(2,1)} async-done(((bf16[4,2,2,16,16,128]{5,4,3,2,1,0:T(8,128)(2,1)}), bf16[4,2,2,16,16,128]{5,4,3,2,1,0:T(8,128)(2,1)}, u32[]{:S(2)}, u32[]{:S(2)}) %all-to-all-start.1) | async-done | bytes 1048608 | tf_op jit(solution)/shard_map/all_to_all | solution.py:304
  100.2 3.5 %all-to-all-start.2 = ((bf16[4,2,2,16,16,128]{5,4,3,2,1,0:T(8,128)(2,1)}), bf16[4,2,2,16,16,128]{5,4,3,2,1,0:T(8,128)(2,1)S(1)}, u32[]{:S(2)}, u32[]{:S(2)}) async-start(bf16[4,2,2,16,16,128]{5,4,3,2,1,0:T(8,128)(2,1)} %shard_map.31), calls=%async_computation.2 | async-start | bytes 2097152 | tf_op jit(solution)/shard_map/all_to_all | solution.py:304
  103.8 3.3 %collective-permute-done.16.x_mine = bf16[16,240,128]{2,1,0:T(8,128)(2,1)} collective-permute-done((bf16[16,240,128]{2,1,0:T(8,128)(2,1)}, bf16[16,240,128]{2,1,0:T(8,128)(2,1)}, u32[]{:S(2)}, u32[]{:S(2)}) %collective-permute-start.16) | collective-permute-done | bytes 983072 | tf_op jit(solution)/shard_map/ppermute | solution.py:20
  107.1 0.1 broadcast_select_fusion
  107.2 0.5 collective-permute-start.19
  107.8 1.4 slice_bitcast_fusion.2
  109.2 1.2 collective-permute-start.4
  110.4 3.4 %collective-permute-start.5 = (bf16[4,2,16,16,128]{4,3,2,1,0:T(8,128)(2,1)S(1)}, bf16[4,2,16,16,128]{4,3,2,1,0:T(8,128)(2,1)S(1)}, u32[]{:S(2)}, u32[]{:S(2)}) collective-permute-start(bf16[4,2,16,16,128]{4,3,2,1,0:T(8,128)(2,1)S(1)} %get-tuple-element.59), channel_id=1, source_target_pairs={{0,16},{4,20},{8,8},{12,12},{16,0},{20,4},{24,24},{28,28},{1,17},{... | collective-permute-start | bytes 1572872 | tf_op jit(solution)/shard_map/ppermute | solution.py:20
  113.8 2.4 %slice_bitcast_fusion = (bf16[4,2,16,16,128]{4,3,2,1,0:T(8,128)(2,1)}, bf16[4,2,16,16,128]{4,3,2,1,0:T(8,128)(2,1)}) fusion(bf16[4,2,2,16,16,128]{5,4,3,2,1,0:T(8,128)(2,1)} %all-to-all-done.1), kind=kLoop, calls=%fused_computation.16 | loop fusion | bytes 2097152 | tf_op jit(solution)/shard_map/squeeze | solution.py:307
  116.3 2.4 %collective-permute-start.11 = (bf16[4,2,16,16,128]{4,3,2,1,0:T(8,128)(2,1)}, bf16[4,2,16,16,128]{4,3,2,1,0:T(8,128)(2,1)}, u32[]{:S(2)}, u32[]{:S(2)}) collective-permute-start(bf16[4,2,16,16,128]{4,3,2,1,0:T(8,128)(2,1)} %get-tuple-element.57), channel_id=1, source_target_pairs={{0,16},{4,20},{8,8},{12,12},{16,0},{20,4},{24,24},{28,28},{1,17},{... | collective-permute-start | bytes 1572872 | tf_op jit(solution)/shard_map/ppermute | solution.py:20
  118.7 5.4 %collective-permute-done.4.refs_0_ = bf16[4,2,16,16,128]{4,3,2,1,0:T(8,128)(2,1)S(1)} collective-permute-done((bf16[4,2,16,16,128]{4,3,2,1,0:T(8,128)(2,1)S(1)}, bf16[4,2,16,16,128]{4,3,2,1,0:T(8,128)(2,1)S(1)}, u32[]{:S(2)}, u32[]{:S(2)}) %collective-permute-start.4) | collective-permute-done | bytes 524320 | tf_op jit(solution)/shard_map/ppermute | solution.py:20
  124.0 3.0 %collective-permute-done.5.refs_1_ = bf16[4,2,16,16,128]{4,3,2,1,0:T(8,128)(2,1)S(1)} collective-permute-done((bf16[4,2,16,16,128]{4,3,2,1,0:T(8,128)(2,1)S(1)}, bf16[4,2,16,16,128]{4,3,2,1,0:T(8,128)(2,1)S(1)}, u32[]{:S(2)}, u32[]{:S(2)}) %collective-permute-start.5) | collective-permute-done | bytes 524320 | tf_op jit(solution)/shard_map/ppermute | solution.py:20
  127.1 4.7 %shard_map.32 = (bf16[2,16,16,128]{3,2,1,0:T(8,128)(2,1)S(1)}, bf16[2,16,16,128]{3,2,1,0:T(8,128)(2,1)S(1)}, bf16[2,16,16,128]{3,2,1,0:T(8,128)(2,1)S(1)}, bf16[...) custom-call(s32[4]{0:T(128)S(1)} %get-tuple-element.47.scalars, ...), custom_call_target="tpu_custom_call" | custom-call | flops 503316480 | bytes 5963776 | tf_op jit(solution)/shard_map/pallas_call | solution.py:119
  131.7 0.8 copy-done.8
  132.5 0.7 copy-done.10
  133.3 3.5 %collective-permute-start.21 = (bf16[4,2,16,16,128]{4,3,2,1,0:T(8,128)(2,1)S(1)}, bf16[4,2,16,16,128]{4,3,2,1,0:T(8,128)(2,1)S(1)}, u32[]{:S(2)}, u32[]{:S(2)}) collective-permute-start(bf16[4,2,16,16,128]{4,3,2,1,0:T(8,128)(2,1)S(1)} %get-tuple-element.39), channel_id=1, source_target_pairs={{0,16},{4,20},{8,8},{12,12},{16,0},{20,4},{24,24},{28,28},{1,17},{... | collective-permute-start | bytes 1572872 | tf_op jit(solution)/shard_map/ppermute | solution.py:20
  136.8 1.4 collective-permute-start.22
  138.2 1.3 collective-permute-start.23
  139.5 2.8 %collective-permute-start.24 = (bf16[2,16,16,128]{3,2,1,0:T(8,128)(2,1)S(1)}, bf16[2,16,16,128]{3,2,1,0:T(8,128)(2,1)S(1)}, u32[]{:S(2)}, u32[]{:S(2)}) collective-permute-start(bf16[2,16,16,128]{3,2,1,0:T(8,128)(2,1)S(1)} %get-tuple-element.42), channel_id=1, source_target_pairs={{0,9},{1,10},{2,11},{3,8},{4,13},{5,14},{6,15},{7,12},{8,1},{9,2},... | collective-permute-start | bytes 393224 | tf_op jit(solution)/shard_map/ppermute | solution.py:25
  142.3 10.0 %collective-permute-done.22.refs_6_ = bf16[2,16,16,128]{3,2,1,0:T(8,128)(2,1)S(1)} collective-permute-done((bf16[2,16,16,128]{3,2,1,0:T(8,128)(2,1)}, bf16[2,16,16,128]{3,2,1,0:T(8,128)(2,1)S(1)}, u32[]{:S(2)}, u32[]{:S(2)}) %collective-permute-start.22) | collective-permute-done | bytes 131104 | tf_op jit(solution)/shard_map/ppermute | solution.py:25
  152.3 1.9 %collective-permute-done.23.refs_7_ = bf16[2,16,16,128]{3,2,1,0:T(8,128)(2,1)S(1)} collective-permute-done((bf16[2,16,16,128]{3,2,1,0:T(8,128)(2,1)S(1)}, bf16[2,16,16,128]{3,2,1,0:T(8,128)(2,1)S(1)}, u32[]{:S(2)}, u32[]{:S(2)}) %collective-permute-start.23) | collective-permute-done | bytes 131104 | tf_op jit(solution)/shard_map/ppermute | solution.py:25
  154.2 1.7 collective-permute-start.26
  155.9 1.6 collective-permute-start.28
  157.5 2.5 %collective-permute-done.25.refs_9_ = bf16[2,16,16,128]{3,2,1,0:T(8,128)(2,1)S(1)} collective-permute-done((bf16[2,16,16,128]{3,2,1,0:T(8,128)(2,1)S(1)}, bf16[2,16,16,128]{3,2,1,0:T(8,128)(2,1)S(1)}, u32[]{:S(2)}, u32[]{:S(2)}) %collective-permute-start.25) | collective-permute-done | bytes 131104 | tf_op jit(solution)/shard_map/ppermute | solution.py:25
  160.0 1.3 collective-permute-done.26.refs_10_
  161.3 3.3 %collective-permute-start.29 = (bf16[2,16,16,128]{3,2,1,0:T(8,128)(2,1)S(1)}, bf16[2,16,16,128]{3,2,1,0:T(8,128)(2,1)S(1)}, u32[]{:S(2)}, u32[]{:S(2)}) collective-permute-start(bf16[2,16,16,128]{3,2,1,0:T(8,128)(2,1)S(1)} %get-tuple-element.46), channel_id=1, source_target_pairs={{0,16},{1,17},{2,18},{3,19},{4,20},{5,21},{6,22},{7,23},{8,8},{9,9... | collective-permute-start | bytes 393224 | tf_op jit(solution)/shard_map/ppermute | solution.py:25
  164.7 1.2 collective-permute-done.27.refs_11_
  165.9 2.3 %collective-permute-done.29.refs_13_ = bf16[2,16,16,128]{3,2,1,0:T(8,128)(2,1)S(1)} collective-permute-done((bf16[2,16,16,128]{3,2,1,0:T(8,128)(2,1)S(1)}, bf16[2,16,16,128]{3,2,1,0:T(8,128)(2,1)S(1)}, u32[]{:S(2)}, u32[]{:S(2)}) %collective-permute-start.29) | collective-permute-done | bytes 131104 | tf_op jit(solution)/shard_map/ppermute | solution.py:25
  168.2 1.0 copy-done.9
  169.2 7.7 %shard_map.34 = bf16[2,1,1024,1024]{3,2,1,0:T(8,128)(2,1)} custom-call(bf16[4,2,16,16,128]{4,3,2,1,0:T(8,128)(2,1)S(1)} %collective-permute-done.4.refs_0_, bf16[4,2,16,16,128]{4,3,2,1,0:T(8,128)(2,1)S(1)} %copy-done.9, bf16[4,2,16,16,128]{4,3,2,1,0:T(8,128)(2,1)} %collective-permute-done.10.refs_2_, ...), custom_call_target="tpu_custom_call" | custom-call | flops 4294967296 | bytes 10485760 | tf_op jit(solution)/shard_map/pallas_call | solution.py:214
  (58 shorter events, 0.8 us)
Async XLA Ops:
  2.9 25.0 %collective-permute-start = (bf16[16,240,128]{2,1,0:T(8,128)(2,1)}, bf16[16,240,128]{2,1,0:T(8,128)(2,1)}, u32[]{:S(2)}, u32[]{:S(2)}) collective-permute-start(bf16[16,240,128]{2,1,0:T(8,128)(2,1)} %get-tuple-element.26), channel_id=1, source_target_pairs={{0,8},{4,12},{8,0},{12,4},{16,24},{20,28},{24,16},{28,20},{1,9},{5... | collective-permute-start | bytes 2949128 | tf_op jit(solution)/shard_map/ppermute | solution.py:20
  5.8 23.5 %collective-permute-start.1 = (bf16[16,240,128]{2,1,0:T(8,128)(2,1)}, bf16[16,240,128]{2,1,0:T(8,128)(2,1)}, u32[]{:S(2)}, u32[]{:S(2)}) collective-permute-start(bf16[16,240,128]{2,1,0:T(8,128)(2,1)} %get-tuple-element.27.own), channel_id=1, source_target_pairs={{0,16},{4,20},{8,24},{12,28},{16,0},{20,4},{24,8},{28,12},{1,17},{... | collective-permute-start | bytes 2949128 | tf_op jit(solution)/shard_map/ppermute | solution.py:20
  10.1 2.6 %copy-start.11 = (f32[512]{0:T(512)S(1)}, f32[512]{0:T(512)}, u32[]{:S(2)}) copy-start(f32[512]{0:T(512)} %param.3) | copy-start | bytes 6148
  25.1 6.1 %copy-start.1 = (bf16[512,1024]{1,0:T(8,128)(2,1)}, bf16[512,1024]{1,0:T(8,128)(2,1)S(1)}, u32[]{:S(2)}) copy-start(bf16[512,1024]{1,0:T(8,128)(2,1)S(1)} %get-tuple-element.61.refs_7_.refs_15_) | copy-start | bytes 3145732
  25.1 6.1 %copy-start.2 = (bf16[512,1024]{1,0:T(8,128)(2,1)}, bf16[512,1024]{1,0:T(8,128)(2,1)S(1)}, u32[]{:S(2)}) copy-start(bf16[512,1024]{1,0:T(8,128)(2,1)S(1)} %get-tuple-element.62.refs_6_.refs_14_) | copy-start | bytes 3145732
  27.9 5.6 %collective-permute-start.2 = (bf16[16,240,128]{2,1,0:T(8,128)(2,1)}, bf16[16,240,128]{2,1,0:T(8,128)(2,1)S(1)}, u32[]{:S(2)}, u32[]{:S(2)}) collective-permute-start(bf16[16,240,128]{2,1,0:T(8,128)(2,1)} %collective-permute-done.x_mine), channel_id=1, source_target_pairs={{0,4},{4,0},{8,12},{12,8},{16,20},{20,16},{24,28},{28,24},{1,5},{5... | collective-permute-start | bytes 2949128 | tf_op jit(solution)/shard_map/ppermute | solution.py:20
  31.2 2.6 %collective-permute-start.3 = (bf16[16,240,128]{2,1,0:T(8,128)(2,1)S(1)}, bf16[16,240,128]{2,1,0:T(8,128)(2,1)S(1)}, u32[]{:S(2)}, u32[]{:S(2)}) collective-permute-start(bf16[16,240,128]{2,1,0:T(8,128)(2,1)S(1)} %shard_map.28), channel_id=1, source_target_pairs={{0,4},{4,0},{8,12},{12,8},{16,20},{20,16},{24,28},{28,24},{1,5},{5... | collective-permute-start | bytes 2949128 | tf_op jit(solution)/shard_map/ppermute | solution.py:20
  31.2 24.5 %collective-permute-start.6 = (bf16[16,240,128]{2,1,0:T(8,128)(2,1)}, bf16[16,240,128]{2,1,0:T(8,128)(2,1)}, u32[]{:S(2)}, u32[]{:S(2)}) collective-permute-start(bf16[16,240,128]{2,1,0:T(8,128)(2,1)} %get-tuple-element.29.refs_0_), channel_id=1, source_target_pairs={{0,8},{4,12},{8,0},{12,4},{16,24},{20,28},{24,16},{28,20},{1,9},{5... | collective-permute-start | bytes 2949128 | tf_op jit(solution)/shard_map/ppermute | solution.py:20
  32.0 23.7 %collective-permute-start.7 = (bf16[16,240,128]{2,1,0:T(8,128)(2,1)S(1)}, bf16[16,240,128]{2,1,0:T(8,128)(2,1)}, u32[]{:S(2)}, u32[]{:S(2)}) collective-permute-start(bf16[16,240,128]{2,1,0:T(8,128)(2,1)S(1)} %get-tuple-element.30.refs_1_), channel_id=1, source_target_pairs={{0,16},{4,20},{8,24},{12,28},{16,0},{20,4},{24,8},{28,12},{1,17},{... | collective-permute-start | bytes 2949128 | tf_op jit(solution)/shard_map/ppermute | solution.py:20
  38.7 1.0 copy-start
  39.7 31.0 %all-to-all-start = ((bf16[4,2,2,16,16,128]{5,4,3,2,1,0:T(8,128)(2,1)}), bf16[4,2,2,16,16,128]{5,4,3,2,1,0:T(8,128)(2,1)}, u32[]{:S(2)}, u32[]{:S(2)}) async-start(bf16[4,2,2,16,16,128]{5,4,3,2,1,0:T(8,128)(2,1)} %copy-done), calls=%async_computation | async-start | bytes 2097152 | tf_op jit(solution)/shard_map/all_to_all | solution.py:304
  55.7 4.0 %collective-permute-start.8 = (bf16[16,240,128]{2,1,0:T(8,128)(2,1)}, bf16[16,240,128]{2,1,0:T(8,128)(2,1)S(1)}, u32[]{:S(2)}, u32[]{:S(2)}) collective-permute-start(bf16[16,240,128]{2,1,0:T(8,128)(2,1)} %collective-permute-done.6.x_mine), channel_id=1, source_target_pairs={{0,4},{4,0},{8,12},{12,8},{16,20},{20,16},{24,28},{28,24},{1,5},{5... | collective-permute-start | bytes 2949128 | tf_op jit(solution)/shard_map/ppermute | solution.py:20
  57.1 2.6 %collective-permute-start.9 = (bf16[16,240,128]{2,1,0:T(8,128)(2,1)S(1)}, bf16[16,240,128]{2,1,0:T(8,128)(2,1)S(1)}, u32[]{:S(2)}, u32[]{:S(2)}) collective-permute-start(bf16[16,240,128]{2,1,0:T(8,128)(2,1)S(1)} %broadcast_select_fusion.2), channel_id=1, source_target_pairs={{0,4},{4,0},{8,12},{12,8},{16,20},{20,16},{24,28},{28,24},{1,5},{5... | collective-permute-start | bytes 2949128 | tf_op jit(solution)/shard_map/ppermute | solution.py:20
  57.2 24.5 %collective-permute-start.12 = (bf16[16,240,128]{2,1,0:T(8,128)(2,1)}, bf16[16,240,128]{2,1,0:T(8,128)(2,1)}, u32[]{:S(2)}, u32[]{:S(2)}) collective-permute-start(bf16[16,240,128]{2,1,0:T(8,128)(2,1)} %get-tuple-element.32.refs_2_), channel_id=1, source_target_pairs={{0,8},{4,12},{8,0},{12,4},{16,24},{20,28},{24,16},{28,20},{1,9},{5... | collective-permute-start | bytes 2949128 | tf_op jit(solution)/shard_map/ppermute | solution.py:20
  58.0 23.6 %collective-permute-start.13 = (bf16[16,240,128]{2,1,0:T(8,128)(2,1)S(1)}, bf16[16,240,128]{2,1,0:T(8,128)(2,1)S(1)}, u32[]{:S(2)}, u32[]{:S(2)}) collective-permute-start(bf16[16,240,128]{2,1,0:T(8,128)(2,1)S(1)} %get-tuple-element.33.refs_3_), channel_id=1, source_target_pairs={{0,16},{4,20},{8,24},{12,28},{16,0},{20,4},{24,8},{28,12},{1,17},{... | collective-permute-start | bytes 2949128 | tf_op jit(solution)/shard_map/ppermute | solution.py:20
  70.7 29.6 %all-to-all-start.1 = ((bf16[4,2,2,16,16,128]{5,4,3,2,1,0:T(8,128)(2,1)}), bf16[4,2,2,16,16,128]{5,4,3,2,1,0:T(8,128)(2,1)}, u32[]{:S(2)}, u32[]{:S(2)}) async-start(bf16[4,2,2,16,16,128]{5,4,3,2,1,0:T(8,128)(2,1)} %shard_map.30), calls=%async_computation.1 | async-start | bytes 2097152 | tf_op jit(solution)/shard_map/all_to_all | solution.py:304
  81.6 3.9 %collective-permute-start.14 = (bf16[16,240,128]{2,1,0:T(8,128)(2,1)}, bf16[16,240,128]{2,1,0:T(8,128)(2,1)S(1)}, u32[]{:S(2)}, u32[]{:S(2)}) collective-permute-start(bf16[16,240,128]{2,1,0:T(8,128)(2,1)} %collective-permute-done.12.x_mine), channel_id=1, source_target_pairs={{0,4},{4,0},{8,12},{12,8},{16,20},{20,16},{24,28},{28,24},{1,5},{5... | collective-permute-start | bytes 2949128 | tf_op jit(solution)/shard_map/ppermute | solution.py:20
  81.6 0.9 copy-start.6
  81.8 3.8 %collective-permute-start.15 = (bf16[16,240,128]{2,1,0:T(8,128)(2,1)S(1)}, bf16[16,240,128]{2,1,0:T(8,128)(2,1)S(1)}, u32[]{:S(2)}, u32[]{:S(2)}) collective-permute-start(bf16[16,240,128]{2,1,0:T(8,128)(2,1)S(1)} %broadcast_select_fusion.1), channel_id=1, source_target_pairs={{0,4},{4,0},{8,12},{12,8},{16,20},{20,16},{24,28},{28,24},{1,5},{5... | collective-permute-start | bytes 2949128 | tf_op jit(solution)/shard_map/ppermute | solution.py:20
  82.6 24.5 %collective-permute-start.16 = (bf16[16,240,128]{2,1,0:T(8,128)(2,1)}, bf16[16,240,128]{2,1,0:T(8,128)(2,1)}, u32[]{:S(2)}, u32[]{:S(2)}) collective-permute-start(bf16[16,240,128]{2,1,0:T(8,128)(2,1)} %get-tuple-element.35.refs_4_), channel_id=1, source_target_pairs={{0,8},{4,12},{8,0},{12,4},{16,24},{20,28},{24,16},{28,20},{1,9},{5... | collective-permute-start | bytes 2949128 | tf_op jit(solution)/shard_map/ppermute | solution.py:20
  84.0 23.1 %collective-permute-start.17 = (bf16[16,240,128]{2,1,0:T(8,128)(2,1)S(1)}, bf16[16,240,128]{2,1,0:T(8,128)(2,1)S(1)}, u32[]{:S(2)}, u32[]{:S(2)}) collective-permute-start(bf16[16,240,128]{2,1,0:T(8,128)(2,1)S(1)} %get-tuple-element.36.refs_5_), channel_id=1, source_target_pairs={{0,16},{4,20},{8,24},{12,28},{16,0},{20,4},{24,8},{28,12},{1,17},{... | collective-permute-start | bytes 2949128 | tf_op jit(solution)/shard_map/ppermute | solution.py:20
  85.6 1.2 copy-start.7
  100.2 33.0 %all-to-all-start.2 = ((bf16[4,2,2,16,16,128]{5,4,3,2,1,0:T(8,128)(2,1)}), bf16[4,2,2,16,16,128]{5,4,3,2,1,0:T(8,128)(2,1)S(1)}, u32[]{:S(2)}, u32[]{:S(2)}) async-start(bf16[4,2,2,16,16,128]{5,4,3,2,1,0:T(8,128)(2,1)} %shard_map.31), calls=%async_computation.2 | async-start | bytes 2097152 | tf_op jit(solution)/shard_map/all_to_all | solution.py:304
  107.1 9.2 %collective-permute-start.18 = (bf16[16,240,128]{2,1,0:T(8,128)(2,1)}, bf16[16,240,128]{2,1,0:T(8,128)(2,1)S(1)}, u32[]{:S(2)}, u32[]{:S(2)}) collective-permute-start(bf16[16,240,128]{2,1,0:T(8,128)(2,1)} %collective-permute-done.16.x_mine), channel_id=1, source_target_pairs={{0,4},{4,0},{8,12},{12,8},{16,20},{20,16},{24,28},{28,24},{1,5},{5... | collective-permute-start | bytes 2949128 | tf_op jit(solution)/shard_map/ppermute | solution.py:20
  107.1 2.1 %copy-start.4 = (bf16[16,240,128]{2,1,0:T(8,128)(2,1)}, bf16[16,240,128]{2,1,0:T(8,128)(2,1)S(1)}, u32[]{:S(2)}) copy-start(bf16[16,240,128]{2,1,0:T(8,128)(2,1)S(1)} %collective-permute-done.17.y_mine) | copy-start | bytes 2949124
  107.2 11.4 %collective-permute-start.19 = (bf16[16,240,128]{2,1,0:T(8,128)(2,1)S(1)}, bf16[16,240,128]{2,1,0:T(8,128)(2,1)S(1)}, u32[]{:S(2)}, u32[]{:S(2)}) collective-permute-start(bf16[16,240,128]{2,1,0:T(8,128)(2,1)S(1)} %broadcast_select_fusion), channel_id=1, source_target_pairs={{0,4},{4,0},{8,12},{12,8},{16,20},{20,16},{24,28},{28,24},{1,5},{5... | collective-permute-start | bytes 2949128 | tf_op jit(solution)/shard_map/ppermute | solution.py:20
  109.2 17.8 %copy-start.5 = (bf16[16,240,128]{2,1,0:T(8,128)(2,1)S(1)}, bf16[16,240,128]{2,1,0:T(8,128)(2,1)}, u32[]{:S(2)}) copy-start(bf16[16,240,128]{2,1,0:T(8,128)(2,1)} %copy-done.4) | copy-start | bytes 2949124
  109.2 14.8 %collective-permute-start.4 = (bf16[4,2,16,16,128]{4,3,2,1,0:T(8,128)(2,1)S(1)}, bf16[4,2,16,16,128]{4,3,2,1,0:T(8,128)(2,1)S(1)}, u32[]{:S(2)}, u32[]{:S(2)}) collective-permute-start(bf16[4,2,16,16,128]{4,3,2,1,0:T(8,128)(2,1)S(1)} %get-tuple-element.60), channel_id=1, source_target_pairs={{0,8},{4,12},{8,0},{12,4},{16,24},{20,28},{24,16},{28,20},{1,9},{5... | collective-permute-start | bytes 1572872 | tf_op jit(solution)/shard_map/ppermute | solution.py:20
  110.4 16.7 %collective-permute-start.5 = (bf16[4,2,16,16,128]{4,3,2,1,0:T(8,128)(2,1)S(1)}, bf16[4,2,16,16,128]{4,3,2,1,0:T(8,128)(2,1)S(1)}, u32[]{:S(2)}, u32[]{:S(2)}) collective-permute-start(bf16[4,2,16,16,128]{4,3,2,1,0:T(8,128)(2,1)S(1)} %get-tuple-element.59), channel_id=1, source_target_pairs={{0,16},{4,20},{8,8},{12,12},{16,0},{20,4},{24,24},{28,28},{1,17},{... | collective-permute-start | bytes 1572872 | tf_op jit(solution)/shard_map/ppermute | solution.py:20
  116.3 21.9 %collective-permute-start.10 = (bf16[4,2,16,16,128]{4,3,2,1,0:T(8,128)(2,1)}, bf16[4,2,16,16,128]{4,3,2,1,0:T(8,128)(2,1)}, u32[]{:S(2)}, u32[]{:S(2)}) collective-permute-start(bf16[4,2,16,16,128]{4,3,2,1,0:T(8,128)(2,1)} %get-tuple-element.58), channel_id=1, source_target_pairs={{0,8},{4,12},{8,0},{12,4},{16,24},{20,28},{24,16},{28,20},{1,9},{5... | collective-permute-start | bytes 1572872 | tf_op jit(solution)/shard_map/ppermute | solution.py:20
  116.3 23.2 %collective-permute-start.11 = (bf16[4,2,16,16,128]{4,3,2,1,0:T(8,128)(2,1)}, bf16[4,2,16,16,128]{4,3,2,1,0:T(8,128)(2,1)}, u32[]{:S(2)}, u32[]{:S(2)}) collective-permute-start(bf16[4,2,16,16,128]{4,3,2,1,0:T(8,128)(2,1)} %get-tuple-element.57), channel_id=1, source_target_pairs={{0,16},{4,20},{8,8},{12,12},{16,0},{20,4},{24,24},{28,28},{1,17},{... | collective-permute-start | bytes 1572872 | tf_op jit(solution)/shard_map/ppermute | solution.py:20
  127.1 41.1 %copy-start.3 = (bf16[512,1024]{1,0:T(8,128)(2,1)S(1)}, bf16[512,1024]{1,0:T(8,128)(2,1)}, u32[]{:S(2)}) copy-start(bf16[512,1024]{1,0:T(8,128)(2,1)} %copy-done.2) | copy-start | bytes 3145732
  131.7 0.8 copy-start.8
  132.5 0.7 copy-start.10
  133.3 34.9 %collective-permute-start.20 = (bf16[4,2,16,16,128]{4,3,2,1,0:T(8,128)(2,1)S(1)}, bf16[4,2,16,16,128]{4,3,2,1,0:T(8,128)(2,1)S(1)}, u32[]{:S(2)}, u32[]{:S(2)}) collective-permute-start(bf16[4,2,16,16,128]{4,3,2,1,0:T(8,128)(2,1)S(1)} %get-tuple-element.38), channel_id=1, source_target_pairs={{0,8},{4,12},{8,0},{12,4},{16,24},{20,28},{24,16},{28,20},{1,9},{5... | collective-permute-start | bytes 1572872 | tf_op jit(solution)/shard_map/ppermute | solution.py:20
  133.3 34.8 %collective-permute-start.21 = (bf16[4,2,16,16,128]{4,3,2,1,0:T(8,128)(2,1)S(1)}, bf16[4,2,16,16,128]{4,3,2,1,0:T(8,128)(2,1)S(1)}, u32[]{:S(2)}, u32[]{:S(2)}) collective-permute-start(bf16[4,2,16,16,128]{4,3,2,1,0:T(8,128)(2,1)S(1)} %get-tuple-element.39), channel_id=1, source_target_pairs={{0,16},{4,20},{8,8},{12,12},{16,0},{20,4},{24,24},{28,28},{1,17},{... | collective-permute-start | bytes 1572872 | tf_op jit(solution)/shard_map/ppermute | solution.py:20
  136.8 15.5 %collective-permute-start.22 = (bf16[2,16,16,128]{3,2,1,0:T(8,128)(2,1)}, bf16[2,16,16,128]{3,2,1,0:T(8,128)(2,1)S(1)}, u32[]{:S(2)}, u32[]{:S(2)}) collective-permute-start(bf16[2,16,16,128]{3,2,1,0:T(8,128)(2,1)} %copy-done.10), channel_id=1, source_target_pairs={{0,10},{1,11},{2,8},{3,9},{4,14},{5,15},{6,12},{7,13},{8,2},{9,3},... | collective-permute-start | bytes 393224 | tf_op jit(solution)/shard_map/ppermute | solution.py:25
  138.2 16.0 %collective-permute-start.23 = (bf16[2,16,16,128]{3,2,1,0:T(8,128)(2,1)S(1)}, bf16[2,16,16,128]{3,2,1,0:T(8,128)(2,1)S(1)}, u32[]{:S(2)}, u32[]{:S(2)}) collective-permute-start(bf16[2,16,16,128]{3,2,1,0:T(8,128)(2,1)S(1)} %get-tuple-element.41), channel_id=1, source_target_pairs={{0,18},{1,19},{2,16},{3,17},{4,22},{5,23},{6,20},{7,21},{8,10},{9,... | collective-permute-start | bytes 393224 | tf_op jit(solution)/shard_map/ppermute | solution.py:25
  139.5 16.4 %collective-permute-start.24 = (bf16[2,16,16,128]{3,2,1,0:T(8,128)(2,1)S(1)}, bf16[2,16,16,128]{3,2,1,0:T(8,128)(2,1)S(1)}, u32[]{:S(2)}, u32[]{:S(2)}) collective-permute-start(bf16[2,16,16,128]{3,2,1,0:T(8,128)(2,1)S(1)} %get-tuple-element.42), channel_id=1, source_target_pairs={{0,9},{1,10},{2,11},{3,8},{4,13},{5,14},{6,15},{7,12},{8,1},{9,2},... | collective-permute-start | bytes 393224 | tf_op jit(solution)/shard_map/ppermute | solution.py:25
  152.3 7.8 %collective-permute-start.25 = (bf16[2,16,16,128]{3,2,1,0:T(8,128)(2,1)S(1)}, bf16[2,16,16,128]{3,2,1,0:T(8,128)(2,1)S(1)}, u32[]{:S(2)}, u32[]{:S(2)}) collective-permute-start(bf16[2,16,16,128]{3,2,1,0:T(8,128)(2,1)S(1)} %get-tuple-element.43), channel_id=1, source_target_pairs={{0,17},{1,18},{2,19},{3,16},{4,21},{5,22},{6,23},{7,20},{8,9},{9,1... | collective-permute-start | bytes 393224 | tf_op jit(solution)/shard_map/ppermute | solution.py:25
  154.2 7.1 %collective-permute-start.26 = (bf16[2,16,16,128]{3,2,1,0:T(8,128)(2,1)S(1)}, bf16[2,16,16,128]{3,2,1,0:T(8,128)(2,1)S(1)}, u32[]{:S(2)}, u32[]{:S(2)}) collective-permute-start(bf16[2,16,16,128]{3,2,1,0:T(8,128)(2,1)S(1)} %get-tuple-element.44), channel_id=1, source_target_pairs={{0,11},{1,8},{2,9},{3,10},{4,15},{5,12},{6,13},{7,14},{8,3},{9,0},... | collective-permute-start | bytes 393224 | tf_op jit(solution)/shard_map/ppermute | solution.py:25
  155.9 10.0 %collective-permute-start.28 = (bf16[2,16,16,128]{3,2,1,0:T(8,128)(2,1)S(1)}, bf16[2,16,16,128]{3,2,1,0:T(8,128)(2,1)S(1)}, u32[]{:S(2)}, u32[]{:S(2)}) collective-permute-start(bf16[2,16,16,128]{3,2,1,0:T(8,128)(2,1)S(1)} %get-tuple-element.37.refs_0_), channel_id=1, source_target_pairs={{0,8},{1,9},{2,10},{3,11},{4,12},{5,13},{6,14},{7,15},{8,0},{9,1},... | collective-permute-start | bytes 393224 | tf_op jit(solution)/shard_map/ppermute | solution.py:25
  160.0 5.9 %collective-permute-start.27 = (bf16[2,16,16,128]{3,2,1,0:T(8,128)(2,1)S(1)}, bf16[2,16,16,128]{3,2,1,0:T(8,128)(2,1)S(1)}, u32[]{:S(2)}, u32[]{:S(2)}) collective-permute-start(bf16[2,16,16,128]{3,2,1,0:T(8,128)(2,1)S(1)} %get-tuple-element.45), channel_id=1, source_target_pairs={{0,19},{1,16},{2,17},{3,18},{4,23},{5,20},{6,21},{7,22},{8,11},{9,... | collective-permute-start | bytes 393224 | tf_op jit(solution)/shard_map/ppermute | solution.py:25
  161.3 6.8 %collective-permute-start.29 = (bf16[2,16,16,128]{3,2,1,0:T(8,128)(2,1)S(1)}, bf16[2,16,16,128]{3,2,1,0:T(8,128)(2,1)S(1)}, u32[]{:S(2)}, u32[]{:S(2)}) collective-permute-start(bf16[2,16,16,128]{3,2,1,0:T(8,128)(2,1)S(1)} %get-tuple-element.46), channel_id=1, source_target_pairs={{0,16},{1,17},{2,18},{3,19},{4,20},{5,21},{6,22},{7,23},{8,8},{9,9... | collective-permute-start | bytes 393224 | tf_op jit(solution)/shard_map/ppermute | solution.py:25
  168.2 1.0 copy-start.9
